TPU v7x, 256 devices: a whole 4x4x8 slice. The times are simulated.
256 devices in a mesh: gx: 4 (over x_hi, core), gy: 16 (over z, x_lo), mz: 4 (over y).
Axes of the slice: x: 4 (x_hi: 2, x_lo: 2; x = x_hi * 2 + x_lo), y: 4, z: 8, core: 2. Of those that a mesh axis runs over, the one named last changes fastest.
Arguments:
- counts: int32 [128, 32, 256, 256], P('mz', 'gx', 'gy'), may hold values from 0 to 24
- kernel_taps: float32 [3, 5], replicated, may hold values from 0.1 to 1
- peak_bins: int32 [24, 4], replicated, may hold values from 0 to 127, as said below
- peak_share: float32 [24, 4], replicated, may hold values from 0.1 to 1
Outputs:
- abundance: float32 [24, 32, 256, 256], P(None, ('gx', 'mz'), 'gy')
Inputs may be any that keep to these rules, and one draw needn't show every extreme that they name: `peak_bins`: no two isotope peaks of the same element share a bin; peaks of different elements may.
All inputs are finite; a program needn't handle non-finite values.
Results may differ from a plain program's by a relative error of at most 0.000092.
Values sent between devices are 32-bit elements; how exact they have to be, the bound alone decides.
No kernel may reach another device: no remote copies, remote signals or barrier semaphores. Data moves between devices by JAX's collectives and lax.ppermute only.
A program may use at most 64 MiB of HBM per device.

v0:
```python
import jax
import jax.numpy as jnp
from jax import lax
from jax.sharding import PartitionSpec as P

RIDGE_WEIGHT = 0.5


def extended(block, sides, width):
    for axis, dim in sides:
        count = lax.axis_size(axis)
        forward = [(i, i + 1) for i in range(count - 1)]
        backward = [(target, source) for source, target in forward]
        low = lax.ppermute(
            lax.slice_in_dim(block, block.shape[dim] - width, None, axis=dim), axis, forward
        )
        high = lax.ppermute(lax.slice_in_dim(block, 0, width, axis=dim), axis, backward)
        block = jnp.concatenate([low, block, high], axis=dim)
    return block


def pad_axis(values, along):
    widths = [(0, 0)] * values.ndim
    widths[along] = (2, 2)
    return jnp.pad(values, widths)


def run_taps(padded, weights, along, length):
    summed = weights[0] * lax.slice_in_dim(padded, 0, length, axis=along)
    for offset in range(1, 5):
        summed = summed + weights[offset] * lax.slice_in_dim(
            padded, offset, offset + length, axis=along
        )
    return summed


def coordinate(positions, extent):
    return (2.0 * positions.astype(jnp.float32) + 1.0) / float(extent) - 1.0


def squares(size_x, size_y, size_z):
    full_x = coordinate(jnp.arange(size_x, dtype=jnp.int32), size_x)
    full_y = coordinate(jnp.arange(size_y, dtype=jnp.int32), size_y)
    full_z = coordinate(jnp.arange(size_z, dtype=jnp.int32), size_z)
    return jnp.stack(
        [
            jnp.asarray(float(size_x * size_y * size_z), jnp.float32),
            jnp.sum(full_x * full_x) * float(size_y * size_z),
            jnp.sum(full_y * full_y) * float(size_x * size_z),
            jnp.sum(full_z * full_z) * float(size_x * size_y),
        ]
    )


def moments(values, coord_x, coord_y, coord_z):
    plane_x = jnp.sum(values, axis=(2, 3))
    plane_y = jnp.sum(values, axis=(1, 3))
    plane_z = jnp.sum(values, axis=(1, 2))
    return jnp.stack(
        [
            jnp.sum(plane_x, axis=1),
            jnp.dot(plane_x, coord_x, precision=lax.Precision.HIGHEST),
            jnp.dot(plane_y, coord_y, precision=lax.Precision.HIGHEST),
            jnp.dot(plane_z, coord_z, precision=lax.Precision.HIGHEST),
        ],
        axis=1,
    )


def background(fitted, coord_x, coord_y, coord_z):
    return (
        fitted[:, 0, None, None, None]
        + fitted[:, 1, None, None, None] * coord_x[None, :, None, None]
        + fitted[:, 2, None, None, None] * coord_y[None, None, :, None]
        + fitted[:, 3, None, None, None] * coord_z[None, None, None, :]
    )


def unmix_matrix(peak_bins, peak_share, all_bins):
    one_hot = (
        peak_bins[:, :, None] == jnp.arange(all_bins, dtype=jnp.int32)[None, None, :]
    ).astype(jnp.float32)
    mixing_t = jnp.sum(peak_share[:, :, None] * one_hot, axis=1)
    gram_matrix = jnp.dot(
        mixing_t.T, mixing_t, precision=lax.Precision.HIGHEST
    ) + RIDGE_WEIGHT * jnp.eye(all_bins, dtype=jnp.float32)
    factor = jnp.linalg.cholesky(gram_matrix)
    lower_part = lax.linalg.triangular_solve(factor, mixing_t.T, left_side=True, lower=True)
    solved = lax.linalg.triangular_solve(
        factor, lower_part, left_side=True, lower=True, transpose_a=True
    )
    return solved.T


def shards(counts, kernel_taps, peak_bins, peak_share):
    weights = kernel_taps / jnp.sum(kernel_taps, axis=1, keepdims=True)
    local_bins, local_x, local_y, depth = counts.shape
    split_count = lax.axis_size("mz")
    all_bins = local_bins * split_count
    size_x = local_x * lax.axis_size("gx")
    size_y = local_y * lax.axis_size("gy")
    values = counts.astype(jnp.float32)
    values = run_taps(pad_axis(values, 3), weights[2], 3, depth)
    padded = extended(values, (("gx", 1), ("gy", 2)), 2)
    values = run_taps(padded, weights[0], 1, local_x)
    values = run_taps(values, weights[1], 2, local_y)
    coord_x = coordinate(
        lax.axis_index("gx") * local_x + jnp.arange(local_x, dtype=jnp.int32), size_x
    )
    coord_y = coordinate(
        lax.axis_index("gy") * local_y + jnp.arange(local_y, dtype=jnp.int32), size_y
    )
    coord_z = coordinate(jnp.arange(depth, dtype=jnp.int32), depth)
    squares_all = squares(size_x, size_y, depth)
    local_moments = moments(values, coord_x, coord_y, coord_z)
    unmix_rows = unmix_matrix(peak_bins, peak_share, all_bins)
    totals = lax.psum(local_moments, ("gx", "gy"))
    fitted = totals / squares_all[None, :]
    values = values - background(fitted, coord_x, coord_y, coord_z)
    regrouped = lax.all_to_all(values, "mz", split_axis=1, concat_axis=0, tiled=True)
    block_shape = regrouped.shape
    products = jnp.dot(
        unmix_rows, regrouped.reshape(block_shape[0], -1), precision=lax.Precision.HIGHEST
    )
    return products.reshape((unmix_rows.shape[0],) + tuple(block_shape[1:]))


def solution(mesh):
    return jax.shard_map(
        shards,
        mesh=mesh,
        in_specs=(P("mz", "gx", "gy", None), P(), P(), P()),
        out_specs=P(None, ("gx", "mz"), "gy", None),
        check_vma=False,
    )
```

profile of v0, /device:TPU:4, one launch (start us, length us, event | category | flops | bytes accessed | tf_op | source)
XLA Modules:
  0.0 295.5 jit_solution(18421523107518772411)
XLA Ops:
  0.0 0.8 reduce_sum.77
  0.8 0.8 broadcast_divide_fusion.1
  1.6 0.7 fusion.27
  2.3 4.6 %copy_convert_fusion = f32[32,8,16,256]{3,0,2,1:T(8,128)S(1)} fusion(s32[32,8,16,256]{3,2,1,0:T(8,128)} %param.4), kind=kLoop, calls=%fused_computation.32 | loop fusion | flops 1048576 | bytes 8388608 | tf_op jit(solution)/shard_map/convert_element_type | solution.py:102
  6.8 7.9 %fusion.8 = f32[32,8,16,256]{3,0,2,1:T(8,128)S(1)} fusion(f32[32,8,16,256]{3,0,2,1:T(8,128)S(1)} %copy_convert_fusion, f32[]{:T(128)} %bitcast.11, f32[]{:T(128)} %bitcast.10, f32[]{:T(128)} %bitcast.9, f32[]{:T(128)} %bitcast.8, f32[]{:T(128)} %bitcast.7), kind=kLoop, calls=%fused_computation.18 | loop fusion | flops 9437184 | bytes 8388628 | tf_op jit(solution)/shard_map/add | solution.py:31
  15.0 1.9 collective-permute-start
  16.9 5.1 %collective-permute-start.1 = (f32[32,2,16,256]{3,0,2,1:T(8,128)S(1)}, f32[32,2,16,256]{3,0,2,1:T(8,128)S(1)}, u32[]{:S(2)}, u32[]{:S(2)}) collective-permute-start(f32[32,2,16,256]{3,0,2,1:T(8,128)S(1)} %get-tuple-element.13), channel_id=1, source_target_pairs={{64,0},{128,64},{192,128},{65,1},{129,65},{193,129},{66,2},{130,66... | collective-permute-start | bytes 3145736 | tf_op jit(solution)/shard_map/ppermute | solution.py:17
  22.1 13.0 %collective-permute-done = f32[32,2,16,256]{3,0,2,1:T(8,128)S(1)} collective-permute-done((f32[32,2,16,256]{3,0,2,1:T(8,128)S(1)}, f32[32,2,16,256]{3,0,2,1:T(8,128)S(1)}, u32[]{:S(2)}, u32[]{:S(2)}) %collective-permute-start) | collective-permute-done | bytes 1048608 | tf_op jit(solution)/shard_map/ppermute | solution.py:14
  35.1 15.8 %collective-permute-done.1 = f32[32,2,16,256]{3,0,2,1:T(8,128)S(1)} collective-permute-done((f32[32,2,16,256]{3,0,2,1:T(8,128)S(1)}, f32[32,2,16,256]{3,0,2,1:T(8,128)S(1)}, u32[]{:S(2)}, u32[]{:S(2)}) %collective-permute-start.1) | collective-permute-done | bytes 1048608 | tf_op jit(solution)/shard_map/ppermute | solution.py:17
  50.8 1.3 pad_maximum_fusion.3
  52.1 1.3 collective-permute-start.2
  53.4 1.3 collective-permute-start.3
  54.7 0.6 multiply_reduce_fusion.1
  56.0 0.6 multiply_reduce_fusion
  57.3 14.3 %collective-permute-done.2 = f32[32,12,2,256]{3,0,2,1:T(8,128)S(1)} collective-permute-done((f32[32,12,2,256]{3,0,2,1:T(8,128)}, f32[32,12,2,256]{3,0,2,1:T(8,128)S(1)}, u32[]{:S(2)}, u32[]{:S(2)}) %collective-permute-start.2) | collective-permute-done | bytes 786464 | tf_op jit(solution)/shard_map/ppermute | solution.py:14
  71.6 3.2 %pad_maximum_fusion = f32[32,12,20,256]{3,0,2,1:T(8,128)S(1)} fusion(f32[32,12,2,256]{3,0,2,1:T(8,128)} %collective-permute-done.3, f32[32,2,16,256]{3,0,2,1:T(8,128)S(1)} %collective-permute-done.1, f32[32,8,16,256]{3,0,2,1:T(8,128)} %copy-done, f32[32,2,16,256]{3,0,2,1:T(8,128)S(1)} %collective-permute-done, f32[32,12,2,256]{3,0,2,1:T(8,128)S(1)} %collective-permute-done.2), kind=kLoop, calls=%fused_computation.4 | loop fusion | flops 7864320 | bytes 15728640 | tf_op jit(solution)/shard_map/concatenate | solution.py:18
  74.8 7.0 %fusion = f32[32,8,20,256]{3,0,2,1:T(8,128)S(1)} fusion(f32[32,12,20,256]{3,0,2,1:T(8,128)S(1)} %pad_maximum_fusion, f32[]{:T(128)} %bitcast.15, f32[]{:T(128)} %bitcast.14, f32[]{:T(128)} %bitcast.13, f32[]{:T(128)} %bitcast.12, f32[]{:T(128)} %bitcast.6), kind=kLoop, calls=%fused_computation.6 | loop fusion | flops 11796480 | bytes 31457300 | tf_op jit(solution)/shard_map/add | solution.py:31
  81.8 7.5 %fusion.24 = (f32[32]{0:T(128)S(1)}, f32[32,256]{1,0:T(8,128)S(1)}, f32[32,16]{0,1:T(8,128)S(1)}, f32[32,8]{0,1:T(8,128)S(1)}, f32[32,8,16,256]{3,0,2,1:T(8,128)}) fusion(f32[32,8,20,256]{3,0,2,1:T(8,128)S(1)} %fusion, f32[]{:T(128)} %bitcast.19, f32[]{:T(128)} %bitcast.18, f32[]{:T(128)} %bitcast.17, f32[]{:T(128)} %bitcast.16, f32[]{:T(128)} %bitcast.5), kind=kLoop, calls=%fused_computation.75 | loop fusion | flops 13622496 | bytes 25201812 | tf_op jit(solution)/shard_map/reduce_sum | solution.py:61
  89.7 122.0 %psum.7 = f32[32,4]{0,1:T(4,128)S(1)} all-reduce(f32[32,4]{0,1:T(4,128)S(1)} %pad_maximum_fusion.4), channel_id=1, replica_groups=mesh['gx'=4,'gy'=16,'mz'=4] {'gx','gy'}, use_global_device_ids=true, to_apply=%region_8.9 | all-reduce | flops 128 | bytes 1024 | tf_op jit(solution)/shard_map/psum | solution.py:117
  212.0 2.6 add_subtract_fusion
  214.6 4.4 %copy.34 = f32[32,8,16,256]{3,2,0,1:T(8,128)} copy(f32[32,8,16,256]{3,0,2,1:T(8,128)S(1)} %add_subtract_fusion) | data formatting | bytes 8388608 | tf_op jit(solution)/shard_map/sub | solution.py:119
  219.0 5.0 %all-to-all-start = ((f32[32,8,16,256]{3,2,0,1:T(8,128)}), f32[32,8,16,256]{3,2,0,1:T(8,128)}, u32[]{:S(2)}, u32[]{:S(2)}) async-start(f32[32,8,16,256]{3,2,0,1:T(8,128)} %copy.34), calls=%async_computation | async-start | bytes 8388608 | tf_op jit(solution)/shard_map/all_to_all | solution.py:120
  224.6 11.7 %cholesky.16 = f32[128,128]{1,0:T(8,128)S(1)} custom-call(f32[128,128]{1,0:T(8,128)S(1)} %fusion.21), custom_call_target="Cholesky" | custom-call | tf_op jit(solution)/shard_map/jit(cholesky)/cholesky | solution.py:87
  236.3 0.6 compare_reduce_fusion
  237.0 0.7 fusion.16
  237.6 9.8 %custom-call.8 = f32[1,128,128]{1,2,0:T(8,128)S(1)} custom-call(f32[1,128,128]{2,1,0:T(8,128)S(1)} %fusion.16), custom_call_target="InvertDiagBlocksLowerTriangular" | custom-call | tf_op jit(solution)/shard_map/triangular_solve | solution.py:89
  247.8 25.6 %all-to-all-done = f32[32,8,16,256]{3,2,0,1:T(8,128)} async-done(((f32[32,8,16,256]{3,2,0,1:T(8,128)}), f32[32,8,16,256]{3,2,0,1:T(8,128)}, u32[]{:S(2)}, u32[]{:S(2)}) %all-to-all-start) | async-done | bytes 4194336 | tf_op jit(solution)/shard_map/all_to_all | solution.py:120
  273.4 4.8 %copy.41 = f32[32,4,2,16,256]{4,3,2,0,1:T(8,128)} copy(f32[32,4,2,16,256]{4,3,0,2,1:T(8,128)} %bitcast.36) | data formatting | bytes 8388608 | tf_op jit(solution)/shard_map/all_to_all | solution.py:120
  278.2 4.9 %reshape.204 = f32[128,8192]{1,0:T(8,128)} reshape(f32[4,32,2,16,256]{4,3,2,1,0:T(8,128)} %bitcast.78) | data formatting | bytes 8388608 | tf_op jit(solution)/shard_map/reshape | solution.py:123
  283.1 5.6 %copy.36 = f32[8192,128]{1,0:T(8,128)} copy(f32[8192,128]{0,1:T(8,128)} %bitcast.79) | data formatting | bytes 8388608 | tf_op jit(solution)/shard_map/dot_general | solution.py:122
  288.7 5.7 %fusion.29 = f32[24,2,16,256]{3,0,2,1:T(8,128)S(1)} fusion(f32[128,24,1,1]{0,1,3,2:T(8,128)S(1)} %convolution_bitcast_fusion, f32[2,16,256,128]{3,2,1,0:T(8,128)} %bitcast.77), kind=kOutput, calls=%fused_computation.79 | convolution fusion | flops 301989888 | bytes 4993024 | tf_op jit(solution)/shard_map/dot_general | solution.py:122
  294.4 1.1 copy.37
  (29 shorter events, 2.0 us)
Async XLA Ops:
  14.7 37.3 %copy-start = (f32[32,8,16,256]{3,0,2,1:T(8,128)}, f32[32,8,16,256]{3,0,2,1:T(8,128)S(1)}, u32[]{:S(2)}) copy-start(f32[32,8,16,256]{3,0,2,1:T(8,128)S(1)} %fusion.8) | copy-start | bytes 12582916
  15.0 20.1 %collective-permute-start = (f32[32,2,16,256]{3,0,2,1:T(8,128)S(1)}, f32[32,2,16,256]{3,0,2,1:T(8,128)S(1)}, u32[]{:S(2)}, u32[]{:S(2)}) collective-permute-start(f32[32,2,16,256]{3,0,2,1:T(8,128)S(1)} %get-tuple-element.12), channel_id=1, source_target_pairs={{0,64},{64,128},{128,192},{1,65},{65,129},{129,193},{2,66},{66,130... | collective-permute-start | bytes 3145736 | tf_op jit(solution)/shard_map/ppermute | solution.py:14
  16.9 33.9 %collective-permute-start.1 = (f32[32,2,16,256]{3,0,2,1:T(8,128)S(1)}, f32[32,2,16,256]{3,0,2,1:T(8,128)S(1)}, u32[]{:S(2)}, u32[]{:S(2)}) collective-permute-start(f32[32,2,16,256]{3,0,2,1:T(8,128)S(1)} %get-tuple-element.13), channel_id=1, source_target_pairs={{64,0},{128,64},{192,128},{65,1},{129,65},{193,129},{66,2},{130,66... | collective-permute-start | bytes 3145736 | tf_op jit(solution)/shard_map/ppermute | solution.py:17
  52.1 19.5 %collective-permute-start.2 = (f32[32,12,2,256]{3,0,2,1:T(8,128)}, f32[32,12,2,256]{3,0,2,1:T(8,128)S(1)}, u32[]{:S(2)}, u32[]{:S(2)}) collective-permute-start(f32[32,12,2,256]{3,0,2,1:T(8,128)} %get-tuple-element.10), channel_id=1, source_target_pairs={{0,4},{4,8},{8,12},{12,16},{16,20},{20,24},{24,28},{28,32},{32,36}... | collective-permute-start | bytes 2359304 | tf_op jit(solution)/shard_map/ppermute | solution.py:14
  53.4 18.2 %collective-permute-start.3 = (f32[32,12,2,256]{3,0,2,1:T(8,128)}, f32[32,12,2,256]{3,0,2,1:T(8,128)}, u32[]{:S(2)}, u32[]{:S(2)}) collective-permute-start(f32[32,12,2,256]{3,0,2,1:T(8,128)} %get-tuple-element.11), channel_id=1, source_target_pairs={{4,0},{8,4},{12,8},{16,12},{20,16},{24,20},{28,24},{32,28},{36,32}... | collective-permute-start | bytes 2359304 | tf_op jit(solution)/shard_map/ppermute | solution.py:17
  219.0 5.0 %copy-start.1 = (f32[24,4]{0,1:T(4,128)S(1)}, f32[24,4]{0,1:T(4,128)}, u32[]{:S(2)}) copy-start(f32[24,4]{0,1:T(4,128)} %param.7) | copy-start | bytes 1156
  219.0 5.0 %copy-start.2 = (s32[24,4]{0,1:T(4,128)S(1)}, s32[24,4]{0,1:T(4,128)}, u32[]{:S(2)}) copy-start(s32[24,4]{0,1:T(4,128)} %param.6) | copy-start | bytes 1156
  219.0 54.3 %all-to-all-start = ((f32[32,8,16,256]{3,2,0,1:T(8,128)}), f32[32,8,16,256]{3,2,0,1:T(8,128)}, u32[]{:S(2)}, u32[]{:S(2)}) async-start(f32[32,8,16,256]{3,2,0,1:T(8,128)} %copy.34), calls=%async_computation | async-start | bytes 8388608 | tf_op jit(solution)/shard_map/all_to_all | solution.py:120
where the time goes:
time: 296 us; the launch traced here: 295 us
  blocking collectives  122 us (41%)
  waiting for transfers between devices  68.6 us (23%)
  other arithmetic  60.2 us (20%)
  local copies, waits for them, and re-layouts  21.9 us (7%)
  starting transfers between devices  14.7 us (5%)
  matrix products  6.73 us (2%)
    psum x1, blocking collectives, shards(): totals = lax.psum(local_moments, ('gx', 'gy'))  122 us
    ppermute x2, waiting for transfers between devices, extended(): lax.ppermute(lax.slice_in_dim(block, block.shape[dim] - width, None, axis...  27.3 us
    all_to_all x1, waiting for transfers between devices, shards(): lax.all_to_all(values, 'mz', split_axis=1, concat_axis=0, tiled=True)  25.6 us
    ppermute x2, waiting for transfers between devices, extended(): lax.ppermute(lax.slice_in_dim(block, 0, width, axis=dim), axis, backward)  15.8 us
    add x2, other arithmetic, run_taps(): summed + weights[offset] * lax.slice_in_dim(padded, offset, offset + leng...  14.9 us
    another operation x3, other arithmetic, unmix_matrix(): factor = jnp.linalg.cholesky(gram_matrix)  12.4 us
    another operation x2, other arithmetic, unmix_matrix(): lax.linalg.triangular_solve(factor, lower_part, left_side=True, lower=Tru...  10.5 us
    reduce_sum x1, other arithmetic, moments(): jnp.sum(plane_x, axis=1)  7.48 us
  transfers between devices with their start and end apart: 5, of which 4 were waited for; matrix products, arithmetic and copies ran while one was open for 8% of the time, Pallas kernels for 0%

commit v1 on v0

v1 whole, which is shorter than its diff:
```python
import functools

import jax
import jax.numpy as jnp
from jax import lax
from jax.experimental import pallas as pl
from jax.experimental.pallas import tpu as pltpu
from jax.sharding import PartitionSpec as P

RIDGE_WEIGHT = 0.5
TAPS = 5
REACH = 2
LANES = 128
HIGHEST = lax.Precision.HIGHEST
VMEM_LIMIT = 48 * 1024 * 1024

GROUPS = ((tuple(range(8)), tuple(range(8, 16))),)


def iota(shape, dim):
    return lax.broadcasted_iota(jnp.int32, shape, dim)


def normalized(taps_ref):
    taps = taps_ref[...]
    return taps / jnp.sum(taps, axis=1, keepdims=True)


def tap(weights, axis, offset):
    return weights[axis : axis + 1, offset : offset + 1]


def adjoint(weights, axis, positions, extent):
    ones = jnp.zeros(positions.shape, jnp.float32)
    linear = jnp.zeros(positions.shape, jnp.float32)
    for offset in range(TAPS):
        target = positions - (offset - REACH)
        inside = (target >= 0) & (target < extent)
        weight = jnp.where(inside, tap(weights, axis, offset), 0.0)
        coordinate = (2.0 * target.astype(jnp.float32) + 1.0) / float(extent) - 1.0
        ones = ones + weight
        linear = linear + weight * coordinate
    return ones, linear


def unmix_rows(bins_ref, share_ref, all_bins):
    elements, peaks = bins_ref.shape
    bins = bins_ref[...]
    share = share_ref[...]
    lanes = iota((elements, all_bins), 1)
    mixing_t = jnp.zeros((elements, all_bins), jnp.float32)
    for peak in range(peaks):
        mixing_t = mixing_t + jnp.where(
            lanes == bins[:, peak : peak + 1], share[:, peak : peak + 1], 0.0
        )
    left = lax.dot_general(
        mixing_t, mixing_t, (((1,), (1,)), ((), ())), precision=HIGHEST,
        preferred_element_type=jnp.float32,
    )
    square = (elements, elements)
    left = left + jnp.where(iota(square, 0) == iota(square, 1), RIDGE_WEIGHT, 0.0)
    right = mixing_t
    for step in range(elements):
        inverse = 1.0 / left[step : step + 1, step : step + 1]
        left_row = left[step : step + 1, :] * inverse
        right_row = right[step : step + 1, :] * inverse
        column = left[:, step : step + 1]
        here = iota((elements, 1), 0) == step
        left = jnp.where(here, left_row, left - column * left_row)
        right = jnp.where(here, right_row, right - column * right_row)
    return right


def mix_kernel(sizes, groups, place_ref, taps_ref, bins_ref, share_ref, counts_ref, *rest):
    local_bins, local_x, local_y, depth, elements, split, all_bins, size_x, size_y, devices = sizes
    count = len(groups)
    outs, moments_ref = rest[: 3 * count], rest[3 * count]
    held, table, sums, sem = rest[3 * count + 1 :]
    rows_in = local_bins * local_x
    copies = [
        pltpu.make_async_copy(counts_ref.at[:, pl.ds(lane * LANES, LANES)], held.at[lane], sem.at[lane])
        for lane in range(depth // LANES)
    ]
    for copy in copies:
        copy.start()
    at_x, at_y, at_m = place_ref[0], place_ref[1], place_ref[2]
    weights = normalized(taps_ref)
    unmix = unmix_rows(bins_ref, share_ref, all_bins)
    expand_shape = (all_bins, rows_in)
    expand = jnp.where(
        iota(expand_shape, 0) == at_m * local_bins + iota(expand_shape, 1) // local_x, 1.0, 0.0
    )
    spread = jnp.dot(unmix, expand, precision=HIGHEST, preferred_element_type=jnp.float32)
    layer = iota((1, rows_in), 1) % local_x
    targets = []
    for ahead in range(split):
        owner = (at_m + ahead) % split
        targets += [owner * REACH + j for j in range(REACH)]
    targets += [j - REACH for j in range(REACH)] + [local_x + j for j in range(REACH)]
    for place, target in enumerate(targets):
        factor = jnp.zeros((1, rows_in), jnp.float32)
        for offset in range(TAPS):
            factor = jnp.where(layer - target + REACH == offset, tap(weights, 0, offset), factor)
        table[pl.ds(place * elements, elements), :] = spread * factor
    wide = table[...]
    high = wide.astype(jnp.bfloat16)
    low = (wide - high.astype(jnp.float32)).astype(jnp.bfloat16)
    rows_y = at_y * local_y + iota((local_y, depth), 0)
    ones_y, linear_y = adjoint(weights, 1, rows_y, size_y)
    for copy in copies:
        copy.wait()
    block = REACH * elements
    first = True
    for group, halves in enumerate(groups):
        main_ref, up_ref, down_ref = outs[3 * group : 3 * group + 3]
        for slot, row in enumerate(halves[0] + halves[1]):
            plane = jnp.concatenate(
                [
                    held[lane, pl.ds(row, rows_in, stride=local_y), :]
                    for lane in range(depth // LANES)
                ],
                axis=1,
            )
            plane = plane.astype(jnp.float32).astype(jnp.bfloat16)
            mixed = jnp.dot(high, plane, preferred_element_type=jnp.float32) + jnp.dot(
                low, plane, preferred_element_type=jnp.float32
            )
            for ahead in range(split):
                main_ref[ahead, slot] = mixed[ahead * block : (ahead + 1) * block]
            up_ref[slot] = mixed[split * block : (split + 1) * block]
            down_ref[slot] = mixed[(split + 1) * block :]
            plain = mixed * ones_y[row : row + 1, :]
            tilted = mixed * linear_y[row : row + 1, :]
            if first:
                sums[0], sums[1] = plain, tilted
                first = False
            else:
                sums[0] += plain
                sums[1] += tilted
    parts = [jnp.zeros((elements, depth), jnp.float32) for _ in range(3)]
    for place, target in enumerate(targets):
        x = at_x * local_x + target
        inside = jnp.where((x >= 0) & (x < size_x), 1.0, 0.0)
        coordinate = (2.0 * lax.convert_element_type(x, jnp.float32) + 1.0) / float(size_x) - 1.0
        rows = pl.ds(place * elements, elements)
        plain = sums[0, rows, :] * inside
        parts[0] = parts[0] + plain
        parts[1] = parts[1] + plain * coordinate
        parts[2] = parts[2] + sums[1, rows, :] * inside
    stacked = jnp.concatenate(
        [parts[0], parts[1], parts[2], parts[0], jnp.zeros((128 - 4 * elements, depth), jnp.float32)],
        axis=0,
    )
    ones_z, linear_z = adjoint(weights, 2, iota((8, depth), 1), depth)
    profile = jnp.where(iota((8, depth), 0) == 0, ones_z, linear_z)
    products = lax.dot_general(
        profile, stacked, (((1,), (1,)), ((), ())), precision=HIGHEST,
        preferred_element_type=jnp.float32,
    )
    row = jnp.where(iota((1, 128), 1) < 3 * elements, products[0:1], products[1:2])
    moments_ref[...] = jnp.broadcast_to(row, (devices, 128))


def mix(place, taps, bins, share, counts, sizes, groups):
    local_bins, local_x, local_y, depth, elements, split, _, _, _, devices = sizes
    block = REACH * elements
    shapes = []
    for halves in groups:
        length = len(halves[0]) + len(halves[1])
        shapes.append((split, length, block, depth))
        shapes += [(length, block, depth)] * 2
    shapes.append((devices, 128))
    rows_out = (split + 2) * block
    vmem = pl.BlockSpec(memory_space=pltpu.VMEM)
    return pl.pallas_call(
        functools.partial(mix_kernel, sizes, groups),
        out_shape=[jax.ShapeDtypeStruct(shape, jnp.float32) for shape in shapes],
        in_specs=[pl.BlockSpec(memory_space=pltpu.SMEM), vmem, vmem, vmem,
                  pl.BlockSpec(memory_space=pl.ANY)],
        out_specs=[vmem] * len(shapes),
        scratch_shapes=[
            pltpu.VMEM((depth // LANES, local_bins * local_x * local_y, LANES), jnp.int32),
            pltpu.VMEM((rows_out, local_bins * local_x), jnp.float32),
            pltpu.VMEM((2, rows_out, depth), jnp.float32),
            pltpu.SemaphoreType.DMA((depth // LANES,)),
        ],
        compiler_params=pltpu.CompilerParams(vmem_limit_bytes=VMEM_LIMIT),
        cost_estimate=pl.CostEstimate(
            flops=4 * rows_out * local_bins * local_x * local_y * depth,
            bytes_accessed=10 * 1024 * 1024,
            transcendentals=0,
        ),
        name="mix_bins",
    )(place, taps, bins, share, counts.reshape(-1, depth))


def finish_kernel(sizes, groups, squares, place_ref, taps_ref, moments_ref, before_ref, after_ref, *rest):
    local_y, depth, elements, split, local_x, size_x, size_y = sizes
    out_ref, turned = rest[-2:]
    block = REACH * elements
    at_x, at_y, at_m = place_ref[0], place_ref[1], place_ref[2]
    weights = normalized(taps_ref)
    planes = {}
    for j in range(REACH):
        planes[j - REACH] = before_ref[j]
        planes[local_y + j] = after_ref[j]
    for group, halves in enumerate(groups):
        refs = rest[5 * group : 5 * group + 5]
        own, near, far = refs[0], refs[1:3], refs[3:5]
        length = len(halves[0])
        for half in range(2):
            for slot, row in enumerate(halves[half]):
                planes[row] = own[half * length + slot] + near[half][slot] + far[half][slot]
    totals = jnp.sum(moments_ref[...], axis=0, keepdims=True)
    lanes = iota((elements, 128), 1)
    rows = iota((elements, 128), 0)
    fitted = [
        jnp.sum(jnp.where(lanes == rows + j * elements, totals, 0.0), axis=1, keepdims=True)
        / squares[j]
        for j in range(4)
    ]
    at = at_x * local_x + at_m * REACH
    bases = []
    for j in range(REACH):
        coordinate = (2.0 * lax.convert_element_type(at + j, jnp.float32) + 1.0) / float(size_x) - 1.0
        bases.append(fitted[0] + fitted[1] * coordinate)
    base = jnp.concatenate(bases, axis=0)
    slope_y = jnp.concatenate([fitted[2]] * REACH, axis=0)
    slope_z = jnp.concatenate([fitted[3]] * REACH, axis=0)
    line = iota((1, depth), 1)
    tilted = base + slope_z * ((2.0 * line.astype(jnp.float32) + 1.0) / float(depth) - 1.0)
    edge = []
    for offset in range(TAPS):
        source = line + (offset - REACH)
        edge.append(jnp.where((source >= 0) & (source < depth), tap(weights, 2, offset), 0.0))
    for row in range(local_y):
        smooth = tap(weights, 1, 0) * planes[row - REACH]
        for offset in range(1, TAPS):
            smooth = smooth + tap(weights, 1, offset) * planes[row + offset - REACH]
        y = at_y * local_y + row
        coordinate = (2.0 * lax.convert_element_type(y, jnp.float32) + 1.0) / float(size_y) - 1.0
        result = -(tilted + slope_y * coordinate)
        for offset in range(TAPS):
            shifted = smooth if offset == REACH else pltpu.roll(smooth, (REACH - offset) % depth, 1)
            result = result + edge[offset] * shifted
        for j in range(REACH):
            for lane in range(depth // LANES):
                turned[lane, pl.ds(j * local_y + row, elements, stride=REACH * local_y), :] = result[
                    j * elements : (j + 1) * elements, lane * LANES : (lane + 1) * LANES
                ]
    for lane in range(depth // LANES):
        out_ref[:, lane * LANES : (lane + 1) * LANES] = turned[lane]


def finish(place, taps, moments, before, after, parts, sizes, groups, squares):
    local_y, depth, elements = sizes[:3]
    vmem = pl.BlockSpec(memory_space=pltpu.VMEM)
    return pl.pallas_call(
        functools.partial(finish_kernel, sizes, groups, squares),
        out_shape=jax.ShapeDtypeStruct((elements * REACH * local_y, depth), jnp.float32),
        in_specs=[pl.BlockSpec(memory_space=pltpu.SMEM)] + [vmem] * (4 + len(parts)),
        out_specs=vmem,
        scratch_shapes=[
            pltpu.VMEM((depth // LANES, elements * REACH * local_y, LANES), jnp.float32)
        ],
        compiler_params=pltpu.CompilerParams(vmem_limit_bytes=VMEM_LIMIT),
        cost_estimate=pl.CostEstimate(
            flops=30 * elements * REACH * local_y * depth,
            bytes_accessed=4 * 1024 * 1024,
            transcendentals=0,
        ),
        name="finish",
    )(place, taps, moments, before, after, *parts)


def shift(values, axis, by):
    count = lax.axis_size(axis)
    return lax.ppermute(
        values, axis, [(i, i + by) for i in range(count) if 0 <= i + by < count]
    )


def turn(values, axis, by):
    count = lax.axis_size(axis)
    return lax.ppermute(values, axis, [(i, (i + by) % count) for i in range(count)])


def squared_norms(size_x, size_y, size_z):
    def of(extent):
        return sum(((2.0 * i + 1.0) / extent - 1.0) ** 2 for i in range(extent))

    return (
        float(size_x * size_y * size_z),
        of(size_x) * size_y * size_z,
        of(size_y) * size_x * size_z,
        of(size_z) * size_x * size_y,
    )


def shards(counts, kernel_taps, peak_bins, peak_share):
    local_bins, local_x, local_y, depth = counts.shape
    elements = peak_bins.shape[0]
    split = lax.axis_size("mz")
    size_x = local_x * lax.axis_size("gx")
    size_y = local_y * lax.axis_size("gy")
    devices = split * lax.axis_size("gx") * lax.axis_size("gy")
    at_m = lax.axis_index("mz")
    place = jnp.stack([lax.axis_index("gx"), lax.axis_index("gy"), at_m]).astype(jnp.int32)
    sizes = (local_bins, local_x, local_y, depth, elements, split, local_bins * split,
             size_x, size_y, devices)
    *mixed, moments = mix(place, kernel_taps, peak_bins, peak_share, counts, sizes, GROUPS)
    gathered = lax.all_to_all(moments, ("gx", "gy", "mz"), 0, 0, tiled=True)
    parts = []
    complete = {}
    for group, halves in enumerate(GROUPS):
        main, up, down = mixed[3 * group : 3 * group + 3]
        length = len(halves[0])
        from_above = shift(up, "gx", -1)
        from_below = shift(down, "gx", 1)
        spans = (slice(0, length), slice(length, 2 * length))

        def full(ahead, span):
            owner = (at_m + ahead) % split
            return (
                main[ahead, span]
                + jnp.where(owner == split - 1, from_above[span], 0.0)
                + jnp.where(owner == 0, from_below[span], 0.0)
            )

        leaf_up = turn(full(2, spans[0]), "mz", 1)
        leaf_down = turn(full(2, spans[1]), "mz", -1)
        direct_up = turn(full(1, spans[1]), "mz", 1)
        direct_down = turn(full(3, spans[0]), "mz", -1)
        late_up = turn(full(1, spans[0]) + leaf_up, "mz", 1)
        late_down = turn(full(3, spans[1]) + leaf_down, "mz", -1)
        own = full(0, slice(0, 2 * length))
        parts += [own, direct_down, direct_up, late_up, late_down]
        for half, (near, far) in enumerate(((direct_down, late_up), (direct_up, late_down))):
            for slot, row in enumerate(halves[half]):
                complete[row] = (own, half * length + slot, near, far, slot)

    def rows_of(rows):
        out = []
        for row in rows:
            own, index, near, far, slot = complete[row]
            out.append(own[index] + near[slot] + far[slot])
        return jnp.stack(out)

    before = shift(rows_of(range(local_y - REACH, local_y)), "gy", 1)
    after = shift(rows_of(range(REACH)), "gy", -1)
    result = finish(
        place, kernel_taps, gathered, before, after, parts,
        (local_y, depth, elements, split, local_x, size_x, size_y), GROUPS,
        squared_norms(size_x, size_y, depth),
    )
    return result.reshape(elements, local_x // split, local_y, depth)


def solution(mesh):
    return jax.shard_map(
        shards,
        mesh=mesh,
        in_specs=(P("mz", "gx", "gy", None), P(), P(), P()),
        out_specs=P(None, ("gx", "mz"), "gy", None),
        check_vma=False,
    )
```

time: 296 us -> 82.5 us (0.28)
  the two profiles are of different devices: /device:TPU:4 before, /device:TPU:98 now
where the time goes in v1:
time: 82.5 us; the launch traced here: 81.8 us
  starting transfers between devices  43.7 us (53%)
  waiting for transfers between devices  15 us (18%)
  Pallas kernels  12.5 us (15%)
  other arithmetic  7.55 us (9%)
  local copies, waits for them, and re-layouts  2.85 us (3%)
    all_to_all x1, starting transfers between devices, shards(): gathered = lax.all_to_all(moments, ('gx', 'gy', 'mz'), 0, 0, tiled=True)  24.5 us
    ppermute x4, waiting for transfers between devices, shift(): lax.ppermute(values, axis, [(i, i + by) for i in range(count) if 0 <= i +...  10.9 us
    ppermute x4, starting transfers between devices, shift(): lax.ppermute(values, axis, [(i, i + by) for i in range(count) if 0 <= i +...  10.7 us
    pallas_call x1, Pallas kernels, mix(): pl.pallas_call(functools.partial(mix_kernel, sizes, groups), out_shape=[j...  8.77 us
    ppermute x6, starting transfers between devices, turn(): lax.ppermute(values, axis, [(i, (i + by) % count) for i in range(count)])  8.5 us
    ppermute x6, waiting for transfers between devices, turn(): lax.ppermute(values, axis, [(i, (i + by) % count) for i in range(count)])  4.09 us
    add x2, other arithmetic, full(): main[ahead, span] + jnp.where(owner == split - 1, from_above[span], 0.0)  4.09 us
    pallas_call x1, Pallas kernels, finish(): pl.pallas_call(functools.partial(finish_kernel, sizes, groups, squares),...  3.72 us
  transfers between devices with their start and end apart: 11, of which 5 were waited for; matrix products, arithmetic and copies ran while one was open for 6% of the time, Pallas kernels for 0%

profile of v1, /device:TPU:98, one launch (start us, length us, event | category | flops | bytes accessed | tf_op | source)
XLA Modules:
  0.0 81.8 jit_solution(13041401936373000946)
XLA Ops:
  0.0 0.8 copy.7.bins_ref
  0.8 0.8 copy.8.share_ref
  1.5 0.1 pad_add_fusion.place_ref
  1.6 0.7 copy-done.2
  2.3 8.8 %mix_bins.1 = (f32[4,16,48,256]{3,2,1,0:T(8,128)S(1)}, f32[16,48,256]{2,1,0:T(8,128)}, f32[16,48,256]{2,1,0:T(8,128)}, f32[256,128]{1,0:T(8,128)S(1)}) custom-call(s32[3]{0:T(128)S(1)} %pad_add_fusion.place_ref, f32[3,5]{1,0:T(4,128)S(1)} %copy-done.2, s32[24,4]{1,0:T(8,128)S(1)} %copy.7.bins_ref, f32[24,4]{1,0:T(8,128)S(1)} %copy.8.share_ref, ...), custom_call_target="tpu_custom_call" | custom-call | flops 1207959552 | bytes 10485760 | tf_op jit(solution)/shard_map/mix_bins/pallas_call | solution.py:175
  11.1 0.6 copy-done.1
  11.7 2.6 %collective-permute-start.1 = (f32[16,48,256]{2,1,0:T(8,128)}, f32[16,48,256]{2,1,0:T(8,128)}, u32[]{:S(2)}, u32[]{:S(2)}) collective-permute-start(f32[16,48,256]{2,1,0:T(8,128)} %get-tuple-element.12), channel_id=1, source_target_pairs={{0,64},{64,128},{128,192},{1,65},{65,129},{129,193},{2,66},{66,130... | collective-permute-start | bytes 2359304 | tf_op jit(solution)/shard_map/ppermute | solution.py:278
  14.4 1.3 %collective-permute-start = (f32[16,48,256]{2,1,0:T(8,128)}, f32[16,48,256]{2,1,0:T(8,128)}, u32[]{:S(2)}, u32[]{:S(2)}) collective-permute-start(f32[16,48,256]{2,1,0:T(8,128)} %get-tuple-element.11), channel_id=1, source_target_pairs={{64,0},{128,64},{192,128},{65,1},{129,65},{193,129},{66,2},{130,66... | collective-permute-start | bytes 2359304 | tf_op jit(solution)/shard_map/ppermute | solution.py:278
  15.7 0.0 collective-permute-done.1
  15.7 4.2 %collective-permute-done = f32[16,48,256]{2,1,0:T(8,128)} collective-permute-done((f32[16,48,256]{2,1,0:T(8,128)}, f32[16,48,256]{2,1,0:T(8,128)}, u32[]{:S(2)}, u32[]{:S(2)}) %collective-permute-start) | collective-permute-done | bytes 786464 | tf_op jit(solution)/shard_map/ppermute | solution.py:278
  19.9 2.5 %fusion.4 = (f32[8,48,256]{2,1,0:T(8,128)}, f32[8,48,256]{2,1,0:T(8,128)S(1)}, f32[8,48,256]{2,1,0:T(8,128)S(1)}, f32[8,48,256]{2,1,0:T(8,128)}) fusion(f32[4,16,48,256]{3,2,1,0:T(8,128)S(1)} %get-tuple-element.10, f32[16,48,256]{2,1,0:T(8,128)} %collective-permute-done.1, f32[16,48,256]{2,1,0:T(8,128)} %collective-permute-done, pred[]{:T(512)S(6)} %eq.43, ...), kind=kLoop, calls=%fused_computation.8 | loop fusion | flops 1572864 | bytes 4718598 | tf_op jit(solution)/shard_map/add | solution.py:325
  22.4 1.6 %collective-permute-start.7 = (f32[8,48,256]{2,1,0:T(8,128)S(1)}, f32[8,48,256]{2,1,0:T(8,128)S(1)}, u32[]{:S(2)}, u32[]{:S(2)}) collective-permute-start(f32[8,48,256]{2,1,0:T(8,128)S(1)} %get-tuple-element.14), channel_id=1, source_target_pairs={{0,1},{1,2},{2,3},{3,0},{4,5},{5,6},{6,7},{7,4},{8,9},{9,10},{10,1... | collective-permute-start | bytes 1179656 | tf_op jit(solution)/shard_map/ppermute | solution.py:285
  24.0 1.7 %collective-permute-start.3 = (f32[8,48,256]{2,1,0:T(8,128)S(1)}, f32[8,48,256]{2,1,0:T(8,128)S(1)}, u32[]{:S(2)}, u32[]{:S(2)}) collective-permute-start(f32[8,48,256]{2,1,0:T(8,128)S(1)} %get-tuple-element.15), channel_id=1, source_target_pairs={{0,3},{1,0},{2,1},{3,2},{4,7},{5,4},{6,5},{7,6},{8,11},{9,8},{10,9... | collective-permute-start | bytes 1179656 | tf_op jit(solution)/shard_map/ppermute | solution.py:285
  25.7 1.8 %collective-permute-start.6 = (f32[8,48,256]{2,1,0:T(8,128)}, f32[8,48,256]{2,1,0:T(8,128)S(1)}, u32[]{:S(2)}, u32[]{:S(2)}) collective-permute-start(f32[8,48,256]{2,1,0:T(8,128)} %get-tuple-element.13), channel_id=1, source_target_pairs={{0,3},{1,0},{2,1},{3,2},{4,7},{5,4},{6,5},{7,6},{8,11},{9,8},{10,9... | collective-permute-start | bytes 1179656 | tf_op jit(solution)/shard_map/ppermute | solution.py:285
  27.5 0.2 collective-permute-start.2
  27.7 3.7 %collective-permute-done.7 = f32[8,48,256]{2,1,0:T(8,128)S(1)} collective-permute-done((f32[8,48,256]{2,1,0:T(8,128)S(1)}, f32[8,48,256]{2,1,0:T(8,128)S(1)}, u32[]{:S(2)}, u32[]{:S(2)}) %collective-permute-start.7) | collective-permute-done | bytes 393248 | tf_op jit(solution)/shard_map/ppermute | solution.py:285
  31.4 0.4 collective-permute-done.3
  31.8 2.5 %fusion.3 = (f32[8,48,256]{2,1,0:T(8,128)}, f32[8,48,256]{2,1,0:T(8,128)}) fusion(f32[8,48,256]{2,1,0:T(8,128)S(1)} %collective-permute-done.7, f32[4,16,48,256]{3,2,1,0:T(8,128)S(1)} %get-tuple-element.10, f32[16,48,256]{2,1,0:T(8,128)} %collective-permute-done.1, f32[16,48,256]{2,1,0:T(8,128)} %collective-permute-done, pred[]{:T(512)S(6)} %eq.41, ...), kind=kLoop, calls=%fused_computation.6 | loop fusion | flops 983040 | bytes 3932164 | tf_op jit(solution)/shard_map/add | solution.py:334
  34.3 1.6 %collective-permute-start.8 = (f32[8,48,256]{2,1,0:T(8,128)}, f32[8,48,256]{2,1,0:T(8,128)S(1)}, u32[]{:S(2)}, u32[]{:S(2)}) collective-permute-start(f32[8,48,256]{2,1,0:T(8,128)} %get-tuple-element.17), channel_id=1, source_target_pairs={{0,1},{1,2},{2,3},{3,0},{4,5},{5,6},{6,7},{7,4},{8,9},{9,10},{10,1... | collective-permute-start | bytes 1179656 | tf_op jit(solution)/shard_map/ppermute | solution.py:285
  35.9 1.7 %collective-permute-start.4 = (f32[8,48,256]{2,1,0:T(8,128)}, f32[8,48,256]{2,1,0:T(8,128)S(1)}, u32[]{:S(2)}, u32[]{:S(2)}) collective-permute-start(f32[8,48,256]{2,1,0:T(8,128)} %get-tuple-element.18), channel_id=1, source_target_pairs={{0,3},{1,0},{2,1},{3,2},{4,7},{5,4},{6,5},{7,6},{8,11},{9,8},{10,9... | collective-permute-start | bytes 1179656 | tf_op jit(solution)/shard_map/ppermute | solution.py:285
  37.5 24.5 %all-to-all-start = ((f32[256,1,128]{2,1,0:T(1,128)}), f32[256,1,128]{2,1,0:T(1,128)S(1)}, u32[]{:S(2)}, u32[]{:S(2)}) async-start(f32[256,1,128]{2,1,0:T(1,128)} %bitcast.42), calls=%async_computation | async-start | bytes 262144 | tf_op jit(solution)/shard_map/all_to_all | solution.py:312
  62.1 1.5 %fusion.rest_0_ = f32[16,48,256]{2,1,0:T(8,128)S(1)} fusion(f32[16,48,256]{2,1,0:T(8,128)} %collective-permute-done.1, f32[16,48,256]{2,1,0:T(8,128)} %collective-permute-done, f32[4,16,48,256]{3,2,1,0:T(8,128)} %copy-done, pred[]{:T(512)S(6)} %eq.39, pred[]{:T(512)S(6)} %eq.38), kind=kLoop, calls=%fused_computation.1 | loop fusion | flops 786432 | bytes 3145730 | tf_op jit(solution)/shard_map/add | solution.py:325
  63.6 0.0 collective-permute-done.6.rest_1_
  63.6 0.0 collective-permute-done.2.rest_2_
  63.7 0.0 collective-permute-done.8.rest_3_
  63.7 0.9 %slice_add_fusion.2 = (f32[1,48,256]{2,1,0:T(8,128)S(1)}, f32[1,48,256]{2,1,0:T(8,128)S(1)}, f32[1,48,256]{2,1,0:T(8,128)S(1)}, f32[1,48,256]{2,1,0:T(8,128)S(1)}) fusion(f32[8,48,256]{2,1,0:T(8,128)S(1)} %collective-permute-done.8.rest_3_, f32[8,48,256]{2,1,0:T(8,128)S(1)} %collective-permute-done.6.rest_1_, f32[16,48,256]{2,1,0:T(8,128)S(1)} %fusion.rest_0_, ...), kind=kLoop, calls=%fused_computation.20 | loop fusion | flops 98304 | bytes 786432 | tf_op jit(solution)/shard_map/add | solution.py:346
  64.6 4.8 %collective-permute-start.5 = (f32[2,48,256]{2,1,0:T(8,128)S(1)}, f32[2,48,256]{2,1,0:T(8,128)S(1)}, u32[]{:S(2)}, u32[]{:S(2)}) collective-permute-start(f32[2,48,256]{2,1,0:T(8,128)S(1)} %pad_maximum_fusion), channel_id=1, source_target_pairs={{0,4},{4,8},{8,12},{12,16},{16,20},{20,24},{24,28},{28,32},{32,36}... | collective-permute-start | bytes 294920 | tf_op jit(solution)/shard_map/ppermute | solution.py:278
  69.4 1.9 %collective-permute-start.9 = (f32[2,48,256]{2,1,0:T(8,128)S(1)}, f32[2,48,256]{2,1,0:T(8,128)S(1)}, u32[]{:S(2)}, u32[]{:S(2)}) collective-permute-start(f32[2,48,256]{2,1,0:T(8,128)S(1)} %pad_maximum_fusion.1), channel_id=1, source_target_pairs={{4,0},{8,4},{12,8},{16,12},{20,16},{24,20},{28,24},{32,28},{36,32}... | collective-permute-start | bytes 294920 | tf_op jit(solution)/shard_map/ppermute | solution.py:278
  71.4 0.0 all-to-all-done
  71.4 0.4 collective-permute-done.5.before_ref
  71.8 6.3 %collective-permute-done.9.after_ref = f32[2,48,256]{2,1,0:T(8,128)S(1)} collective-permute-done((f32[2,48,256]{2,1,0:T(8,128)S(1)}, f32[2,48,256]{2,1,0:T(8,128)S(1)}, u32[]{:S(2)}, u32[]{:S(2)}) %collective-permute-start.9) | collective-permute-done | bytes 98336 | tf_op jit(solution)/shard_map/ppermute | solution.py:278
  78.0 3.7 %finish.1 = f32[768,256]{1,0:T(8,128)} custom-call(s32[3]{0:T(128)S(1)} %pad_add_fusion.place_ref, f32[3,5]{1,0:T(4,128)S(1)} %copy-done.3, f32[256,128]{1,0:T(8,128)S(1)} %bitcast.41, f32[2,48,256]{2,1,0:T(8,128)S(1)} %collective-permute-done.5.before_ref, f32[2,48,256]{2,1,0:T(8,128)S(1)} %collective-permute-done.9.after_ref, ...), custom_call_target="tpu_custom_call" | custom-call | flops 5898240 | bytes 4194304 | tf_op jit(solution)/shard_map/finish/pallas_call | solution.py:258
  (9 shorter events, 0.0 us)
Async XLA Ops:
  1.6 0.7 copy-start.2
  11.1 0.7 copy-start.1
  11.7 22.6 %copy-start = (f32[4,16,48,256]{3,2,1,0:T(8,128)}, f32[4,16,48,256]{3,2,1,0:T(8,128)S(1)}, u32[]{:S(2)}) copy-start(f32[4,16,48,256]{3,2,1,0:T(8,128)S(1)} %get-tuple-element.10) | copy-start | bytes 9437188
  11.7 4.0 %collective-permute-start.1 = (f32[16,48,256]{2,1,0:T(8,128)}, f32[16,48,256]{2,1,0:T(8,128)}, u32[]{:S(2)}, u32[]{:S(2)}) collective-permute-start(f32[16,48,256]{2,1,0:T(8,128)} %get-tuple-element.12), channel_id=1, source_target_pairs={{0,64},{64,128},{128,192},{1,65},{65,129},{129,193},{2,66},{66,130... | collective-permute-start | bytes 2359304 | tf_op jit(solution)/shard_map/ppermute | solution.py:278
  14.4 5.5 %collective-permute-start = (f32[16,48,256]{2,1,0:T(8,128)}, f32[16,48,256]{2,1,0:T(8,128)}, u32[]{:S(2)}, u32[]{:S(2)}) collective-permute-start(f32[16,48,256]{2,1,0:T(8,128)} %get-tuple-element.11), channel_id=1, source_target_pairs={{64,0},{128,64},{192,128},{65,1},{129,65},{193,129},{66,2},{130,66... | collective-permute-start | bytes 2359304 | tf_op jit(solution)/shard_map/ppermute | solution.py:278
  22.4 9.0 %collective-permute-start.7 = (f32[8,48,256]{2,1,0:T(8,128)S(1)}, f32[8,48,256]{2,1,0:T(8,128)S(1)}, u32[]{:S(2)}, u32[]{:S(2)}) collective-permute-start(f32[8,48,256]{2,1,0:T(8,128)S(1)} %get-tuple-element.14), channel_id=1, source_target_pairs={{0,1},{1,2},{2,3},{3,0},{4,5},{5,6},{6,7},{7,4},{8,9},{9,10},{10,1... | collective-permute-start | bytes 1179656 | tf_op jit(solution)/shard_map/ppermute | solution.py:285
  24.0 7.8 %collective-permute-start.3 = (f32[8,48,256]{2,1,0:T(8,128)S(1)}, f32[8,48,256]{2,1,0:T(8,128)S(1)}, u32[]{:S(2)}, u32[]{:S(2)}) collective-permute-start(f32[8,48,256]{2,1,0:T(8,128)S(1)} %get-tuple-element.15), channel_id=1, source_target_pairs={{0,3},{1,0},{2,1},{3,2},{4,7},{5,4},{6,5},{7,6},{8,11},{9,8},{10,9... | collective-permute-start | bytes 1179656 | tf_op jit(solution)/shard_map/ppermute | solution.py:285
  25.7 38.0 %collective-permute-start.6 = (f32[8,48,256]{2,1,0:T(8,128)}, f32[8,48,256]{2,1,0:T(8,128)S(1)}, u32[]{:S(2)}, u32[]{:S(2)}) collective-permute-start(f32[8,48,256]{2,1,0:T(8,128)} %get-tuple-element.13), channel_id=1, source_target_pairs={{0,3},{1,0},{2,1},{3,2},{4,7},{5,4},{6,5},{7,6},{8,11},{9,8},{10,9... | collective-permute-start | bytes 1179656 | tf_op jit(solution)/shard_map/ppermute | solution.py:285
  27.5 36.2 %collective-permute-start.2 = (f32[8,48,256]{2,1,0:T(8,128)}, f32[8,48,256]{2,1,0:T(8,128)}, u32[]{:S(2)}, u32[]{:S(2)}) collective-permute-start(f32[8,48,256]{2,1,0:T(8,128)} %get-tuple-element.16), channel_id=1, source_target_pairs={{0,1},{1,2},{2,3},{3,0},{4,5},{5,6},{6,7},{7,4},{8,9},{9,10},{10,1... | collective-permute-start | bytes 1179656 | tf_op jit(solution)/shard_map/ppermute | solution.py:285
  34.3 43.8 %copy-start.3 = (f32[3,5]{1,0:T(4,128)S(1)}, f32[3,5]{1,0:T(4,128)}, u32[]{:S(2)}) copy-start(f32[3,5]{1,0:T(4,128)} %taps_ref.3) | copy-start | bytes 184
  34.3 29.4 %collective-permute-start.8 = (f32[8,48,256]{2,1,0:T(8,128)}, f32[8,48,256]{2,1,0:T(8,128)S(1)}, u32[]{:S(2)}, u32[]{:S(2)}) collective-permute-start(f32[8,48,256]{2,1,0:T(8,128)} %get-tuple-element.17), channel_id=1, source_target_pairs={{0,1},{1,2},{2,3},{3,0},{4,5},{5,6},{6,7},{7,4},{8,9},{9,10},{10,1... | collective-permute-start | bytes 1179656 | tf_op jit(solution)/shard_map/ppermute | solution.py:285
  35.9 27.8 %collective-permute-start.4 = (f32[8,48,256]{2,1,0:T(8,128)}, f32[8,48,256]{2,1,0:T(8,128)S(1)}, u32[]{:S(2)}, u32[]{:S(2)}) collective-permute-start(f32[8,48,256]{2,1,0:T(8,128)} %get-tuple-element.18), channel_id=1, source_target_pairs={{0,3},{1,0},{2,1},{3,2},{4,7},{5,4},{6,5},{7,6},{8,11},{9,8},{10,9... | collective-permute-start | bytes 1179656 | tf_op jit(solution)/shard_map/ppermute | solution.py:285
  37.5 33.8 %all-to-all-start = ((f32[256,1,128]{2,1,0:T(1,128)}), f32[256,1,128]{2,1,0:T(1,128)S(1)}, u32[]{:S(2)}, u32[]{:S(2)}) async-start(f32[256,1,128]{2,1,0:T(1,128)} %bitcast.42), calls=%async_computation | async-start | bytes 262144 | tf_op jit(solution)/shard_map/all_to_all | solution.py:312
  64.6 7.2 %collective-permute-start.5 = (f32[2,48,256]{2,1,0:T(8,128)S(1)}, f32[2,48,256]{2,1,0:T(8,128)S(1)}, u32[]{:S(2)}, u32[]{:S(2)}) collective-permute-start(f32[2,48,256]{2,1,0:T(8,128)S(1)} %pad_maximum_fusion), channel_id=1, source_target_pairs={{0,4},{4,8},{8,12},{12,16},{16,20},{20,24},{24,28},{28,32},{32,36}... | collective-permute-start | bytes 294920 | tf_op jit(solution)/shard_map/ppermute | solution.py:278
  69.4 8.6 %collective-permute-start.9 = (f32[2,48,256]{2,1,0:T(8,128)S(1)}, f32[2,48,256]{2,1,0:T(8,128)S(1)}, u32[]{:S(2)}, u32[]{:S(2)}) collective-permute-start(f32[2,48,256]{2,1,0:T(8,128)S(1)} %pad_maximum_fusion.1), channel_id=1, source_target_pairs={{4,0},{8,4},{12,8},{16,12},{20,16},{24,20},{28,24},{32,28},{36,32}... | collective-permute-start | bytes 294920 | tf_op jit(solution)/shard_map/ppermute | solution.py:278

commit v2 on v1

v2 whole, which is shorter than its diff:
```python
import functools

import jax
import jax.numpy as jnp
from jax import lax
from jax.experimental import pallas as pl
from jax.experimental.pallas import tpu as pltpu
from jax.sharding import PartitionSpec as P

RIDGE_WEIGHT = 0.5
TAPS = 5
REACH = 2
LANES = 128
HIGHEST = lax.Precision.HIGHEST
MIB = 1024 * 1024

def iota(shape, dim):
    return lax.broadcasted_iota(jnp.int32, shape, dim)


def normalized(taps_ref):
    taps = taps_ref[...]
    return taps / jnp.sum(taps, axis=1, keepdims=True)


def tap(weights, axis, offset):
    return weights[axis : axis + 1, offset : offset + 1]


def adjoint(weights, axis, positions, extent):
    ones = jnp.zeros(positions.shape, jnp.float32)
    linear = jnp.zeros(positions.shape, jnp.float32)
    for offset in range(TAPS):
        target = positions - (offset - REACH)
        inside = (target >= 0) & (target < extent)
        weight = jnp.where(inside, tap(weights, axis, offset), 0.0)
        coordinate = (2.0 * target.astype(jnp.float32) + 1.0) / float(extent) - 1.0
        ones = ones + weight
        linear = linear + weight * coordinate
    return ones, linear


def unmix_rows(bins_ref, share_ref, all_bins):
    peaks, elements = bins_ref.shape
    bins = bins_ref[...]
    share = share_ref[...]
    rows = iota((all_bins, elements), 0)
    mixing = jnp.zeros((all_bins, elements), jnp.float32)
    for peak in range(peaks):
        mixing = mixing + jnp.where(
            rows == bins[peak : peak + 1, :], share[peak : peak + 1, :], 0.0
        )

    def transposed_product(values):
        return lax.dot_general(
            mixing, values, (((0,), (0,)), ((), ())), precision=HIGHEST,
            preferred_element_type=jnp.float32,
        )

    left = transposed_product(mixing)
    full = (all_bins, all_bins)
    mixing_t = transposed_product(jnp.where(iota(full, 0) == iota(full, 1), 1.0, 0.0))
    square = (elements, elements)
    left = left + jnp.where(iota(square, 0) == iota(square, 1), RIDGE_WEIGHT, 0.0)
    right = mixing_t
    for step in range(elements):
        inverse = 1.0 / left[step : step + 1, step : step + 1]
        left_row = left[step : step + 1, :] * inverse
        right_row = right[step : step + 1, :] * inverse
        column = left[:, step : step + 1]
        here = iota((elements, 1), 0) == step
        left = jnp.where(here, left_row, left - column * left_row)
        right = jnp.where(here, right_row, right - column * right_row)
    return right


def position(axis):
    return lax.axis_index(axis)


def coordinate(at, extent):
    return (2.0 * lax.convert_element_type(at, jnp.float32) + 1.0) / float(extent) - 1.0


def split_pieces(wide):
    high = wide.astype(jnp.bfloat16)
    return high, (wide - high.astype(jnp.float32)).astype(jnp.bfloat16)


def lane_parts(depth):
    return range(depth // LANES)


def plane_of(held, row, count, stride):
    parts = [held[lane, pl.ds(row, count, stride=stride), :] for lane in range(held.shape[0])]
    return jnp.concatenate(parts, axis=1).astype(jnp.float32).astype(jnp.bfloat16)


def fill_table(table, spread, layer, targets, weights):
    elements = spread.shape[0]
    for place, target in enumerate(targets):
        factor = jnp.zeros(layer.shape, jnp.float32)
        for offset in range(TAPS):
            factor = jnp.where(layer - target + REACH == offset, tap(weights, 0, offset), factor)
        table[pl.ds(place * elements, elements), :] = spread * factor
    return split_pieces(table[...])


def product(high, low, plane):
    return jnp.dot(high, plane, preferred_element_type=jnp.float32) + jnp.dot(
        low, plane, preferred_element_type=jnp.float32
    )


def add_sums(sums, mixed, ones_y, linear_y, row, first):
    plain = mixed * ones_y[row : row + 1, :]
    tilted = mixed * linear_y[row : row + 1, :]
    if first:
        sums[0], sums[1] = plain, tilted
    else:
        sums[0] += plain
        sums[1] += tilted


def plane_moments(parts, sums, targets, elements, local_x, size_x):
    for place, target in enumerate(targets):
        x = position("gx") * local_x + target
        inside = jnp.where((x >= 0) & (x < size_x), 1.0, 0.0)
        rows = pl.ds(place * elements, elements)
        plain = sums[0, rows, :] * inside
        parts[0] = parts[0] + plain
        parts[1] = parts[1] + plain * coordinate(x, size_x)
        parts[2] = parts[2] + sums[1, rows, :] * inside
    return parts


def mix_kernel(sizes, taps_hbm, bins_hbm, share_hbm, counts_ref, main_ref, up_ref, down_ref, moments_ref,
               taps_ref, bins_ref, share_ref, held, table, sums, small_sem, sem):
    local_bins, local_x, local_y, depth, elements, split, all_bins, size_x, size_y = sizes
    rows_in = local_bins * local_x
    small = [
        pltpu.make_async_copy(source, target, small_sem.at[i])
        for i, (source, target) in enumerate(
            ((taps_hbm, taps_ref), (bins_hbm, bins_ref), (share_hbm, share_ref))
        )
    ]
    copies = [
        pltpu.make_async_copy(
            counts_ref.at[:, pl.ds(lane * LANES, LANES)], held.at[lane], sem.at[lane]
        )
        for lane in lane_parts(depth)
    ]
    for copy in small + copies:
        copy.start()
    for copy in small:
        copy.wait()
    weights = normalized(taps_ref)
    unmix = unmix_rows(bins_ref, share_ref, all_bins)
    shape = (all_bins, rows_in)
    expand = jnp.where(
        iota(shape, 0) == position("mz") * local_bins + iota(shape, 1) // local_x, 1.0, 0.0
    )
    spread = jnp.dot(unmix, expand, precision=HIGHEST, preferred_element_type=jnp.float32)
    layer = iota((1, rows_in), 1) % local_x
    targets = []
    for ahead in range(split):
        owner = (position("mz") + ahead) % split
        targets += [owner * REACH + j for j in range(REACH)]
    targets += [j - REACH for j in range(REACH)] + [local_x + j for j in range(REACH)]
    high, low = fill_table(table, spread, layer, targets, weights)
    rows_y = position("gy") * local_y + iota((local_y, depth), 0)
    ones_y, linear_y = adjoint(weights, 1, rows_y, size_y)
    block = REACH * elements
    for copy in copies:
        copy.wait()
    for row in range(local_y):
        mixed = product(high, low, plane_of(held, row, rows_in, local_y))
        for ahead in range(split):
            main_ref[ahead, row] = mixed[ahead * block : (ahead + 1) * block]
        up_ref[row] = mixed[split * block : (split + 1) * block]
        down_ref[row] = mixed[(split + 1) * block :]
        add_sums(sums, mixed, ones_y, linear_y, row, row == 0)
    parts = [jnp.zeros((elements, depth), jnp.float32) for _ in range(3)]
    parts = plane_moments(parts, sums, targets, elements, local_x, size_x)
    rest = jnp.zeros((LANES - 4 * elements, depth), jnp.float32)
    stacked = jnp.concatenate([parts[0], parts[1], parts[2], parts[0], rest], axis=0)
    ones_z, linear_z = adjoint(weights, 2, iota((8, depth), 1), depth)
    profile = jnp.where(iota((8, depth), 0) == 0, ones_z, linear_z)
    products = lax.dot_general(
        profile, stacked, (((1,), (1,)), ((), ())), precision=HIGHEST,
        preferred_element_type=jnp.float32,
    )
    row = jnp.where(iota((1, LANES), 1) < 3 * elements, products[0:1], products[1:2])
    moments_ref[...] = jnp.broadcast_to(row, moments_ref.shape)


def mix(taps, bins, share, counts, sizes, peers):
    local_bins, local_x, local_y, depth, elements, split, _, _, _ = sizes
    block = REACH * elements
    rows_in = local_bins * local_x
    rows_out = (split + 2) * block
    vmem = pl.BlockSpec(memory_space=pltpu.VMEM)
    hbm = pl.BlockSpec(memory_space=pltpu.HBM)
    shapes = [(split, local_y, block, depth)] + [(local_y, block, depth)] * 2 + [(8, LANES)]
    return pl.pallas_call(
        functools.partial(mix_kernel, sizes),
        out_shape=[jax.ShapeDtypeStruct(shape, jnp.float32) for shape in shapes],
        in_specs=[hbm] * 4,
        out_specs=[vmem] * len(shapes),
        scratch_shapes=[
            pltpu.VMEM(taps.shape, jnp.float32),
            pltpu.VMEM(bins.shape, jnp.int32),
            pltpu.VMEM(share.shape, jnp.float32),
            pltpu.VMEM((depth // LANES, rows_in * local_y, LANES), jnp.int32),
            pltpu.VMEM((rows_out, rows_in), jnp.float32),
            pltpu.VMEM((2, rows_out, depth), jnp.float32),
            pltpu.SemaphoreType.DMA((3,)),
            pltpu.SemaphoreType.DMA((depth // LANES,)),
        ],
        compiler_params=pltpu.CompilerParams(vmem_limit_bytes=12 * MIB),
        cost_estimate=pl.CostEstimate(
            flops=4 * rows_out * rows_in * local_y * depth,
            bytes_accessed=8 << 20,
            transcendentals=0,
        ),
        name="mix_bins",
    )(*[
        pltpu.with_memory_space_constraint(values, pltpu.HBM)
        for values in (taps, bins, share, counts.reshape(-1, depth))
    ])


def owner_flags(ahead, split):
    owner = (position("mz") + ahead) % split
    above = jnp.where(owner == split - 1, 1.0, 0.0)
    below = jnp.where(owner == 0, 1.0, 0.0)
    return above, below


def with_edges(main_ref, above_ref, below_ref, flags, ahead, row):
    return main_ref[ahead, row] + flags[0] * above_ref[row] + flags[1] * below_ref[row]


def rows_at(slot, block):
    return pl.ds(slot * block, block)


def add_kernel(*refs):
    total = refs[0][...]
    for ref in refs[1:-1]:
        total = total + ref[...]
    refs[-1][...] = total


def peers_kernel(gathered_ref, out_ref):
    total = gathered_ref[0:8]
    for peer in range(1, gathered_ref.shape[0] // 8):
        total = total + gathered_ref[8 * peer : 8 * peer + 8]
    out_ref[...] = total


def first_kernel(split, half, main_ref, above_ref, below_ref, moments_ref, other_ref, up_ref, down_ref,
                 spread_ref):
    block = main_ref.shape[2]
    total = moments_ref[...] + other_ref[...]
    for peer in range(spread_ref.shape[0] // 8):
        spread_ref[8 * peer : 8 * peer + 8] = total
    for out, pieces in ((up_ref, ((2, 0), (1, half))), (down_ref, ((2, half), (3, 0)))):
        for place, (ahead, base) in enumerate(pieces):
            flags = owner_flags(ahead, split)
            for slot in range(half):
                out[rows_at(place * half + slot, block), :] = with_edges(
                    main_ref, above_ref, below_ref, flags, ahead, base + slot
                )


def late_kernel(split, half, main_ref, above_ref, below_ref, up_ref, down_ref, gathered_ref,
                late_up, late_down, summed_ref):
    peers_kernel(gathered_ref, summed_ref)
    block = main_ref.shape[2]
    for ahead, base, leaf, out in ((1, 0, up_ref, late_up), (3, half, down_ref, late_down)):
        flags = owner_flags(ahead, split)
        for slot in range(half):
            rows = rows_at(slot, block)
            value = with_edges(main_ref, above_ref, below_ref, flags, ahead, base + slot)
            out[rows, :] = value + leaf[rows, :]


def own_kernel(split, half, main_ref, above_ref, below_ref, up_ref, down_ref, out_ref):
    block = main_ref.shape[2]
    flags = owner_flags(0, split)
    for row in range(2 * half):
        direct = down_ref if row < half else up_ref
        out_ref[rows_at(row, block), :] = (
            with_edges(main_ref, above_ref, below_ref, flags, 0, row)
            + direct[rows_at(half + row % half, block), :]
        )


def rim_kernel(half, block, own_ref, late_up, late_down, moments_ref, other_ref,
               low_ref, high_ref, summed_ref):
    summed_ref[...] = moments_ref[...] + other_ref[...]
    low, high = pl.ds(0, REACH * block), pl.ds((half - REACH) * block, REACH * block)
    low_ref[...] = own_ref[low, :] + late_up[low, :]
    high_ref[...] = own_ref[pl.ds((2 * half - REACH) * block, REACH * block), :] + late_down[high, :]


def local_call(kernel, shapes, args, name, weight=1):
    vmem = pl.BlockSpec(memory_space=pltpu.VMEM)
    size = sum(a.size for a in args) * 4 * weight
    return pl.pallas_call(
        kernel,
        out_shape=[jax.ShapeDtypeStruct(shape, jnp.float32) for shape in shapes],
        in_specs=[vmem] * len(args),
        out_specs=[vmem] * len(shapes),
        compiler_params=pltpu.CompilerParams(vmem_limit_bytes=4 * MIB),
        cost_estimate=pl.CostEstimate(flops=size, bytes_accessed=size, transcendentals=0),
        name=name,
    )(*args)


def finish_kernel(sizes, squares, taps_hbm, before_ref, after_ref, low_ref, high_ref,
                  own_ref, late_up, late_down, *rest):
    moments, (out_ref, taps_ref, turned, sem) = rest[:-4], rest[-4:]
    local_y, depth, elements, split, local_x, size_x, size_y = sizes
    copy = pltpu.make_async_copy(taps_hbm, taps_ref, sem)
    copy.start()
    half = local_y // 2
    block = REACH * elements
    copy.wait()
    weights = normalized(taps_ref)
    planes = {}
    for j in range(REACH):
        rows = rows_at(j, block)
        planes[j - REACH] = before_ref[rows, :]
        planes[local_y + j] = after_ref[rows, :]
        planes[j] = low_ref[rows, :]
        planes[local_y - REACH + j] = high_ref[rows, :]
    for row in range(REACH, local_y - REACH):
        late = late_up if row < half else late_down
        planes[row] = own_ref[rows_at(row, block), :] + late[rows_at(row % half, block), :]
    totals = moments[0][0:1]
    for other in moments[1:]:
        totals = totals + other[0:1]
    lanes = iota((elements, LANES), 1)
    rows = iota((elements, LANES), 0)
    fitted = [
        jnp.sum(jnp.where(lanes == rows + j * elements, totals, 0.0), axis=1, keepdims=True)
        / squares[j]
        for j in range(4)
    ]
    at = position("gx") * local_x + position("mz") * REACH
    base = jnp.concatenate(
        [fitted[0] + fitted[1] * coordinate(at + j, size_x) for j in range(REACH)], axis=0
    )
    slope_y = jnp.concatenate([fitted[2]] * REACH, axis=0)
    slope_z = jnp.concatenate([fitted[3]] * REACH, axis=0)
    line = iota((1, depth), 1)
    tilted = base + slope_z * coordinate(line, depth)
    edge = []
    for offset in range(TAPS):
        source = line + (offset - REACH)
        edge.append(jnp.where((source >= 0) & (source < depth), tap(weights, 2, offset), 0.0))
    for row in range(local_y):
        smooth = tap(weights, 1, 0) * planes[row - REACH]
        for offset in range(1, TAPS):
            smooth = smooth + tap(weights, 1, offset) * planes[row + offset - REACH]
        result = -(tilted + slope_y * coordinate(position("gy") * local_y + row, size_y))
        for offset in range(TAPS):
            shifted = smooth if offset == REACH else pltpu.roll(smooth, (REACH - offset) % depth, 1)
            result = result + edge[offset] * shifted
        for j in range(REACH):
            for lane in lane_parts(depth):
                turned[lane, pl.ds(j * local_y + row, elements, stride=REACH * local_y), :] = result[
                    j * elements : (j + 1) * elements, lane * LANES : (lane + 1) * LANES
                ]
    for lane in lane_parts(depth):
        out_ref[:, lane * LANES : (lane + 1) * LANES] = turned[lane]


def finish(taps, args, sizes, squares):
    local_y, depth, elements = sizes[:3]
    vmem = pl.BlockSpec(memory_space=pltpu.VMEM)
    hbm = pl.BlockSpec(memory_space=pltpu.HBM)
    rows = elements * REACH * local_y
    return pl.pallas_call(
        functools.partial(finish_kernel, sizes, squares),
        out_shape=jax.ShapeDtypeStruct((rows, depth), jnp.float32),
        in_specs=[hbm] + [vmem] * len(args),
        out_specs=vmem,
        scratch_shapes=[
            pltpu.VMEM(taps.shape, jnp.float32),
            pltpu.VMEM((depth // LANES, rows, LANES), jnp.float32),
            pltpu.SemaphoreType.DMA,
        ],
        compiler_params=pltpu.CompilerParams(vmem_limit_bytes=8 * MIB),
        cost_estimate=pl.CostEstimate(
            flops=30 * rows * depth, bytes_accessed=4 << 20, transcendentals=0
        ),
        name="finish",
    )(pltpu.with_memory_space_constraint(taps, pltpu.HBM), *args)


def shift(values, axis, by):
    count = lax.axis_size(axis)
    return lax.ppermute(
        values, axis, [(i, i + by) for i in range(count) if 0 <= i + by < count]
    )


def turn(values, axis, by):
    count = lax.axis_size(axis)
    return lax.ppermute(values, axis, [(i, (i + by) % count) for i in range(count)])


def squared_norms(size_x, size_y, size_z):
    def of(extent):
        return sum(((2.0 * i + 1.0) / extent - 1.0) ** 2 for i in range(extent))

    return (
        float(size_x * size_y * size_z),
        of(size_x) * size_y * size_z,
        of(size_y) * size_x * size_z,
        of(size_z) * size_x * size_y,
    )


def shards(counts, kernel_taps, peak_bins, peak_share):
    local_bins, local_x, local_y, depth = counts.shape
    elements = peak_bins.shape[0]
    split = lax.axis_size("mz")
    across = lax.axis_size("gx")
    along = lax.axis_size("gy")
    size_x = local_x * across
    size_y = local_y * along
    half = local_y // 2
    block = REACH * elements
    sizes = (local_bins, local_x, local_y, depth, elements, split, local_bins * split, size_x, size_y)
    tile = (8, LANES)
    main, up, down, moments = mix(
        kernel_taps, peak_bins.T, peak_share.T, counts, sizes, across * split
    )
    from_above = shift(up, "gx", -1)
    from_below = shift(down, "gx", 1)
    (moments,) = local_call(add_kernel, [tile], (moments, turn(moments, "mz", 1)), "add_sums")
    blocks = (main, from_above, from_below)
    both = (2 * half * block, depth)
    whole = (half * block, depth)
    up, down, spread = local_call(
        functools.partial(first_kernel, split, half), [both, both, (8 * along, LANES)],
        blocks + (moments, turn(moments, "mz", 2)), "first_blocks",
    )
    up = turn(up, "mz", 1)
    down = turn(down, "mz", -1)
    gathered = lax.all_to_all(spread, "gy", 0, 0, tiled=True)
    late_up, late_down, moments = local_call(
        functools.partial(late_kernel, split, half), [whole, whole, tile],
        blocks + (up, down, gathered), "late_blocks",
    )
    late_up = turn(late_up, "mz", 1)
    late_down = turn(late_down, "mz", -1)
    (own,) = local_call(
        functools.partial(own_kernel, split, half), [(local_y * block, depth)],
        blocks + (up, down), "own_blocks",
    )
    (moments,) = local_call(add_kernel, [tile], (moments, turn(moments, "gx", 1)), "add_sums")
    rim = (REACH * block, depth)
    low, high, moments = local_call(
        functools.partial(rim_kernel, half, block), [rim, rim, tile],
        (own, late_up, late_down, moments, turn(moments, "gx", 2)), "rim_blocks",
    )
    before = shift(high, "gy", 1)
    after = shift(low, "gy", -1)
    result = finish(
        kernel_taps,
        (before, after, low, high, own, late_up, late_down, moments),
        (local_y, depth, elements, split, local_x, size_x, size_y),
        squared_norms(size_x, size_y, depth),
    )
    return result.reshape(elements, local_x // split, local_y, depth)


def solution(mesh):
    return jax.shard_map(
        shards,
        mesh=mesh,
        in_specs=(P("mz", "gx", "gy", None), P(), P(), P()),
        out_specs=P(None, ("gx", "mz"), "gy", None),
        check_vma=False,
    )
```

time: 82.5 us -> 73.3 us (0.89)
  starting transfers between devices: 43.7 us -> 22.4 us
  blocking collectives: 0 us -> 13.9 us
  waiting for transfers between devices: 15 us -> 25.9 us
  other arithmetic: 7.55 us -> 0 us
  local copies, waits for them, and re-layouts: 2.85 us -> 0 us
  Pallas kernels: 12.5 us -> 10.8 us
    all_to_all x1 -> x0, starting transfers between devices: 24.5 us -> none  [shards(): gathered = lax.all_to_all(moments, ('gx', 'gy', 'mz'), 0, 0, tiled=True)]
    ppermute x6 -> x8, waiting for transfers between devices: 4.09 us -> 19.2 us  [turn(): lax.ppermute(values, axis, [(i, (i + by) % count) for i in range(count)])]
    all_to_all x0 -> x1, blocking collectives: none -> 13.9 us  [shards(): gathered = lax.all_to_all(spread, 'gy', 0, 0, tiled=True)]
    add x4 -> x0, other arithmetic: 7.46 us -> none  [the longest x2 4.09 us: full(): main[ahead, span] + jnp.where(owner == split - 1, from_above[span], 0.0)]
    ppermute x4, waiting for transfers between devices: 10.9 us -> 6.7 us  [shift(): lax.ppermute(values, axis, [(i, i + by) for i in range(count) if 0 <= i +...]
    unnamed x10 -> x0, local copies, waits for them, and re-layouts: 2.85 us -> none
    ppermute x6 -> x8, starting transfers between devices: 8.5 us -> 11.1 us  [turn(): lax.ppermute(values, axis, [(i, (i + by) % count) for i in range(count)])]
    pallas_call x2 -> x8, Pallas kernels: 12.5 us -> 10.8 us  [the longest x1 6.59 us: mix(): pl.pallas_call(functools.partial(mix_kernel, sizes), out_shape=[jax.Shape...]
  transfers between devices with their start and end apart: 11 -> 12, of which waited for: 5 -> 7; matrix products, arithmetic and copies ran while one was open for 6% -> 0% of each run, Pallas kernels for 0% -> 0%
where the time goes in v2:
time: 73.3 us; the launch traced here: 73.1 us
  waiting for transfers between devices  25.9 us (35%)
  starting transfers between devices  22.4 us (31%)
  blocking collectives  13.9 us (19%)
  Pallas kernels  10.8 us (15%)
    ppermute x8, waiting for transfers between devices, turn(): lax.ppermute(values, axis, [(i, (i + by) % count) for i in range(count)])  19.2 us
    all_to_all x1, blocking collectives, shards(): gathered = lax.all_to_all(spread, 'gy', 0, 0, tiled=True)  13.9 us
    ppermute x4, starting transfers between devices, shift(): lax.ppermute(values, axis, [(i, i + by) for i in range(count) if 0 <= i +...  11.3 us
    ppermute x8, starting transfers between devices, turn(): lax.ppermute(values, axis, [(i, (i + by) % count) for i in range(count)])  11.1 us
    ppermute x4, waiting for transfers between devices, shift(): lax.ppermute(values, axis, [(i, i + by) for i in range(count) if 0 <= i +...  6.7 us
    pallas_call x1, Pallas kernels, mix(): pl.pallas_call(functools.partial(mix_kernel, sizes), out_shape=[jax.Shape...  6.59 us
    pallas_call x1, Pallas kernels, finish(): pl.pallas_call(functools.partial(finish_kernel, sizes, squares), out_shap...  3.4 us
  transfers between devices with their start and end apart: 12, of which 7 were waited for; matrix products, arithmetic and copies ran while one was open for 0% of the time, Pallas kernels for 0%

profile of v2, /device:TPU:98, one launch (start us, length us, event | category | flops | bytes accessed | tf_op | source)
XLA Modules:
  0.0 73.1 jit_solution(12950575517936894850)
XLA Ops:
  0.0 6.6 %mix_bins.1 = (f32[4,16,48,256]{3,2,1,0:T(8,128)S(1)}, f32[16,48,256]{2,1,0:T(8,128)S(1)}, f32[16,48,256]{2,1,0:T(8,128)S(1)}, f32[8,128]{1,0:T(8,128)S(1)}) custom-call(f32[3,5]{1,0:T(4,128)} %taps_hbm.3, s32[4,24]{1,0:T(4,128)} %bitcast.9, f32[4,24]{1,0:T(4,128)} %bitcast.10, s32[4096,256]{1,0:T(8,128)} %bitcast.8), custom_call_target="tpu_custom_call" | custom-call | flops 1207959552 | bytes 8388608 | tf_op jit(solution)/shard_map/mix_bins/pallas_call | solution.py:205
  6.6 1.3 %collective-permute-start = (f32[16,48,256]{2,1,0:T(8,128)S(1)}, f32[16,48,256]{2,1,0:T(8,128)S(1)}, u32[]{:S(2)}, u32[]{:S(2)}) collective-permute-start(f32[16,48,256]{2,1,0:T(8,128)S(1)} %get-tuple-element.19), channel_id=1, source_target_pairs={{64,0},{128,64},{192,128},{65,1},{129,65},{193,129},{66,2},{130,66... | collective-permute-start | bytes 2359304 | tf_op jit(solution)/shard_map/ppermute | solution.py:406
  7.9 3.1 %collective-permute-start.1 = (f32[16,48,256]{2,1,0:T(8,128)S(1)}, f32[16,48,256]{2,1,0:T(8,128)S(1)}, u32[]{:S(2)}, u32[]{:S(2)}) collective-permute-start(f32[16,48,256]{2,1,0:T(8,128)S(1)} %get-tuple-element.20), channel_id=1, source_target_pairs={{0,64},{64,128},{128,192},{1,65},{65,129},{129,193},{2,66},{66,130... | collective-permute-start | bytes 2359304 | tf_op jit(solution)/shard_map/ppermute | solution.py:406
  11.0 1.7 %collective-permute-start.2 = (f32[8,128]{1,0:T(8,128)S(1)}, f32[8,128]{1,0:T(8,128)S(1)}, u32[]{:S(2)}, u32[]{:S(2)}) collective-permute-start(f32[8,128]{1,0:T(8,128)S(1)} %get-tuple-element.21.refs_0_), channel_id=1, source_target_pairs={{0,1},{1,2},{2,3},{3,0},{4,5},{5,6},{6,7},{7,4},{8,9},{9,10},{10,1... | collective-permute-start | bytes 12296 | tf_op jit(solution)/shard_map/ppermute | solution.py:413
  12.6 3.2 %collective-permute-done.2.refs_1_ = f32[8,128]{1,0:T(8,128)S(1)} collective-permute-done((f32[8,128]{1,0:T(8,128)S(1)}, f32[8,128]{1,0:T(8,128)S(1)}, u32[]{:S(2)}, u32[]{:S(2)}) %collective-permute-start.2) | collective-permute-done | bytes 4128 | tf_op jit(solution)/shard_map/ppermute | solution.py:413
  15.9 2.0 %collective-permute-start.3 = (f32[8,128]{1,0:T(8,128)S(1)}, f32[8,128]{1,0:T(8,128)S(1)}, u32[]{:S(2)}, u32[]{:S(2)}) collective-permute-start(f32[8,128]{1,0:T(8,128)S(1)} %add_sums.2.moments_ref), channel_id=1, source_target_pairs={{0,2},{1,3},{2,0},{3,1},{4,6},{5,7},{6,4},{7,5},{8,10},{9,11},{10,... | collective-permute-start | bytes 12296 | tf_op jit(solution)/shard_map/ppermute | solution.py:413
  17.9 3.1 %collective-permute-done.3.other_ref = f32[8,128]{1,0:T(8,128)S(1)} collective-permute-done((f32[8,128]{1,0:T(8,128)S(1)}, f32[8,128]{1,0:T(8,128)S(1)}, u32[]{:S(2)}, u32[]{:S(2)}) %collective-permute-start.3) | collective-permute-done | bytes 4128 | tf_op jit(solution)/shard_map/ppermute | solution.py:413
  21.0 0.0 collective-permute-done.above_ref
  21.0 0.0 collective-permute-done.1.below_ref
  21.0 0.3 first_blocks.1
  21.3 0.4 collective-permute-start.4
  21.8 2.9 %collective-permute-start.5 = (f32[768,256]{1,0:T(8,128)S(1)}, f32[768,256]{1,0:T(8,128)S(1)}, u32[]{:S(2)}, u32[]{:S(2)}) collective-permute-start(f32[768,256]{1,0:T(8,128)S(1)} %get-tuple-element.23), channel_id=1, source_target_pairs={{0,3},{1,0},{2,1},{3,2},{4,7},{5,4},{6,5},{7,6},{8,11},{9,8},{10,9... | collective-permute-start | bytes 2359304 | tf_op jit(solution)/shard_map/ppermute | solution.py:413
  24.6 13.9 %all_to_all.11 = f32[16,8,128]{2,1,0:T(8,128)S(1)} all-to-all(f32[16,8,128]{2,1,0:T(8,128)S(1)} %bitcast.7), channel_id=1, replica_groups=mesh['gx'=4,'gy'=16,'mz'=4] {'gy'}, dimensions={0} | all-to-all | bytes 131072 | tf_op jit(solution)/shard_map/all_to_all | solution.py:455
  38.6 4.0 %collective-permute-done.4.up_ref = f32[768,256]{1,0:T(8,128)S(1)} collective-permute-done((f32[768,256]{1,0:T(8,128)S(1)}, f32[768,256]{1,0:T(8,128)S(1)}, u32[]{:S(2)}, u32[]{:S(2)}) %collective-permute-start.4) | collective-permute-done | bytes 786464 | tf_op jit(solution)/shard_map/ppermute | solution.py:413
  42.6 0.0 collective-permute-done.5.down_ref
  42.6 0.2 late_blocks.1
  42.8 0.1 collective-permute-start.6
  42.9 3.4 %collective-permute-start.7 = (f32[384,256]{1,0:T(8,128)S(1)}, f32[384,256]{1,0:T(8,128)S(1)}, u32[]{:S(2)}, u32[]{:S(2)}) collective-permute-start(f32[384,256]{1,0:T(8,128)S(1)} %get-tuple-element.26), channel_id=1, source_target_pairs={{0,3},{1,0},{2,1},{3,2},{4,7},{5,4},{6,5},{7,6},{8,11},{9,8},{10,9... | collective-permute-start | bytes 1179656 | tf_op jit(solution)/shard_map/ppermute | solution.py:413
  46.3 0.0 collective-permute-start.8
  46.3 4.5 %collective-permute-done.8.refs_1_ = f32[8,128]{1,0:T(8,128)S(1)} collective-permute-done((f32[8,128]{1,0:T(8,128)S(1)}, f32[8,128]{1,0:T(8,128)S(1)}, u32[]{:S(2)}, u32[]{:S(2)}) %collective-permute-start.8) | collective-permute-done | bytes 4128 | tf_op jit(solution)/shard_map/ppermute | solution.py:413
  50.9 0.6 collective-permute-start.9
  51.5 0.2 own_blocks.1.own_ref
  51.7 4.3 %collective-permute-done.9.other_ref = f32[8,128]{1,0:T(8,128)S(1)} collective-permute-done((f32[8,128]{1,0:T(8,128)S(1)}, f32[8,128]{1,0:T(8,128)S(1)}, u32[]{:S(2)}, u32[]{:S(2)}) %collective-permute-start.9) | collective-permute-done | bytes 4128 | tf_op jit(solution)/shard_map/ppermute | solution.py:413
  56.0 0.0 collective-permute-done.6.late_up
  56.0 0.0 collective-permute-done.7.late_down
  56.0 5.0 %collective-permute-start.10 = (f32[96,256]{1,0:T(8,128)S(1)}, f32[96,256]{1,0:T(8,128)S(1)}, u32[]{:S(2)}, u32[]{:S(2)}) collective-permute-start(f32[96,256]{1,0:T(8,128)S(1)} %get-tuple-element.28.high_ref), channel_id=1, source_target_pairs={{0,4},{4,8},{8,12},{12,16},{16,20},{20,24},{24,28},{28,32},{32,36}... | collective-permute-start | bytes 294920 | tf_op jit(solution)/shard_map/ppermute | solution.py:406
  61.1 1.9 %collective-permute-start.11 = (f32[96,256]{1,0:T(8,128)S(1)}, f32[96,256]{1,0:T(8,128)S(1)}, u32[]{:S(2)}, u32[]{:S(2)}) collective-permute-start(f32[96,256]{1,0:T(8,128)S(1)} %get-tuple-element.29.low_ref), channel_id=1, source_target_pairs={{4,0},{8,4},{12,8},{16,12},{20,16},{24,20},{28,24},{32,28},{36,32}... | collective-permute-start | bytes 294920 | tf_op jit(solution)/shard_map/ppermute | solution.py:406
  63.0 0.3 collective-permute-done.10.before_ref
  63.3 6.4 %collective-permute-done.11.after_ref = f32[96,256]{1,0:T(8,128)S(1)} collective-permute-done((f32[96,256]{1,0:T(8,128)S(1)}, f32[96,256]{1,0:T(8,128)S(1)}, u32[]{:S(2)}, u32[]{:S(2)}) %collective-permute-start.11) | collective-permute-done | bytes 98336 | tf_op jit(solution)/shard_map/ppermute | solution.py:406
  69.7 3.4 %finish.1 = f32[768,256]{1,0:T(8,128)} custom-call(f32[3,5]{1,0:T(4,128)} %taps_hbm.3, f32[96,256]{1,0:T(8,128)S(1)} %collective-permute-done.10.before_ref, f32[96,256]{1,0:T(8,128)S(1)} %collective-permute-done.11.after_ref, f32[96,256]{1,0:T(8,128)S(1)} %get-tuple-element.29.low_ref, f32[96,256]{1,0:T(8,128)S(1)} %get-tuple-element.28.high_ref, ...), custom_call_target="tpu_custom_call" | custom-call | flops 5898240 | bytes 4194304 | tf_op jit(solution)/shard_map/finish/pallas_call | solution.py:386
  (3 shorter events, 0.0 us)
Async XLA Ops:
  6.6 14.4 %collective-permute-start = (f32[16,48,256]{2,1,0:T(8,128)S(1)}, f32[16,48,256]{2,1,0:T(8,128)S(1)}, u32[]{:S(2)}, u32[]{:S(2)}) collective-permute-start(f32[16,48,256]{2,1,0:T(8,128)S(1)} %get-tuple-element.19), channel_id=1, source_target_pairs={{64,0},{128,64},{192,128},{65,1},{129,65},{193,129},{66,2},{130,66... | collective-permute-start | bytes 2359304 | tf_op jit(solution)/shard_map/ppermute | solution.py:406
  7.9 13.1 %collective-permute-start.1 = (f32[16,48,256]{2,1,0:T(8,128)S(1)}, f32[16,48,256]{2,1,0:T(8,128)S(1)}, u32[]{:S(2)}, u32[]{:S(2)}) collective-permute-start(f32[16,48,256]{2,1,0:T(8,128)S(1)} %get-tuple-element.20), channel_id=1, source_target_pairs={{0,64},{64,128},{128,192},{1,65},{65,129},{129,193},{2,66},{66,130... | collective-permute-start | bytes 2359304 | tf_op jit(solution)/shard_map/ppermute | solution.py:406
  11.0 4.9 %collective-permute-start.2 = (f32[8,128]{1,0:T(8,128)S(1)}, f32[8,128]{1,0:T(8,128)S(1)}, u32[]{:S(2)}, u32[]{:S(2)}) collective-permute-start(f32[8,128]{1,0:T(8,128)S(1)} %get-tuple-element.21.refs_0_), channel_id=1, source_target_pairs={{0,1},{1,2},{2,3},{3,0},{4,5},{5,6},{6,7},{7,4},{8,9},{9,10},{10,1... | collective-permute-start | bytes 12296 | tf_op jit(solution)/shard_map/ppermute | solution.py:413
  15.9 5.1 %collective-permute-start.3 = (f32[8,128]{1,0:T(8,128)S(1)}, f32[8,128]{1,0:T(8,128)S(1)}, u32[]{:S(2)}, u32[]{:S(2)}) collective-permute-start(f32[8,128]{1,0:T(8,128)S(1)} %add_sums.2.moments_ref), channel_id=1, source_target_pairs={{0,2},{1,3},{2,0},{3,1},{4,6},{5,7},{6,4},{7,5},{8,10},{9,11},{10,... | collective-permute-start | bytes 12296 | tf_op jit(solution)/shard_map/ppermute | solution.py:413
  21.3 21.3 %collective-permute-start.4 = (f32[768,256]{1,0:T(8,128)S(1)}, f32[768,256]{1,0:T(8,128)S(1)}, u32[]{:S(2)}, u32[]{:S(2)}) collective-permute-start(f32[768,256]{1,0:T(8,128)S(1)} %get-tuple-element.22), channel_id=1, source_target_pairs={{0,1},{1,2},{2,3},{3,0},{4,5},{5,6},{6,7},{7,4},{8,9},{9,10},{10,1... | collective-permute-start | bytes 2359304 | tf_op jit(solution)/shard_map/ppermute | solution.py:413
  21.8 20.8 %collective-permute-start.5 = (f32[768,256]{1,0:T(8,128)S(1)}, f32[768,256]{1,0:T(8,128)S(1)}, u32[]{:S(2)}, u32[]{:S(2)}) collective-permute-start(f32[768,256]{1,0:T(8,128)S(1)} %get-tuple-element.23), channel_id=1, source_target_pairs={{0,3},{1,0},{2,1},{3,2},{4,7},{5,4},{6,5},{7,6},{8,11},{9,8},{10,9... | collective-permute-start | bytes 2359304 | tf_op jit(solution)/shard_map/ppermute | solution.py:413
  42.8 13.2 %collective-permute-start.6 = (f32[384,256]{1,0:T(8,128)S(1)}, f32[384,256]{1,0:T(8,128)S(1)}, u32[]{:S(2)}, u32[]{:S(2)}) collective-permute-start(f32[384,256]{1,0:T(8,128)S(1)} %get-tuple-element.25), channel_id=1, source_target_pairs={{0,1},{1,2},{2,3},{3,0},{4,5},{5,6},{6,7},{7,4},{8,9},{9,10},{10,1... | collective-permute-start | bytes 1179656 | tf_op jit(solution)/shard_map/ppermute | solution.py:413
  42.9 13.1 %collective-permute-start.7 = (f32[384,256]{1,0:T(8,128)S(1)}, f32[384,256]{1,0:T(8,128)S(1)}, u32[]{:S(2)}, u32[]{:S(2)}) collective-permute-start(f32[384,256]{1,0:T(8,128)S(1)} %get-tuple-element.26), channel_id=1, source_target_pairs={{0,3},{1,0},{2,1},{3,2},{4,7},{5,4},{6,5},{7,6},{8,11},{9,8},{10,9... | collective-permute-start | bytes 1179656 | tf_op jit(solution)/shard_map/ppermute | solution.py:413
  46.3 4.5 %collective-permute-start.8 = (f32[8,128]{1,0:T(8,128)S(1)}, f32[8,128]{1,0:T(8,128)S(1)}, u32[]{:S(2)}, u32[]{:S(2)}) collective-permute-start(f32[8,128]{1,0:T(8,128)S(1)} %get-tuple-element.27.refs_0_), channel_id=1, source_target_pairs={{0,64},{64,128},{128,192},{192,0},{1,65},{65,129},{129,193},{193,1... | collective-permute-start | bytes 12296 | tf_op jit(solution)/shard_map/ppermute | solution.py:413
  50.9 5.1 %collective-permute-start.9 = (f32[8,128]{1,0:T(8,128)S(1)}, f32[8,128]{1,0:T(8,128)S(1)}, u32[]{:S(2)}, u32[]{:S(2)}) collective-permute-start(f32[8,128]{1,0:T(8,128)S(1)} %add_sums.3.moments_ref), channel_id=1, source_target_pairs={{0,128},{64,192},{128,0},{192,64},{1,129},{65,193},{129,1},{193,65... | collective-permute-start | bytes 12296 | tf_op jit(solution)/shard_map/ppermute | solution.py:413
  56.0 7.2 %collective-permute-start.10 = (f32[96,256]{1,0:T(8,128)S(1)}, f32[96,256]{1,0:T(8,128)S(1)}, u32[]{:S(2)}, u32[]{:S(2)}) collective-permute-start(f32[96,256]{1,0:T(8,128)S(1)} %get-tuple-element.28.high_ref), channel_id=1, source_target_pairs={{0,4},{4,8},{8,12},{12,16},{16,20},{20,24},{24,28},{28,32},{32,36}... | collective-permute-start | bytes 294920 | tf_op jit(solution)/shard_map/ppermute | solution.py:406
  61.1 8.6 %collective-permute-start.11 = (f32[96,256]{1,0:T(8,128)S(1)}, f32[96,256]{1,0:T(8,128)S(1)}, u32[]{:S(2)}, u32[]{:S(2)}) collective-permute-start(f32[96,256]{1,0:T(8,128)S(1)} %get-tuple-element.29.low_ref), channel_id=1, source_target_pairs={{4,0},{8,4},{12,8},{16,12},{20,16},{24,20},{28,24},{32,28},{36,32}... | collective-permute-start | bytes 294920 | tf_op jit(solution)/shard_map/ppermute | solution.py:406

commit v3 on v2

--- a/solution.py
+++ b/solution.py
@@ -252,19 +252,11 @@
     refs[-1][...] = total
 
 
-def peers_kernel(gathered_ref, out_ref):
-    total = gathered_ref[0:8]
-    for peer in range(1, gathered_ref.shape[0] // 8):
-        total = total + gathered_ref[8 * peer : 8 * peer + 8]
-    out_ref[...] = total
-
-
 def first_kernel(split, half, main_ref, above_ref, below_ref, moments_ref, other_ref, up_ref, down_ref,
                  spread_ref):
     block = main_ref.shape[2]
     total = moments_ref[...] + other_ref[...]
-    for peer in range(spread_ref.shape[0] // 8):
-        spread_ref[8 * peer : 8 * peer + 8] = total
+    spread_ref[...] = jnp.broadcast_to(total[0:1], spread_ref.shape)
     for out, pieces in ((up_ref, ((2, 0), (1, half))), (down_ref, ((2, half), (3, 0)))):
         for place, (ahead, base) in enumerate(pieces):
             flags = owner_flags(ahead, split)
@@ -275,15 +267,21 @@
 
 
 def late_kernel(split, half, main_ref, above_ref, below_ref, up_ref, down_ref, gathered_ref,
-                late_up, late_down, summed_ref):
-    peers_kernel(gathered_ref, summed_ref)
+                early_up, early_down, late_up, late_down, summed_ref):
+    total = jnp.sum(gathered_ref[...], axis=0, keepdims=True)
+    summed_ref[...] = jnp.broadcast_to(total, summed_ref.shape)
     block = main_ref.shape[2]
-    for ahead, base, leaf, out in ((1, 0, up_ref, late_up), (3, half, down_ref, late_down)):
+    for ahead, base, leaf, early, late, rim in (
+        (1, 0, up_ref, early_up, late_up, 0), (3, half, down_ref, early_down, late_down, half - REACH)
+    ):
         flags = owner_flags(ahead, split)
         for slot in range(half):
-            rows = rows_at(slot, block)
             value = with_edges(main_ref, above_ref, below_ref, flags, ahead, base + slot)
-            out[rows, :] = value + leaf[rows, :]
+            value = value + leaf[rows_at(slot, block), :]
+            if rim <= slot < rim + REACH:
+                early[rows_at(slot - rim, block), :] = value
+            else:
+                late[rows_at(slot if rim else slot - REACH, block), :] = value
 
 
 def own_kernel(split, half, main_ref, above_ref, below_ref, up_ref, down_ref, out_ref):
@@ -297,12 +295,10 @@
         )
 
 
-def rim_kernel(half, block, own_ref, late_up, late_down, moments_ref, other_ref,
-               low_ref, high_ref, summed_ref):
-    summed_ref[...] = moments_ref[...] + other_ref[...]
-    low, high = pl.ds(0, REACH * block), pl.ds((half - REACH) * block, REACH * block)
-    low_ref[...] = own_ref[low, :] + late_up[low, :]
-    high_ref[...] = own_ref[pl.ds((2 * half - REACH) * block, REACH * block), :] + late_down[high, :]
+def rim_kernel(half, block, own_ref, early_up, early_down, low_ref, high_ref):
+    rim = REACH * block
+    low_ref[...] = own_ref[pl.ds(0, rim), :] + early_up[...]
+    high_ref[...] = own_ref[pl.ds(2 * half * block - rim, rim), :] + early_down[...]
 
 
 def local_call(kernel, shapes, args, name, weight=1):
@@ -337,8 +333,8 @@
         planes[j] = low_ref[rows, :]
         planes[local_y - REACH + j] = high_ref[rows, :]
     for row in range(REACH, local_y - REACH):
-        late = late_up if row < half else late_down
-        planes[row] = own_ref[rows_at(row, block), :] + late[rows_at(row % half, block), :]
+        late, slot = (late_up, row - REACH) if row < half else (late_down, row - half)
+        planes[row] = own_ref[rows_at(row, block), :] + late[rows_at(slot, block), :]
     totals = moments[0][0:1]
     for other in moments[1:]:
         totals = totals + other[0:1]
@@ -413,6 +409,10 @@
     return lax.ppermute(values, axis, [(i, (i + by) % count) for i in range(count)])
 
 
+def swap(values, axis, bit):
+    return lax.ppermute(values, axis, [(i, i ^ bit) for i in range(lax.axis_size(axis))])
+
+
 def squared_norms(size_x, size_y, size_z):
     def of(extent):
         return sum(((2.0 * i + 1.0) / extent - 1.0) ** 2 for i in range(extent))
@@ -442,38 +442,40 @@
     )
     from_above = shift(up, "gx", -1)
     from_below = shift(down, "gx", 1)
-    (moments,) = local_call(add_kernel, [tile], (moments, turn(moments, "mz", 1)), "add_sums")
+    for axis, by in (("gx", 1), ("mz", 1)):
+        (moments,) = local_call(add_kernel, [tile], (moments, swap(moments, axis, by)), "add_sums")
     blocks = (main, from_above, from_below)
     both = (2 * half * block, depth)
     whole = (half * block, depth)
     up, down, spread = local_call(
-        functools.partial(first_kernel, split, half), [both, both, (8 * along, LANES)],
-        blocks + (moments, turn(moments, "mz", 2)), "first_blocks",
+        functools.partial(first_kernel, split, half), [both, both, (along, LANES)],
+        blocks + (moments, swap(moments, "mz", 2)), "first_blocks",
     )
     up = turn(up, "mz", 1)
     down = turn(down, "mz", -1)
     gathered = lax.all_to_all(spread, "gy", 0, 0, tiled=True)
-    late_up, late_down, moments = local_call(
-        functools.partial(late_kernel, split, half), [whole, whole, tile],
+    rim = (REACH * block, depth)
+    inner = ((half - REACH) * block, depth)
+    early_up, early_down, late_up, late_down, moments = local_call(
+        functools.partial(late_kernel, split, half), [rim, rim, inner, inner, tile],
         blocks + (up, down, gathered), "late_blocks",
     )
+    early_up = turn(early_up, "mz", 1)
+    early_down = turn(early_down, "mz", -1)
     late_up = turn(late_up, "mz", 1)
     late_down = turn(late_down, "mz", -1)
     (own,) = local_call(
         functools.partial(own_kernel, split, half), [(local_y * block, depth)],
         blocks + (up, down), "own_blocks",
     )
-    (moments,) = local_call(add_kernel, [tile], (moments, turn(moments, "gx", 1)), "add_sums")
-    rim = (REACH * block, depth)
-    low, high, moments = local_call(
-        functools.partial(rim_kernel, half, block), [rim, rim, tile],
-        (own, late_up, late_down, moments, turn(moments, "gx", 2)), "rim_blocks",
+    low, high = local_call(
+        functools.partial(rim_kernel, half, block), [rim, rim], (own, early_up, early_down), "rim_blocks"
     )
     before = shift(high, "gy", 1)
     after = shift(low, "gy", -1)
     result = finish(
         kernel_taps,
-        (before, after, low, high, own, late_up, late_down, moments),
+        (before, after, low, high, own, late_up, late_down, moments, swap(moments, "gx", 2)),
         (local_y, depth, elements, split, local_x, size_x, size_y),
         squared_norms(size_x, size_y, depth),
     )

time: 73.3 us -> 71.9 us (0.981)
  waiting for transfers between devices: 25.9 us -> 19.2 us
  starting transfers between devices: 22.4 us -> 28.7 us
  blocking collectives: 13.9 us -> 12.8 us
    ppermute x8 -> x6, waiting for transfers between devices: 19.2 us -> 7.85 us  [turn(): lax.ppermute(values, axis, [(i, (i + by) % count) for i in range(count)])]
    ppermute x0 -> x4, waiting for transfers between devices: none -> 9.87 us  [swap(): lax.ppermute(values, axis, [(i, i ^ bit) for i in range(lax.axis_size(axi...]
    ppermute x0 -> x4, starting transfers between devices: none -> 7.47 us  [swap(): lax.ppermute(values, axis, [(i, i ^ bit) for i in range(lax.axis_size(axi...]
    ppermute x4, waiting for transfers between devices: 6.7 us -> 1.5 us  [shift(): lax.ppermute(values, axis, [(i, i + by) for i in range(count) if 0 <= i +...]
    ppermute x8 -> x6, starting transfers between devices: 11.1 us -> 9.86 us  [turn(): lax.ppermute(values, axis, [(i, (i + by) % count) for i in range(count)])]
    all_to_all x1, blocking collectives: 13.9 us -> 12.8 us  [shards(): gathered = lax.all_to_all(spread, 'gy', 0, 0, tiled=True)]
  transfers between devices with their start and end apart: 12 -> 14, of which waited for: 7 -> 7; matrix products, arithmetic and copies ran while one was open for 0% -> 0% of each run, Pallas kernels for 0% -> 0%
where the time goes in v3:
time: 71.9 us; the launch traced here: 71.7 us
  starting transfers between devices  28.7 us (40%)
  waiting for transfers between devices  19.2 us (27%)
  blocking collectives  12.8 us (18%)
  Pallas kernels  10.8 us (15%)
    all_to_all x1, blocking collectives, shards(): gathered = lax.all_to_all(spread, 'gy', 0, 0, tiled=True)  12.8 us
    ppermute x4, starting transfers between devices, shift(): lax.ppermute(values, axis, [(i, i + by) for i in range(count) if 0 <= i +...  11.4 us
    ppermute x4, waiting for transfers between devices, swap(): lax.ppermute(values, axis, [(i, i ^ bit) for i in range(lax.axis_size(axi...  9.87 us
    ppermute x6, starting transfers between devices, turn(): lax.ppermute(values, axis, [(i, (i + by) % count) for i in range(count)])  9.86 us
    ppermute x6, waiting for transfers between devices, turn(): lax.ppermute(values, axis, [(i, (i + by) % count) for i in range(count)])  7.85 us
    ppermute x4, starting transfers between devices, swap(): lax.ppermute(values, axis, [(i, i ^ bit) for i in range(lax.axis_size(axi...  7.47 us
    pallas_call x1, Pallas kernels, mix(): pl.pallas_call(functools.partial(mix_kernel, sizes), out_shape=[jax.Shape...  6.59 us
    pallas_call x1, Pallas kernels, finish(): pl.pallas_call(functools.partial(finish_kernel, sizes, squares), out_shap...  3.43 us
  transfers between devices with their start and end apart: 14, of which 7 were waited for; matrix products, arithmetic and copies ran while one was open for 0% of the time, Pallas kernels for 0%

profile of v3, /device:TPU:98, one launch (start us, length us, event | category | flops | bytes accessed | tf_op | source)
XLA Modules:
  0.0 71.7 jit_solution(2184968305049639389)
XLA Ops:
  0.0 6.6 %mix_bins.1 = (f32[4,16,48,256]{3,2,1,0:T(8,128)S(1)}, f32[16,48,256]{2,1,0:T(8,128)S(1)}, f32[16,48,256]{2,1,0:T(8,128)S(1)}, f32[8,128]{1,0:T(8,128)S(1)}) custom-call(f32[3,5]{1,0:T(4,128)} %taps_hbm.3, s32[4,24]{1,0:T(4,128)} %bitcast.11, f32[4,24]{1,0:T(4,128)} %bitcast.12, s32[4096,256]{1,0:T(8,128)} %bitcast.10), custom_call_target="tpu_custom_call" | custom-call | flops 1207959552 | bytes 8388608 | tf_op jit(solution)/shard_map/mix_bins/pallas_call | solution.py:205
  6.6 1.3 %collective-permute-start = (f32[16,48,256]{2,1,0:T(8,128)S(1)}, f32[16,48,256]{2,1,0:T(8,128)S(1)}, u32[]{:S(2)}, u32[]{:S(2)}) collective-permute-start(f32[16,48,256]{2,1,0:T(8,128)S(1)} %get-tuple-element.20), channel_id=1, source_target_pairs={{64,0},{128,64},{192,128},{65,1},{129,65},{193,129},{66,2},{130,66... | collective-permute-start | bytes 2359304 | tf_op jit(solution)/shard_map/ppermute | solution.py:402
  7.9 3.1 %collective-permute-start.1 = (f32[16,48,256]{2,1,0:T(8,128)S(1)}, f32[16,48,256]{2,1,0:T(8,128)S(1)}, u32[]{:S(2)}, u32[]{:S(2)}) collective-permute-start(f32[16,48,256]{2,1,0:T(8,128)S(1)} %get-tuple-element.21), channel_id=1, source_target_pairs={{0,64},{64,128},{128,192},{1,65},{65,129},{129,193},{2,66},{66,130... | collective-permute-start | bytes 2359304 | tf_op jit(solution)/shard_map/ppermute | solution.py:402
  11.0 2.6 %collective-permute-start.2 = (f32[8,128]{1,0:T(8,128)S(1)}, f32[8,128]{1,0:T(8,128)S(1)}, u32[]{:S(2)}, u32[]{:S(2)}) collective-permute-start(f32[8,128]{1,0:T(8,128)S(1)} %get-tuple-element.22.refs_0_), channel_id=1, source_target_pairs={{0,64},{64,0},{128,192},{192,128},{1,65},{65,1},{129,193},{193,129... | collective-permute-start | bytes 12296 | tf_op jit(solution)/shard_map/ppermute | solution.py:413
  13.6 0.8 %collective-permute-done.2.refs_1_ = f32[8,128]{1,0:T(8,128)S(1)} collective-permute-done((f32[8,128]{1,0:T(8,128)S(1)}, f32[8,128]{1,0:T(8,128)S(1)}, u32[]{:S(2)}, u32[]{:S(2)}) %collective-permute-start.2) | collective-permute-done | bytes 4128 | tf_op jit(solution)/shard_map/ppermute | solution.py:413
  14.4 1.6 %collective-permute-start.3 = (f32[8,128]{1,0:T(8,128)S(1)}, f32[8,128]{1,0:T(8,128)S(1)}, u32[]{:S(2)}, u32[]{:S(2)}) collective-permute-start(f32[8,128]{1,0:T(8,128)S(1)} %add_sums.2.refs_0_), channel_id=1, source_target_pairs={{0,1},{1,0},{2,3},{3,2},{4,5},{5,4},{6,7},{7,6},{8,9},{9,8},{10,11... | collective-permute-start | bytes 12296 | tf_op jit(solution)/shard_map/ppermute | solution.py:413
  16.0 2.0 %collective-permute-done.3.refs_1_ = f32[8,128]{1,0:T(8,128)S(1)} collective-permute-done((f32[8,128]{1,0:T(8,128)S(1)}, f32[8,128]{1,0:T(8,128)S(1)}, u32[]{:S(2)}, u32[]{:S(2)}) %collective-permute-start.3) | collective-permute-done | bytes 4128 | tf_op jit(solution)/shard_map/ppermute | solution.py:413
  18.0 3.2 %collective-permute-start.4 = (f32[8,128]{1,0:T(8,128)S(1)}, f32[8,128]{1,0:T(8,128)S(1)}, u32[]{:S(2)}, u32[]{:S(2)}) collective-permute-start(f32[8,128]{1,0:T(8,128)S(1)} %add_sums.3.moments_ref), channel_id=1, source_target_pairs={{0,2},{1,3},{2,0},{3,1},{4,6},{5,7},{6,4},{7,5},{8,10},{9,11},{10,... | collective-permute-start | bytes 12296 | tf_op jit(solution)/shard_map/ppermute | solution.py:413
  21.2 1.9 %collective-permute-done.4.other_ref = f32[8,128]{1,0:T(8,128)S(1)} collective-permute-done((f32[8,128]{1,0:T(8,128)S(1)}, f32[8,128]{1,0:T(8,128)S(1)}, u32[]{:S(2)}, u32[]{:S(2)}) %collective-permute-start.4) | collective-permute-done | bytes 4128 | tf_op jit(solution)/shard_map/ppermute | solution.py:413
  23.2 0.0 collective-permute-done.above_ref
  23.2 0.0 collective-permute-done.1.below_ref
  23.2 0.3 first_blocks.1
  23.5 1.7 %collective-permute-start.5 = (f32[768,256]{1,0:T(8,128)S(1)}, f32[768,256]{1,0:T(8,128)S(1)}, u32[]{:S(2)}, u32[]{:S(2)}) collective-permute-start(f32[768,256]{1,0:T(8,128)S(1)} %get-tuple-element.23), channel_id=1, source_target_pairs={{0,1},{1,2},{2,3},{3,0},{4,5},{5,6},{6,7},{7,4},{8,9},{9,10},{10,1... | collective-permute-start | bytes 2359304 | tf_op jit(solution)/shard_map/ppermute | solution.py:409
  25.1 1.7 %collective-permute-start.6 = (f32[768,256]{1,0:T(8,128)S(1)}, f32[768,256]{1,0:T(8,128)S(1)}, u32[]{:S(2)}, u32[]{:S(2)}) collective-permute-start(f32[768,256]{1,0:T(8,128)S(1)} %get-tuple-element.24), channel_id=1, source_target_pairs={{0,3},{1,0},{2,1},{3,2},{4,7},{5,4},{6,5},{7,6},{8,11},{9,8},{10,9... | collective-permute-start | bytes 2359304 | tf_op jit(solution)/shard_map/ppermute | solution.py:409
  26.8 12.8 %all_to_all.11 = f32[16,1,128]{2,1,0:T(1,128)S(1)} all-to-all(f32[16,1,128]{2,1,0:T(1,128)S(1)} %bitcast.9), channel_id=1, replica_groups=mesh['gx'=4,'gy'=16,'mz'=4] {'gy'}, dimensions={0} | all-to-all | bytes 16384 | tf_op jit(solution)/shard_map/all_to_all | solution.py:456
  39.7 3.9 %collective-permute-done.5.up_ref = f32[768,256]{1,0:T(8,128)S(1)} collective-permute-done((f32[768,256]{1,0:T(8,128)S(1)}, f32[768,256]{1,0:T(8,128)S(1)}, u32[]{:S(2)}, u32[]{:S(2)}) %collective-permute-start.5) | collective-permute-done | bytes 786464 | tf_op jit(solution)/shard_map/ppermute | solution.py:409
  43.6 0.0 collective-permute-done.6.down_ref
  43.6 0.2 late_blocks.1
  43.8 1.6 %collective-permute-start.11 = (f32[288,256]{1,0:T(8,128)S(1)}, f32[288,256]{1,0:T(8,128)S(1)}, u32[]{:S(2)}, u32[]{:S(2)}) collective-permute-start(f32[288,256]{1,0:T(8,128)S(1)} %get-tuple-element.30), channel_id=1, source_target_pairs={{0,1},{1,2},{2,3},{3,0},{4,5},{5,6},{6,7},{7,4},{8,9},{9,10},{10,1... | collective-permute-start | bytes 884744 | tf_op jit(solution)/shard_map/ppermute | solution.py:409
  45.5 1.7 %collective-permute-start.12 = (f32[288,256]{1,0:T(8,128)S(1)}, f32[288,256]{1,0:T(8,128)S(1)}, u32[]{:S(2)}, u32[]{:S(2)}) collective-permute-start(f32[288,256]{1,0:T(8,128)S(1)} %get-tuple-element.31), channel_id=1, source_target_pairs={{0,3},{1,0},{2,1},{3,2},{4,7},{5,4},{6,5},{7,6},{8,11},{9,8},{10,9... | collective-permute-start | bytes 884744 | tf_op jit(solution)/shard_map/ppermute | solution.py:409
  47.1 0.4 collective-permute-start.7
  47.5 2.9 %collective-permute-start.8 = (f32[96,256]{1,0:T(8,128)S(1)}, f32[96,256]{1,0:T(8,128)S(1)}, u32[]{:S(2)}, u32[]{:S(2)}) collective-permute-start(f32[96,256]{1,0:T(8,128)S(1)} %get-tuple-element.27), channel_id=1, source_target_pairs={{0,3},{1,0},{2,1},{3,2},{4,7},{5,4},{6,5},{7,6},{8,11},{9,8},{10,9... | collective-permute-start | bytes 294920 | tf_op jit(solution)/shard_map/ppermute | solution.py:409
  50.4 0.2 own_blocks.1.own_ref
  50.6 3.9 %collective-permute-done.7.early_up = f32[96,256]{1,0:T(8,128)S(1)} collective-permute-done((f32[96,256]{1,0:T(8,128)S(1)}, f32[96,256]{1,0:T(8,128)S(1)}, u32[]{:S(2)}, u32[]{:S(2)}) %collective-permute-start.7) | collective-permute-done | bytes 98336 | tf_op jit(solution)/shard_map/ppermute | solution.py:409
  54.5 0.0 collective-permute-done.8.early_down
  54.5 5.1 %collective-permute-start.9 = (f32[96,256]{1,0:T(8,128)S(1)}, f32[96,256]{1,0:T(8,128)S(1)}, u32[]{:S(2)}, u32[]{:S(2)}) collective-permute-start(f32[96,256]{1,0:T(8,128)S(1)} %get-tuple-element.28.high_ref), channel_id=1, source_target_pairs={{0,4},{4,8},{8,12},{12,16},{16,20},{20,24},{24,28},{28,32},{32,36}... | collective-permute-start | bytes 294920 | tf_op jit(solution)/shard_map/ppermute | solution.py:402
  59.6 1.9 %collective-permute-start.10 = (f32[96,256]{1,0:T(8,128)S(1)}, f32[96,256]{1,0:T(8,128)S(1)}, u32[]{:S(2)}, u32[]{:S(2)}) collective-permute-start(f32[96,256]{1,0:T(8,128)S(1)} %get-tuple-element.29.low_ref), channel_id=1, source_target_pairs={{4,0},{8,4},{12,8},{16,12},{20,16},{24,20},{28,24},{32,28},{36,32}... | collective-permute-start | bytes 294920 | tf_op jit(solution)/shard_map/ppermute | solution.py:402
  61.5 0.1 collective-permute-start.13
  61.6 5.1 %collective-permute-done.13.rest_1_ = f32[8,128]{1,0:T(8,128)S(1)} collective-permute-done((f32[8,128]{1,0:T(8,128)S(1)}, f32[8,128]{1,0:T(8,128)S(1)}, u32[]{:S(2)}, u32[]{:S(2)}) %collective-permute-start.13) | collective-permute-done | bytes 4128 | tf_op jit(solution)/shard_map/ppermute | solution.py:413
  66.7 0.0 collective-permute-done.9.before_ref
  66.7 1.5 %collective-permute-done.10.after_ref = f32[96,256]{1,0:T(8,128)S(1)} collective-permute-done((f32[96,256]{1,0:T(8,128)S(1)}, f32[96,256]{1,0:T(8,128)S(1)}, u32[]{:S(2)}, u32[]{:S(2)}) %collective-permute-start.10) | collective-permute-done | bytes 98336 | tf_op jit(solution)/shard_map/ppermute | solution.py:402
  68.2 3.4 %finish.1 = f32[768,256]{1,0:T(8,128)} custom-call(f32[3,5]{1,0:T(4,128)} %taps_hbm.3, f32[96,256]{1,0:T(8,128)S(1)} %collective-permute-done.9.before_ref, f32[96,256]{1,0:T(8,128)S(1)} %collective-permute-done.10.after_ref, f32[96,256]{1,0:T(8,128)S(1)} %get-tuple-element.29.low_ref, f32[96,256]{1,0:T(8,128)S(1)} %get-tuple-element.28.high_ref, ...), custom_call_target="tpu_custom_call" | custom-call | flops 5898240 | bytes 4194304 | tf_op jit(solution)/shard_map/finish/pallas_call | solution.py:382
  (5 shorter events, 0.0 us)
Async XLA Ops:
  6.6 16.6 %collective-permute-start = (f32[16,48,256]{2,1,0:T(8,128)S(1)}, f32[16,48,256]{2,1,0:T(8,128)S(1)}, u32[]{:S(2)}, u32[]{:S(2)}) collective-permute-start(f32[16,48,256]{2,1,0:T(8,128)S(1)} %get-tuple-element.20), channel_id=1, source_target_pairs={{64,0},{128,64},{192,128},{65,1},{129,65},{193,129},{66,2},{130,66... | collective-permute-start | bytes 2359304 | tf_op jit(solution)/shard_map/ppermute | solution.py:402
  7.9 15.3 %collective-permute-start.1 = (f32[16,48,256]{2,1,0:T(8,128)S(1)}, f32[16,48,256]{2,1,0:T(8,128)S(1)}, u32[]{:S(2)}, u32[]{:S(2)}) collective-permute-start(f32[16,48,256]{2,1,0:T(8,128)S(1)} %get-tuple-element.21), channel_id=1, source_target_pairs={{0,64},{64,128},{128,192},{1,65},{65,129},{129,193},{2,66},{66,130... | collective-permute-start | bytes 2359304 | tf_op jit(solution)/shard_map/ppermute | solution.py:402
  11.0 3.4 %collective-permute-start.2 = (f32[8,128]{1,0:T(8,128)S(1)}, f32[8,128]{1,0:T(8,128)S(1)}, u32[]{:S(2)}, u32[]{:S(2)}) collective-permute-start(f32[8,128]{1,0:T(8,128)S(1)} %get-tuple-element.22.refs_0_), channel_id=1, source_target_pairs={{0,64},{64,0},{128,192},{192,128},{1,65},{65,1},{129,193},{193,129... | collective-permute-start | bytes 12296 | tf_op jit(solution)/shard_map/ppermute | solution.py:413
  14.4 3.6 %collective-permute-start.3 = (f32[8,128]{1,0:T(8,128)S(1)}, f32[8,128]{1,0:T(8,128)S(1)}, u32[]{:S(2)}, u32[]{:S(2)}) collective-permute-start(f32[8,128]{1,0:T(8,128)S(1)} %add_sums.2.refs_0_), channel_id=1, source_target_pairs={{0,1},{1,0},{2,3},{3,2},{4,5},{5,4},{6,7},{7,6},{8,9},{9,8},{10,11... | collective-permute-start | bytes 12296 | tf_op jit(solution)/shard_map/ppermute | solution.py:413
  18.0 5.1 %collective-permute-start.4 = (f32[8,128]{1,0:T(8,128)S(1)}, f32[8,128]{1,0:T(8,128)S(1)}, u32[]{:S(2)}, u32[]{:S(2)}) collective-permute-start(f32[8,128]{1,0:T(8,128)S(1)} %add_sums.3.moments_ref), channel_id=1, source_target_pairs={{0,2},{1,3},{2,0},{3,1},{4,6},{5,7},{6,4},{7,5},{8,10},{9,11},{10,... | collective-permute-start | bytes 12296 | tf_op jit(solution)/shard_map/ppermute | solution.py:413
  23.5 20.1 %collective-permute-start.5 = (f32[768,256]{1,0:T(8,128)S(1)}, f32[768,256]{1,0:T(8,128)S(1)}, u32[]{:S(2)}, u32[]{:S(2)}) collective-permute-start(f32[768,256]{1,0:T(8,128)S(1)} %get-tuple-element.23), channel_id=1, source_target_pairs={{0,1},{1,2},{2,3},{3,0},{4,5},{5,6},{6,7},{7,4},{8,9},{9,10},{10,1... | collective-permute-start | bytes 2359304 | tf_op jit(solution)/shard_map/ppermute | solution.py:409
  25.1 18.4 %collective-permute-start.6 = (f32[768,256]{1,0:T(8,128)S(1)}, f32[768,256]{1,0:T(8,128)S(1)}, u32[]{:S(2)}, u32[]{:S(2)}) collective-permute-start(f32[768,256]{1,0:T(8,128)S(1)} %get-tuple-element.24), channel_id=1, source_target_pairs={{0,3},{1,0},{2,1},{3,2},{4,7},{5,4},{6,5},{7,6},{8,11},{9,8},{10,9... | collective-permute-start | bytes 2359304 | tf_op jit(solution)/shard_map/ppermute | solution.py:409
  43.8 24.4 %collective-permute-start.11 = (f32[288,256]{1,0:T(8,128)S(1)}, f32[288,256]{1,0:T(8,128)S(1)}, u32[]{:S(2)}, u32[]{:S(2)}) collective-permute-start(f32[288,256]{1,0:T(8,128)S(1)} %get-tuple-element.30), channel_id=1, source_target_pairs={{0,1},{1,2},{2,3},{3,0},{4,5},{5,6},{6,7},{7,4},{8,9},{9,10},{10,1... | collective-permute-start | bytes 884744 | tf_op jit(solution)/shard_map/ppermute | solution.py:409
  45.5 22.8 %collective-permute-start.12 = (f32[288,256]{1,0:T(8,128)S(1)}, f32[288,256]{1,0:T(8,128)S(1)}, u32[]{:S(2)}, u32[]{:S(2)}) collective-permute-start(f32[288,256]{1,0:T(8,128)S(1)} %get-tuple-element.31), channel_id=1, source_target_pairs={{0,3},{1,0},{2,1},{3,2},{4,7},{5,4},{6,5},{7,6},{8,11},{9,8},{10,9... | collective-permute-start | bytes 884744 | tf_op jit(solution)/shard_map/ppermute | solution.py:409
  47.1 7.4 %collective-permute-start.7 = (f32[96,256]{1,0:T(8,128)S(1)}, f32[96,256]{1,0:T(8,128)S(1)}, u32[]{:S(2)}, u32[]{:S(2)}) collective-permute-start(f32[96,256]{1,0:T(8,128)S(1)} %get-tuple-element.26), channel_id=1, source_target_pairs={{0,1},{1,2},{2,3},{3,0},{4,5},{5,6},{6,7},{7,4},{8,9},{9,10},{10,1... | collective-permute-start | bytes 294920 | tf_op jit(solution)/shard_map/ppermute | solution.py:409
  47.5 7.0 %collective-permute-start.8 = (f32[96,256]{1,0:T(8,128)S(1)}, f32[96,256]{1,0:T(8,128)S(1)}, u32[]{:S(2)}, u32[]{:S(2)}) collective-permute-start(f32[96,256]{1,0:T(8,128)S(1)} %get-tuple-element.27), channel_id=1, source_target_pairs={{0,3},{1,0},{2,1},{3,2},{4,7},{5,4},{6,5},{7,6},{8,11},{9,8},{10,9... | collective-permute-start | bytes 294920 | tf_op jit(solution)/shard_map/ppermute | solution.py:409
  54.5 12.2 %collective-permute-start.9 = (f32[96,256]{1,0:T(8,128)S(1)}, f32[96,256]{1,0:T(8,128)S(1)}, u32[]{:S(2)}, u32[]{:S(2)}) collective-permute-start(f32[96,256]{1,0:T(8,128)S(1)} %get-tuple-element.28.high_ref), channel_id=1, source_target_pairs={{0,4},{4,8},{8,12},{12,16},{16,20},{20,24},{24,28},{28,32},{32,36}... | collective-permute-start | bytes 294920 | tf_op jit(solution)/shard_map/ppermute | solution.py:402
  59.6 8.6 %collective-permute-start.10 = (f32[96,256]{1,0:T(8,128)S(1)}, f32[96,256]{1,0:T(8,128)S(1)}, u32[]{:S(2)}, u32[]{:S(2)}) collective-permute-start(f32[96,256]{1,0:T(8,128)S(1)} %get-tuple-element.29.low_ref), channel_id=1, source_target_pairs={{4,0},{8,4},{12,8},{16,12},{20,16},{24,20},{28,24},{32,28},{36,32}... | collective-permute-start | bytes 294920 | tf_op jit(solution)/shard_map/ppermute | solution.py:402
  61.5 5.2 %collective-permute-start.13 = (f32[8,128]{1,0:T(8,128)S(1)}, f32[8,128]{1,0:T(8,128)S(1)}, u32[]{:S(2)}, u32[]{:S(2)}) collective-permute-start(f32[8,128]{1,0:T(8,128)S(1)} %get-tuple-element.32.rest_0_), channel_id=1, source_target_pairs={{0,128},{64,192},{128,0},{192,64},{1,129},{65,193},{129,1},{193,65... | collective-permute-start | bytes 12296 | tf_op jit(solution)/shard_map/ppermute | solution.py:413

commit v4 on v3

--- a/solution.py
+++ b/solution.py
@@ -135,7 +135,7 @@
 
 
 def mix_kernel(sizes, taps_hbm, bins_hbm, share_hbm, counts_ref, main_ref, up_ref, down_ref, moments_ref,
-               taps_ref, bins_ref, share_ref, held, table, sums, small_sem, sem):
+               weights_ref, taps_ref, bins_ref, share_ref, held, table, sums, small_sem, sem):
     local_bins, local_x, local_y, depth, elements, split, all_bins, size_x, size_y = sizes
     rows_in = local_bins * local_x
     small = [
@@ -155,6 +155,7 @@
     for copy in small:
         copy.wait()
     weights = normalized(taps_ref)
+    weights_ref[...] = weights
     unmix = unmix_rows(bins_ref, share_ref, all_bins)
     shape = (all_bins, rows_in)
     expand = jnp.where(
@@ -201,7 +202,7 @@
     rows_out = (split + 2) * block
     vmem = pl.BlockSpec(memory_space=pltpu.VMEM)
     hbm = pl.BlockSpec(memory_space=pltpu.HBM)
-    shapes = [(split, local_y, block, depth)] + [(local_y, block, depth)] * 2 + [(8, LANES)]
+    shapes = [(split, local_y, block, depth)] + [(local_y, block, depth)] * 2 + [(8, LANES), taps.shape]
     return pl.pallas_call(
         functools.partial(mix_kernel, sizes),
         out_shape=[jax.ShapeDtypeStruct(shape, jnp.float32) for shape in shapes],
@@ -315,16 +316,13 @@
     )(*args)
 
 
-def finish_kernel(sizes, squares, taps_hbm, before_ref, after_ref, low_ref, high_ref,
+def finish_kernel(sizes, squares, weights_ref, before_ref, after_ref, low_ref, high_ref,
                   own_ref, late_up, late_down, *rest):
-    moments, (out_ref, taps_ref, turned, sem) = rest[:-4], rest[-4:]
+    moments, (out_ref, turned, sem) = rest[:-3], rest[-3:]
     local_y, depth, elements, split, local_x, size_x, size_y = sizes
-    copy = pltpu.make_async_copy(taps_hbm, taps_ref, sem)
-    copy.start()
     half = local_y // 2
     block = REACH * elements
-    copy.wait()
-    weights = normalized(taps_ref)
+    weights = weights_ref[...]
     planes = {}
     for j in range(REACH):
         rows = rows_at(j, block)
@@ -357,6 +355,7 @@
     for offset in range(TAPS):
         source = line + (offset - REACH)
         edge.append(jnp.where((source >= 0) & (source < depth), tap(weights, 2, offset), 0.0))
+    copies = []
     for row in range(local_y):
         smooth = tap(weights, 1, 0) * planes[row - REACH]
         for offset in range(1, TAPS):
@@ -370,31 +369,41 @@
                 turned[lane, pl.ds(j * local_y + row, elements, stride=REACH * local_y), :] = result[
                     j * elements : (j + 1) * elements, lane * LANES : (lane + 1) * LANES
                 ]
-    for lane in lane_parts(depth):
-        out_ref[:, lane * LANES : (lane + 1) * LANES] = turned[lane]
-
-
-def finish(taps, args, sizes, squares):
+        if row % 8 == 7:
+            rows = pl.ds(row - 7, 8)
+            for lane in lane_parts(depth):
+                source = turned.at[lane].reshape(elements * REACH, local_y, LANES)
+                copy = pltpu.make_async_copy(
+                    source.at[:, rows, :],
+                    out_ref.at[:, rows, pl.ds(lane * LANES, LANES)],
+                    sem.at[row // 8, lane],
+                )
+                copy.start()
+                copies.append(copy)
+    for copy in copies:
+        copy.wait()
+
+
+def finish(weights, args, sizes, squares):
     local_y, depth, elements = sizes[:3]
     vmem = pl.BlockSpec(memory_space=pltpu.VMEM)
     hbm = pl.BlockSpec(memory_space=pltpu.HBM)
     rows = elements * REACH * local_y
     return pl.pallas_call(
         functools.partial(finish_kernel, sizes, squares),
-        out_shape=jax.ShapeDtypeStruct((rows, depth), jnp.float32),
-        in_specs=[hbm] + [vmem] * len(args),
-        out_specs=vmem,
+        out_shape=jax.ShapeDtypeStruct((elements * REACH, local_y, depth), jnp.float32),
+        in_specs=[vmem] * (1 + len(args)),
+        out_specs=hbm,
         scratch_shapes=[
-            pltpu.VMEM(taps.shape, jnp.float32),
             pltpu.VMEM((depth // LANES, rows, LANES), jnp.float32),
-            pltpu.SemaphoreType.DMA,
+            pltpu.SemaphoreType.DMA((local_y // 8, depth // LANES)),
         ],
         compiler_params=pltpu.CompilerParams(vmem_limit_bytes=8 * MIB),
         cost_estimate=pl.CostEstimate(
             flops=30 * rows * depth, bytes_accessed=4 << 20, transcendentals=0
         ),
         name="finish",
-    )(pltpu.with_memory_space_constraint(taps, pltpu.HBM), *args)
+    )(weights, *args)
 
 
 def shift(values, axis, by):
@@ -437,7 +446,7 @@
     block = REACH * elements
     sizes = (local_bins, local_x, local_y, depth, elements, split, local_bins * split, size_x, size_y)
     tile = (8, LANES)
-    main, up, down, moments = mix(
+    main, up, down, moments, weights = mix(
         kernel_taps, peak_bins.T, peak_share.T, counts, sizes, across * split
     )
     from_above = shift(up, "gx", -1)
@@ -474,7 +483,7 @@
     before = shift(high, "gy", 1)
     after = shift(low, "gy", -1)
     result = finish(
-        kernel_taps,
+        weights,
         (before, after, low, high, own, late_up, late_down, moments, swap(moments, "gx", 2)),
         (local_y, depth, elements, split, local_x, size_x, size_y),
         squared_norms(size_x, size_y, depth),

time: 71.9 us -> 70.9 us (0.986)
  Pallas kernels: 10.8 us -> 9.84 us
    pallas_call x1, Pallas kernels: 3.43 us -> 2.44 us  [finish(): pl.pallas_call(functools.partial(finish_kernel, sizes, squares), out_shap...]
where the time goes in v4:
time: 70.9 us; the launch traced here: 70.7 us
  starting transfers between devices  28.7 us (40%)
  waiting for transfers between devices  19.2 us (27%)
  blocking collectives  12.8 us (18%)
  Pallas kernels  9.84 us (14%)
    all_to_all x1, blocking collectives, shards(): gathered = lax.all_to_all(spread, 'gy', 0, 0, tiled=True)  12.8 us
    ppermute x4, starting transfers between devices, shift(): lax.ppermute(values, axis, [(i, i + by) for i in range(count) if 0 <= i +...  11.4 us
    ppermute x4, waiting for transfers between devices, swap(): lax.ppermute(values, axis, [(i, i ^ bit) for i in range(lax.axis_size(axi...  9.87 us
    ppermute x6, starting transfers between devices, turn(): lax.ppermute(values, axis, [(i, (i + by) % count) for i in range(count)])  9.86 us
    ppermute x6, waiting for transfers between devices, turn(): lax.ppermute(values, axis, [(i, (i + by) % count) for i in range(count)])  7.85 us
    ppermute x4, starting transfers between devices, swap(): lax.ppermute(values, axis, [(i, i ^ bit) for i in range(lax.axis_size(axi...  7.47 us
    pallas_call x1, Pallas kernels, mix(): pl.pallas_call(functools.partial(mix_kernel, sizes), out_shape=[jax.Shape...  6.59 us
    pallas_call x1, Pallas kernels, finish(): pl.pallas_call(functools.partial(finish_kernel, sizes, squares), out_shap...  2.44 us
  transfers between devices with their start and end apart: 14, of which 7 were waited for; matrix products, arithmetic and copies ran while one was open for 0% of the time, Pallas kernels for 0%

profile of v4, /device:TPU:98, one launch (start us, length us, event | category | flops | bytes accessed | tf_op | source)
XLA Modules:
  0.0 70.7 jit_solution(14850808304052515637)
XLA Ops:
  0.0 6.6 %mix_bins.1 = (f32[4,16,48,256]{3,2,1,0:T(8,128)S(1)}, f32[16,48,256]{2,1,0:T(8,128)S(1)}, f32[16,48,256]{2,1,0:T(8,128)S(1)}, f32[8,128]{1,0:T(8,128)S(1)}, f32[3,5]{1,0:T(4,128)S(1)}) custom-call(f32[3,5]{1,0:T(4,128)} %taps_hbm.1, s32[4,24]{1,0:T(4,128)} %bitcast.11, f32[4,24]{1,0:T(4,128)} %bitcast.12, s32[4096,256]{1,0:T(8,128)} %bitcast.10), custom_call_target="tpu_custom_call" | custom-call | flops 1207959552 | bytes 8388608 | tf_op jit(solution)/shard_map/mix_bins/pallas_call | solution.py:206
  6.6 1.3 %collective-permute-start = (f32[16,48,256]{2,1,0:T(8,128)S(1)}, f32[16,48,256]{2,1,0:T(8,128)S(1)}, u32[]{:S(2)}, u32[]{:S(2)}) collective-permute-start(f32[16,48,256]{2,1,0:T(8,128)S(1)} %get-tuple-element.22), channel_id=1, source_target_pairs={{64,0},{128,64},{192,128},{65,1},{129,65},{193,129},{66,2},{130,66... | collective-permute-start | bytes 2359304 | tf_op jit(solution)/shard_map/ppermute | solution.py:411
  7.9 3.1 %collective-permute-start.1 = (f32[16,48,256]{2,1,0:T(8,128)S(1)}, f32[16,48,256]{2,1,0:T(8,128)S(1)}, u32[]{:S(2)}, u32[]{:S(2)}) collective-permute-start(f32[16,48,256]{2,1,0:T(8,128)S(1)} %get-tuple-element.23), channel_id=1, source_target_pairs={{0,64},{64,128},{128,192},{1,65},{65,129},{129,193},{2,66},{66,130... | collective-permute-start | bytes 2359304 | tf_op jit(solution)/shard_map/ppermute | solution.py:411
  11.0 2.6 %collective-permute-start.2 = (f32[8,128]{1,0:T(8,128)S(1)}, f32[8,128]{1,0:T(8,128)S(1)}, u32[]{:S(2)}, u32[]{:S(2)}) collective-permute-start(f32[8,128]{1,0:T(8,128)S(1)} %get-tuple-element.24.refs_0_), channel_id=1, source_target_pairs={{0,64},{64,0},{128,192},{192,128},{1,65},{65,1},{129,193},{193,129... | collective-permute-start | bytes 12296 | tf_op jit(solution)/shard_map/ppermute | solution.py:422
  13.6 0.8 %collective-permute-done.2.refs_1_ = f32[8,128]{1,0:T(8,128)S(1)} collective-permute-done((f32[8,128]{1,0:T(8,128)S(1)}, f32[8,128]{1,0:T(8,128)S(1)}, u32[]{:S(2)}, u32[]{:S(2)}) %collective-permute-start.2) | collective-permute-done | bytes 4128 | tf_op jit(solution)/shard_map/ppermute | solution.py:422
  14.4 1.6 %collective-permute-start.3 = (f32[8,128]{1,0:T(8,128)S(1)}, f32[8,128]{1,0:T(8,128)S(1)}, u32[]{:S(2)}, u32[]{:S(2)}) collective-permute-start(f32[8,128]{1,0:T(8,128)S(1)} %add_sums.2.refs_0_), channel_id=1, source_target_pairs={{0,1},{1,0},{2,3},{3,2},{4,5},{5,4},{6,7},{7,6},{8,9},{9,8},{10,11... | collective-permute-start | bytes 12296 | tf_op jit(solution)/shard_map/ppermute | solution.py:422
  16.0 2.0 %collective-permute-done.3.refs_1_ = f32[8,128]{1,0:T(8,128)S(1)} collective-permute-done((f32[8,128]{1,0:T(8,128)S(1)}, f32[8,128]{1,0:T(8,128)S(1)}, u32[]{:S(2)}, u32[]{:S(2)}) %collective-permute-start.3) | collective-permute-done | bytes 4128 | tf_op jit(solution)/shard_map/ppermute | solution.py:422
  18.0 3.2 %collective-permute-start.4 = (f32[8,128]{1,0:T(8,128)S(1)}, f32[8,128]{1,0:T(8,128)S(1)}, u32[]{:S(2)}, u32[]{:S(2)}) collective-permute-start(f32[8,128]{1,0:T(8,128)S(1)} %add_sums.3.moments_ref), channel_id=1, source_target_pairs={{0,2},{1,3},{2,0},{3,1},{4,6},{5,7},{6,4},{7,5},{8,10},{9,11},{10,... | collective-permute-start | bytes 12296 | tf_op jit(solution)/shard_map/ppermute | solution.py:422
  21.2 1.9 %collective-permute-done.4.other_ref = f32[8,128]{1,0:T(8,128)S(1)} collective-permute-done((f32[8,128]{1,0:T(8,128)S(1)}, f32[8,128]{1,0:T(8,128)S(1)}, u32[]{:S(2)}, u32[]{:S(2)}) %collective-permute-start.4) | collective-permute-done | bytes 4128 | tf_op jit(solution)/shard_map/ppermute | solution.py:422
  23.2 0.0 collective-permute-done.above_ref
  23.2 0.3 first_blocks.1
  23.5 1.7 %collective-permute-start.5 = (f32[768,256]{1,0:T(8,128)S(1)}, f32[768,256]{1,0:T(8,128)S(1)}, u32[]{:S(2)}, u32[]{:S(2)}) collective-permute-start(f32[768,256]{1,0:T(8,128)S(1)} %get-tuple-element.25), channel_id=1, source_target_pairs={{0,1},{1,2},{2,3},{3,0},{4,5},{5,6},{6,7},{7,4},{8,9},{9,10},{10,1... | collective-permute-start | bytes 2359304 | tf_op jit(solution)/shard_map/ppermute | solution.py:418
  25.1 1.7 %collective-permute-start.6 = (f32[768,256]{1,0:T(8,128)S(1)}, f32[768,256]{1,0:T(8,128)S(1)}, u32[]{:S(2)}, u32[]{:S(2)}) collective-permute-start(f32[768,256]{1,0:T(8,128)S(1)} %get-tuple-element.26), channel_id=1, source_target_pairs={{0,3},{1,0},{2,1},{3,2},{4,7},{5,4},{6,5},{7,6},{8,11},{9,8},{10,9... | collective-permute-start | bytes 2359304 | tf_op jit(solution)/shard_map/ppermute | solution.py:418
  26.8 12.8 %all_to_all.11 = f32[16,1,128]{2,1,0:T(1,128)S(1)} all-to-all(f32[16,1,128]{2,1,0:T(1,128)S(1)} %bitcast.9), channel_id=1, replica_groups=mesh['gx'=4,'gy'=16,'mz'=4] {'gy'}, dimensions={0} | all-to-all | bytes 16384 | tf_op jit(solution)/shard_map/all_to_all | solution.py:465
  39.7 3.9 %collective-permute-done.5.up_ref = f32[768,256]{1,0:T(8,128)S(1)} collective-permute-done((f32[768,256]{1,0:T(8,128)S(1)}, f32[768,256]{1,0:T(8,128)S(1)}, u32[]{:S(2)}, u32[]{:S(2)}) %collective-permute-start.5) | collective-permute-done | bytes 786464 | tf_op jit(solution)/shard_map/ppermute | solution.py:418
  43.6 0.0 collective-permute-done.6.down_ref
  43.6 0.2 late_blocks.1
  43.8 1.6 %collective-permute-start.11 = (f32[288,256]{1,0:T(8,128)S(1)}, f32[288,256]{1,0:T(8,128)S(1)}, u32[]{:S(2)}, u32[]{:S(2)}) collective-permute-start(f32[288,256]{1,0:T(8,128)S(1)} %get-tuple-element.32), channel_id=1, source_target_pairs={{0,1},{1,2},{2,3},{3,0},{4,5},{5,6},{6,7},{7,4},{8,9},{9,10},{10,1... | collective-permute-start | bytes 884744 | tf_op jit(solution)/shard_map/ppermute | solution.py:418
  45.5 1.7 %collective-permute-start.12 = (f32[288,256]{1,0:T(8,128)S(1)}, f32[288,256]{1,0:T(8,128)S(1)}, u32[]{:S(2)}, u32[]{:S(2)}) collective-permute-start(f32[288,256]{1,0:T(8,128)S(1)} %get-tuple-element.33), channel_id=1, source_target_pairs={{0,3},{1,0},{2,1},{3,2},{4,7},{5,4},{6,5},{7,6},{8,11},{9,8},{10,9... | collective-permute-start | bytes 884744 | tf_op jit(solution)/shard_map/ppermute | solution.py:418
  47.1 0.4 collective-permute-start.7
  47.5 2.9 %collective-permute-start.8 = (f32[96,256]{1,0:T(8,128)S(1)}, f32[96,256]{1,0:T(8,128)S(1)}, u32[]{:S(2)}, u32[]{:S(2)}) collective-permute-start(f32[96,256]{1,0:T(8,128)S(1)} %get-tuple-element.29), channel_id=1, source_target_pairs={{0,3},{1,0},{2,1},{3,2},{4,7},{5,4},{6,5},{7,6},{8,11},{9,8},{10,9... | collective-permute-start | bytes 294920 | tf_op jit(solution)/shard_map/ppermute | solution.py:418
  50.4 0.2 own_blocks.1.own_ref
  50.6 3.9 %collective-permute-done.7.early_up = f32[96,256]{1,0:T(8,128)S(1)} collective-permute-done((f32[96,256]{1,0:T(8,128)S(1)}, f32[96,256]{1,0:T(8,128)S(1)}, u32[]{:S(2)}, u32[]{:S(2)}) %collective-permute-start.7) | collective-permute-done | bytes 98336 | tf_op jit(solution)/shard_map/ppermute | solution.py:418
  54.5 5.1 %collective-permute-start.9 = (f32[96,256]{1,0:T(8,128)S(1)}, f32[96,256]{1,0:T(8,128)S(1)}, u32[]{:S(2)}, u32[]{:S(2)}) collective-permute-start(f32[96,256]{1,0:T(8,128)S(1)} %get-tuple-element.30.high_ref), channel_id=1, source_target_pairs={{0,4},{4,8},{8,12},{12,16},{16,20},{20,24},{24,28},{28,32},{32,36}... | collective-permute-start | bytes 294920 | tf_op jit(solution)/shard_map/ppermute | solution.py:411
  59.6 1.9 %collective-permute-start.10 = (f32[96,256]{1,0:T(8,128)S(1)}, f32[96,256]{1,0:T(8,128)S(1)}, u32[]{:S(2)}, u32[]{:S(2)}) collective-permute-start(f32[96,256]{1,0:T(8,128)S(1)} %get-tuple-element.31.low_ref), channel_id=1, source_target_pairs={{4,0},{8,4},{12,8},{16,12},{20,16},{24,20},{28,24},{32,28},{36,32}... | collective-permute-start | bytes 294920 | tf_op jit(solution)/shard_map/ppermute | solution.py:411
  61.5 0.1 collective-permute-start.13
  61.6 5.1 %collective-permute-done.13.rest_1_ = f32[8,128]{1,0:T(8,128)S(1)} collective-permute-done((f32[8,128]{1,0:T(8,128)S(1)}, f32[8,128]{1,0:T(8,128)S(1)}, u32[]{:S(2)}, u32[]{:S(2)}) %collective-permute-start.13) | collective-permute-done | bytes 4128 | tf_op jit(solution)/shard_map/ppermute | solution.py:422
  66.7 0.0 collective-permute-done.9.before_ref
  66.7 1.5 %collective-permute-done.10.after_ref = f32[96,256]{1,0:T(8,128)S(1)} collective-permute-done((f32[96,256]{1,0:T(8,128)S(1)}, f32[96,256]{1,0:T(8,128)S(1)}, u32[]{:S(2)}, u32[]{:S(2)}) %collective-permute-start.10) | collective-permute-done | bytes 98336 | tf_op jit(solution)/shard_map/ppermute | solution.py:411
  68.2 0.0 collective-permute-done.11.late_up
  68.2 0.0 collective-permute-done.12.late_down
  68.2 2.4 %finish.1 = f32[48,16,256]{2,1,0:T(8,128)} custom-call(f32[3,5]{1,0:T(4,128)S(1)} %get-tuple-element.20.weights_ref, f32[96,256]{1,0:T(8,128)S(1)} %collective-permute-done.9.before_ref, f32[96,256]{1,0:T(8,128)S(1)} %collective-permute-done.10.after_ref, f32[96,256]{1,0:T(8,128)S(1)} %get-tuple-element.31.low_ref, ...), custom_call_target="tpu_custom_call" | custom-call | flops 5898240 | bytes 4194304 | tf_op jit(solution)/shard_map/finish/pallas_call | solution.py:392
  (5 shorter events, 0.0 us)
Async XLA Ops:
  6.6 16.6 %collective-permute-start = (f32[16,48,256]{2,1,0:T(8,128)S(1)}, f32[16,48,256]{2,1,0:T(8,128)S(1)}, u32[]{:S(2)}, u32[]{:S(2)}) collective-permute-start(f32[16,48,256]{2,1,0:T(8,128)S(1)} %get-tuple-element.22), channel_id=1, source_target_pairs={{64,0},{128,64},{192,128},{65,1},{129,65},{193,129},{66,2},{130,66... | collective-permute-start | bytes 2359304 | tf_op jit(solution)/shard_map/ppermute | solution.py:411
  7.9 15.3 %collective-permute-start.1 = (f32[16,48,256]{2,1,0:T(8,128)S(1)}, f32[16,48,256]{2,1,0:T(8,128)S(1)}, u32[]{:S(2)}, u32[]{:S(2)}) collective-permute-start(f32[16,48,256]{2,1,0:T(8,128)S(1)} %get-tuple-element.23), channel_id=1, source_target_pairs={{0,64},{64,128},{128,192},{1,65},{65,129},{129,193},{2,66},{66,130... | collective-permute-start | bytes 2359304 | tf_op jit(solution)/shard_map/ppermute | solution.py:411
  11.0 3.4 %collective-permute-start.2 = (f32[8,128]{1,0:T(8,128)S(1)}, f32[8,128]{1,0:T(8,128)S(1)}, u32[]{:S(2)}, u32[]{:S(2)}) collective-permute-start(f32[8,128]{1,0:T(8,128)S(1)} %get-tuple-element.24.refs_0_), channel_id=1, source_target_pairs={{0,64},{64,0},{128,192},{192,128},{1,65},{65,1},{129,193},{193,129... | collective-permute-start | bytes 12296 | tf_op jit(solution)/shard_map/ppermute | solution.py:422
  14.4 3.6 %collective-permute-start.3 = (f32[8,128]{1,0:T(8,128)S(1)}, f32[8,128]{1,0:T(8,128)S(1)}, u32[]{:S(2)}, u32[]{:S(2)}) collective-permute-start(f32[8,128]{1,0:T(8,128)S(1)} %add_sums.2.refs_0_), channel_id=1, source_target_pairs={{0,1},{1,0},{2,3},{3,2},{4,5},{5,4},{6,7},{7,6},{8,9},{9,8},{10,11... | collective-permute-start | bytes 12296 | tf_op jit(solution)/shard_map/ppermute | solution.py:422
  18.0 5.1 %collective-permute-start.4 = (f32[8,128]{1,0:T(8,128)S(1)}, f32[8,128]{1,0:T(8,128)S(1)}, u32[]{:S(2)}, u32[]{:S(2)}) collective-permute-start(f32[8,128]{1,0:T(8,128)S(1)} %add_sums.3.moments_ref), channel_id=1, source_target_pairs={{0,2},{1,3},{2,0},{3,1},{4,6},{5,7},{6,4},{7,5},{8,10},{9,11},{10,... | collective-permute-start | bytes 12296 | tf_op jit(solution)/shard_map/ppermute | solution.py:422
  23.5 20.1 %collective-permute-start.5 = (f32[768,256]{1,0:T(8,128)S(1)}, f32[768,256]{1,0:T(8,128)S(1)}, u32[]{:S(2)}, u32[]{:S(2)}) collective-permute-start(f32[768,256]{1,0:T(8,128)S(1)} %get-tuple-element.25), channel_id=1, source_target_pairs={{0,1},{1,2},{2,3},{3,0},{4,5},{5,6},{6,7},{7,4},{8,9},{9,10},{10,1... | collective-permute-start | bytes 2359304 | tf_op jit(solution)/shard_map/ppermute | solution.py:418
  25.1 18.4 %collective-permute-start.6 = (f32[768,256]{1,0:T(8,128)S(1)}, f32[768,256]{1,0:T(8,128)S(1)}, u32[]{:S(2)}, u32[]{:S(2)}) collective-permute-start(f32[768,256]{1,0:T(8,128)S(1)} %get-tuple-element.26), channel_id=1, source_target_pairs={{0,3},{1,0},{2,1},{3,2},{4,7},{5,4},{6,5},{7,6},{8,11},{9,8},{10,9... | collective-permute-start | bytes 2359304 | tf_op jit(solution)/shard_map/ppermute | solution.py:418
  43.8 24.4 %collective-permute-start.11 = (f32[288,256]{1,0:T(8,128)S(1)}, f32[288,256]{1,0:T(8,128)S(1)}, u32[]{:S(2)}, u32[]{:S(2)}) collective-permute-start(f32[288,256]{1,0:T(8,128)S(1)} %get-tuple-element.32), channel_id=1, source_target_pairs={{0,1},{1,2},{2,3},{3,0},{4,5},{5,6},{6,7},{7,4},{8,9},{9,10},{10,1... | collective-permute-start | bytes 884744 | tf_op jit(solution)/shard_map/ppermute | solution.py:418
  45.5 22.8 %collective-permute-start.12 = (f32[288,256]{1,0:T(8,128)S(1)}, f32[288,256]{1,0:T(8,128)S(1)}, u32[]{:S(2)}, u32[]{:S(2)}) collective-permute-start(f32[288,256]{1,0:T(8,128)S(1)} %get-tuple-element.33), channel_id=1, source_target_pairs={{0,3},{1,0},{2,1},{3,2},{4,7},{5,4},{6,5},{7,6},{8,11},{9,8},{10,9... | collective-permute-start | bytes 884744 | tf_op jit(solution)/shard_map/ppermute | solution.py:418
  47.1 7.4 %collective-permute-start.7 = (f32[96,256]{1,0:T(8,128)S(1)}, f32[96,256]{1,0:T(8,128)S(1)}, u32[]{:S(2)}, u32[]{:S(2)}) collective-permute-start(f32[96,256]{1,0:T(8,128)S(1)} %get-tuple-element.28), channel_id=1, source_target_pairs={{0,1},{1,2},{2,3},{3,0},{4,5},{5,6},{6,7},{7,4},{8,9},{9,10},{10,1... | collective-permute-start | bytes 294920 | tf_op jit(solution)/shard_map/ppermute | solution.py:418
  47.5 7.0 %collective-permute-start.8 = (f32[96,256]{1,0:T(8,128)S(1)}, f32[96,256]{1,0:T(8,128)S(1)}, u32[]{:S(2)}, u32[]{:S(2)}) collective-permute-start(f32[96,256]{1,0:T(8,128)S(1)} %get-tuple-element.29), channel_id=1, source_target_pairs={{0,3},{1,0},{2,1},{3,2},{4,7},{5,4},{6,5},{7,6},{8,11},{9,8},{10,9... | collective-permute-start | bytes 294920 | tf_op jit(solution)/shard_map/ppermute | solution.py:418
  54.5 12.2 %collective-permute-start.9 = (f32[96,256]{1,0:T(8,128)S(1)}, f32[96,256]{1,0:T(8,128)S(1)}, u32[]{:S(2)}, u32[]{:S(2)}) collective-permute-start(f32[96,256]{1,0:T(8,128)S(1)} %get-tuple-element.30.high_ref), channel_id=1, source_target_pairs={{0,4},{4,8},{8,12},{12,16},{16,20},{20,24},{24,28},{28,32},{32,36}... | collective-permute-start | bytes 294920 | tf_op jit(solution)/shard_map/ppermute | solution.py:411
  59.6 8.6 %collective-permute-start.10 = (f32[96,256]{1,0:T(8,128)S(1)}, f32[96,256]{1,0:T(8,128)S(1)}, u32[]{:S(2)}, u32[]{:S(2)}) collective-permute-start(f32[96,256]{1,0:T(8,128)S(1)} %get-tuple-element.31.low_ref), channel_id=1, source_target_pairs={{4,0},{8,4},{12,8},{16,12},{20,16},{24,20},{28,24},{32,28},{36,32}... | collective-permute-start | bytes 294920 | tf_op jit(solution)/shard_map/ppermute | solution.py:411
  61.5 5.2 %collective-permute-start.13 = (f32[8,128]{1,0:T(8,128)S(1)}, f32[8,128]{1,0:T(8,128)S(1)}, u32[]{:S(2)}, u32[]{:S(2)}) collective-permute-start(f32[8,128]{1,0:T(8,128)S(1)} %get-tuple-element.34.rest_0_), channel_id=1, source_target_pairs={{0,128},{64,192},{128,0},{192,64},{1,129},{65,193},{129,1},{193,65... | collective-permute-start | bytes 12296 | tf_op jit(solution)/shard_map/ppermute | solution.py:422

commit v5 on v4

--- a/solution.py
+++ b/solution.py
@@ -13,6 +13,7 @@
 LANES = 128
 HIGHEST = lax.Precision.HIGHEST
 MIB = 1024 * 1024
+MOVED = 3
 
 def iota(shape, dim):
     return lax.broadcasted_iota(jnp.int32, shape, dim)
@@ -253,53 +254,77 @@
     refs[-1][...] = total
 
 
-def first_kernel(split, half, main_ref, above_ref, below_ref, moments_ref, other_ref, up_ref, down_ref,
-                 spread_ref):
+def first_kernel(split, half, moved, main_ref, above_ref, below_ref, moments_ref, other_ref, up_ref, down_ref,
+                 across_ref, spread_ref):
     block = main_ref.shape[2]
     total = moments_ref[...] + other_ref[...]
     spread_ref[...] = jnp.broadcast_to(total[0:1], spread_ref.shape)
-    for out, pieces in ((up_ref, ((2, 0), (1, half))), (down_ref, ((2, half), (3, 0)))):
-        for place, (ahead, base) in enumerate(pieces):
-            flags = owner_flags(ahead, split)
-            for slot in range(half):
-                out[rows_at(place * half + slot, block), :] = with_edges(
-                    main_ref, above_ref, below_ref, flags, ahead, base + slot
-                )
-
-
-def late_kernel(split, half, main_ref, above_ref, below_ref, up_ref, down_ref, gathered_ref,
-                early_up, early_down, late_up, late_down, summed_ref):
+    inner = half - REACH
+    stay = half - moved
+    passed = owner_flags(2, split)
+    for out, leaf, ahead, start, rim in (
+        (up_ref, REACH, 1, half + moved, 0), (down_ref, half, 3, 0, half + inner)
+    ):
+        flags = owner_flags(ahead, split)
+        rows = [(2, leaf + slot) for slot in range(inner)]
+        rows += [(ahead, start + slot) for slot in range(stay)]
+        rows += [(ahead, rim + slot) for slot in range(REACH)]
+        for place, (part, row) in enumerate(rows):
+            chosen = passed if part == 2 else flags
+            out[rows_at(place, block), :] = with_edges(
+                main_ref, above_ref, below_ref, chosen, part, row
+            )
+    for slot in range(REACH):
+        for side, row in ((0, slot), (1, half + inner + slot)):
+            across_ref[rows_at(side * REACH + slot, block), :] = with_edges(
+                main_ref, above_ref, below_ref, passed, 2, row
+            )
+
+
+def late_kernel(split, half, moved, main_ref, above_ref, below_ref, up_ref, down_ref, across_ref,
+                gathered_ref, late_up, late_down, own_ref, low_ref, high_ref, summed_ref):
     total = jnp.sum(gathered_ref[...], axis=0, keepdims=True)
     summed_ref[...] = jnp.broadcast_to(total, summed_ref.shape)
     block = main_ref.shape[2]
-    for ahead, base, leaf, early, late, rim in (
-        (1, 0, up_ref, early_up, late_up, 0), (3, half, down_ref, early_down, late_down, half - REACH)
+    inner = half - REACH
+    for ahead, base, leaf, late, start in (
+        (1, REACH, up_ref, late_up, half), (3, half, down_ref, late_down, half - moved)
     ):
         flags = owner_flags(ahead, split)
-        for slot in range(half):
+        for slot in range(inner):
+            rows = rows_at(slot, block)
             value = with_edges(main_ref, above_ref, below_ref, flags, ahead, base + slot)
-            value = value + leaf[rows_at(slot, block), :]
-            if rim <= slot < rim + REACH:
-                early[rows_at(slot - rim, block), :] = value
-            else:
-                late[rows_at(slot if rim else slot - REACH, block), :] = value
-
-
-def own_kernel(split, half, main_ref, above_ref, below_ref, up_ref, down_ref, out_ref):
+            late[rows, :] = value + leaf[rows, :]
+        for slot in range(moved):
+            late[rows_at(inner + slot, block), :] = with_edges(
+                main_ref, above_ref, below_ref, flags, ahead, start + slot
+            )
+    own_part(split, half, moved, main_ref, above_ref, below_ref, up_ref, down_ref, across_ref,
+             own_ref, low_ref, high_ref)
+
+
+def own_part(split, half, moved, main_ref, above_ref, below_ref, up_ref, down_ref, across_ref,
+             out_ref, low_ref, high_ref):
     block = main_ref.shape[2]
     flags = owner_flags(0, split)
+    inner = half - REACH
+    stay = half - moved
     for row in range(2 * half):
-        direct = down_ref if row < half else up_ref
-        out_ref[rows_at(row, block), :] = (
-            with_edges(main_ref, above_ref, below_ref, flags, 0, row)
-            + direct[rows_at(half + row % half, block), :]
-        )
-
-
-def rim_kernel(half, block, own_ref, early_up, early_down, low_ref, high_ref):
-    rim = REACH * block
-    low_ref[...] = own_ref[pl.ds(0, rim), :] + early_up[...]
-    high_ref[...] = own_ref[pl.ds(2 * half * block - rim, rim), :] + early_down[...]
+        value = with_edges(main_ref, above_ref, below_ref, flags, 0, row)
+        if row < stay:
+            value = value + down_ref[rows_at(inner + row, block), :]
+        if row >= half + moved:
+            value = value + up_ref[rows_at(inner + row - half - moved, block), :]
+        if row < REACH:
+            value = value + up_ref[rows_at(inner + stay + row, block), :]
+            value = value + across_ref[rows_at(row, block), :]
+            low_ref[rows_at(row, block), :] = value
+        slot = row - half - inner
+        if slot >= 0:
+            value = value + down_ref[rows_at(inner + stay + slot, block), :]
+            value = value + across_ref[rows_at(REACH + slot, block), :]
+            high_ref[rows_at(slot, block), :] = value
+        out_ref[rows_at(row, block), :] = value
 
 
 def local_call(kernel, shapes, args, name, weight=1):
@@ -319,7 +344,7 @@
 def finish_kernel(sizes, squares, weights_ref, before_ref, after_ref, low_ref, high_ref,
                   own_ref, late_up, late_down, *rest):
     moments, (out_ref, turned, sem) = rest[:-3], rest[-3:]
-    local_y, depth, elements, split, local_x, size_x, size_y = sizes
+    local_y, depth, elements, split, local_x, size_x, size_y, moved = sizes
     half = local_y // 2
     block = REACH * elements
     weights = weights_ref[...]
@@ -333,6 +358,11 @@
     for row in range(REACH, local_y - REACH):
         late, slot = (late_up, row - REACH) if row < half else (late_down, row - half)
         planes[row] = own_ref[rows_at(row, block), :] + late[rows_at(slot, block), :]
+        if half - moved <= row < half:
+            extra = rows_at(half - REACH + row - (half - moved), block)
+            planes[row] = planes[row] + late_down[extra, :]
+        elif half <= row < half + moved:
+            planes[row] = planes[row] + late_up[rows_at(half - REACH + row - half, block), :]
     totals = moments[0][0:1]
     for other in moments[1:]:
         totals = totals + other[0:1]
@@ -454,38 +484,31 @@
     for axis, by in (("gx", 1), ("mz", 1)):
         (moments,) = local_call(add_kernel, [tile], (moments, swap(moments, axis, by)), "add_sums")
     blocks = (main, from_above, from_below)
-    both = (2 * half * block, depth)
-    whole = (half * block, depth)
-    up, down, spread = local_call(
-        functools.partial(first_kernel, split, half), [both, both, (along, LANES)],
+    first = ((2 * half - MOVED) * block, depth)
+    rim = (REACH * block, depth)
+    second = ((half - REACH + MOVED) * block, depth)
+    up, down, opposite, spread = local_call(
+        functools.partial(first_kernel, split, half, MOVED),
+        [first, first, (2 * REACH * block, depth), (along, LANES)],
         blocks + (moments, swap(moments, "mz", 2)), "first_blocks",
     )
     up = turn(up, "mz", 1)
     down = turn(down, "mz", -1)
+    opposite = turn(opposite, "mz", 2)
     gathered = lax.all_to_all(spread, "gy", 0, 0, tiled=True)
-    rim = (REACH * block, depth)
-    inner = ((half - REACH) * block, depth)
-    early_up, early_down, late_up, late_down, moments = local_call(
-        functools.partial(late_kernel, split, half), [rim, rim, inner, inner, tile],
-        blocks + (up, down, gathered), "late_blocks",
-    )
-    early_up = turn(early_up, "mz", 1)
-    early_down = turn(early_down, "mz", -1)
+    late_up, late_down, own, low, high, moments = local_call(
+        functools.partial(late_kernel, split, half, MOVED),
+        [second, second, (local_y * block, depth), rim, rim, tile],
+        blocks + (up, down, opposite, gathered), "late_blocks",
+    )
     late_up = turn(late_up, "mz", 1)
     late_down = turn(late_down, "mz", -1)
-    (own,) = local_call(
-        functools.partial(own_kernel, split, half), [(local_y * block, depth)],
-        blocks + (up, down), "own_blocks",
-    )
-    low, high = local_call(
-        functools.partial(rim_kernel, half, block), [rim, rim], (own, early_up, early_down), "rim_blocks"
-    )
     before = shift(high, "gy", 1)
     after = shift(low, "gy", -1)
     result = finish(
         weights,
         (before, after, low, high, own, late_up, late_down, moments, swap(moments, "gx", 2)),
-        (local_y, depth, elements, split, local_x, size_x, size_y),
+        (local_y, depth, elements, split, local_x, size_x, size_y, MOVED),
         squared_norms(size_x, size_y, depth),
     )
     return result.reshape(elements, local_x // split, local_y, depth)

time: 70.9 us -> 66 us (0.931)
  waiting for transfers between devices: 19.2 us -> 15.5 us
  starting transfers between devices: 28.7 us -> 27.5 us
    ppermute x6 -> x5, waiting for transfers between devices: 7.85 us -> 4.16 us  [turn(): lax.ppermute(values, axis, [(i, (i + by) % count) for i in range(count)])]
    ppermute x6 -> x5, starting transfers between devices: 9.86 us -> 8.6 us  [turn(): lax.ppermute(values, axis, [(i, (i + by) % count) for i in range(count)])]
  transfers between devices with their start and end apart: 14 -> 13, of which waited for: 7 -> 6; matrix products, arithmetic and copies ran while one was open for 0% -> 0% of each run, Pallas kernels for 0% -> 0%
where the time goes in v5:
time: 66 us; the launch traced here: 65.7 us
  starting transfers between devices  27.5 us (42%)
  waiting for transfers between devices  15.5 us (23%)
  blocking collectives  12.8 us (19%)
  Pallas kernels  9.84 us (15%)
    all_to_all x1, blocking collectives, shards(): gathered = lax.all_to_all(spread, 'gy', 0, 0, tiled=True)  12.8 us
    ppermute x4, starting transfers between devices, shift(): lax.ppermute(values, axis, [(i, i + by) for i in range(count) if 0 <= i +...  11.4 us
    ppermute x4, waiting for transfers between devices, swap(): lax.ppermute(values, axis, [(i, i ^ bit) for i in range(lax.axis_size(axi...  9.83 us
    ppermute x5, starting transfers between devices, turn(): lax.ppermute(values, axis, [(i, (i + by) % count) for i in range(count)])  8.6 us
    ppermute x4, starting transfers between devices, swap(): lax.ppermute(values, axis, [(i, i ^ bit) for i in range(lax.axis_size(axi...  7.52 us
    pallas_call x1, Pallas kernels, mix(): pl.pallas_call(functools.partial(mix_kernel, sizes), out_shape=[jax.Shape...  6.59 us
    ppermute x5, waiting for transfers between devices, turn(): lax.ppermute(values, axis, [(i, (i + by) % count) for i in range(count)])  4.16 us
    pallas_call x1, Pallas kernels, finish(): pl.pallas_call(functools.partial(finish_kernel, sizes, squares), out_shap...  2.49 us
  transfers between devices with their start and end apart: 13, of which 6 were waited for; matrix products, arithmetic and copies ran while one was open for 0% of the time, Pallas kernels for 0%

profile of v5, /device:TPU:98, one launch (start us, length us, event | category | flops | bytes accessed | tf_op | source)
XLA Modules:
  0.0 65.7 jit_solution(8703592644750585110)
XLA Ops:
  0.0 6.6 %mix_bins.1 = (f32[4,16,48,256]{3,2,1,0:T(8,128)S(1)}, f32[16,48,256]{2,1,0:T(8,128)S(1)}, f32[16,48,256]{2,1,0:T(8,128)S(1)}, f32[8,128]{1,0:T(8,128)S(1)}, f32[3,5]{1,0:T(4,128)S(1)}) custom-call(f32[3,5]{1,0:T(4,128)} %taps_hbm.1, s32[4,24]{1,0:T(4,128)} %bitcast.11, f32[4,24]{1,0:T(4,128)} %bitcast.12, s32[4096,256]{1,0:T(8,128)} %bitcast.10), custom_call_target="tpu_custom_call" | custom-call | flops 1207959552 | bytes 8388608 | tf_op jit(solution)/shard_map/mix_bins/pallas_call | solution.py:207
  6.6 1.3 %collective-permute-start = (f32[16,48,256]{2,1,0:T(8,128)S(1)}, f32[16,48,256]{2,1,0:T(8,128)S(1)}, u32[]{:S(2)}, u32[]{:S(2)}) collective-permute-start(f32[16,48,256]{2,1,0:T(8,128)S(1)} %get-tuple-element.22), channel_id=1, source_target_pairs={{64,0},{128,64},{192,128},{65,1},{129,65},{193,129},{66,2},{130,66... | collective-permute-start | bytes 2359304 | tf_op jit(solution)/shard_map/ppermute | solution.py:441
  7.9 3.1 %collective-permute-start.1 = (f32[16,48,256]{2,1,0:T(8,128)S(1)}, f32[16,48,256]{2,1,0:T(8,128)S(1)}, u32[]{:S(2)}, u32[]{:S(2)}) collective-permute-start(f32[16,48,256]{2,1,0:T(8,128)S(1)} %get-tuple-element.23), channel_id=1, source_target_pairs={{0,64},{64,128},{128,192},{1,65},{65,129},{129,193},{2,66},{66,130... | collective-permute-start | bytes 2359304 | tf_op jit(solution)/shard_map/ppermute | solution.py:441
  11.0 2.6 %collective-permute-start.2 = (f32[8,128]{1,0:T(8,128)S(1)}, f32[8,128]{1,0:T(8,128)S(1)}, u32[]{:S(2)}, u32[]{:S(2)}) collective-permute-start(f32[8,128]{1,0:T(8,128)S(1)} %get-tuple-element.24.refs_0_), channel_id=1, source_target_pairs={{0,64},{64,0},{128,192},{192,128},{1,65},{65,1},{129,193},{193,129... | collective-permute-start | bytes 12296 | tf_op jit(solution)/shard_map/ppermute | solution.py:452
  13.6 0.8 %collective-permute-done.2.refs_1_ = f32[8,128]{1,0:T(8,128)S(1)} collective-permute-done((f32[8,128]{1,0:T(8,128)S(1)}, f32[8,128]{1,0:T(8,128)S(1)}, u32[]{:S(2)}, u32[]{:S(2)}) %collective-permute-start.2) | collective-permute-done | bytes 4128 | tf_op jit(solution)/shard_map/ppermute | solution.py:452
  14.4 1.6 %collective-permute-start.3 = (f32[8,128]{1,0:T(8,128)S(1)}, f32[8,128]{1,0:T(8,128)S(1)}, u32[]{:S(2)}, u32[]{:S(2)}) collective-permute-start(f32[8,128]{1,0:T(8,128)S(1)} %add_sums.2.refs_0_), channel_id=1, source_target_pairs={{0,1},{1,0},{2,3},{3,2},{4,5},{5,4},{6,7},{7,6},{8,9},{9,8},{10,11... | collective-permute-start | bytes 12296 | tf_op jit(solution)/shard_map/ppermute | solution.py:452
  16.0 2.0 %collective-permute-done.3.refs_1_ = f32[8,128]{1,0:T(8,128)S(1)} collective-permute-done((f32[8,128]{1,0:T(8,128)S(1)}, f32[8,128]{1,0:T(8,128)S(1)}, u32[]{:S(2)}, u32[]{:S(2)}) %collective-permute-start.3) | collective-permute-done | bytes 4128 | tf_op jit(solution)/shard_map/ppermute | solution.py:452
  18.0 3.2 %collective-permute-start.4 = (f32[8,128]{1,0:T(8,128)S(1)}, f32[8,128]{1,0:T(8,128)S(1)}, u32[]{:S(2)}, u32[]{:S(2)}) collective-permute-start(f32[8,128]{1,0:T(8,128)S(1)} %add_sums.3.moments_ref), channel_id=1, source_target_pairs={{0,2},{1,3},{2,0},{3,1},{4,6},{5,7},{6,4},{7,5},{8,10},{9,11},{10,... | collective-permute-start | bytes 12296 | tf_op jit(solution)/shard_map/ppermute | solution.py:452
  21.2 1.9 %collective-permute-done.4.other_ref = f32[8,128]{1,0:T(8,128)S(1)} collective-permute-done((f32[8,128]{1,0:T(8,128)S(1)}, f32[8,128]{1,0:T(8,128)S(1)}, u32[]{:S(2)}, u32[]{:S(2)}) %collective-permute-start.4) | collective-permute-done | bytes 4128 | tf_op jit(solution)/shard_map/ppermute | solution.py:452
  23.2 0.0 collective-permute-done.above_ref
  23.2 0.0 collective-permute-done.1.below_ref
  23.2 0.3 first_blocks.1
  23.5 1.7 %collective-permute-start.5 = (f32[624,256]{1,0:T(8,128)S(1)}, f32[624,256]{1,0:T(8,128)S(1)}, u32[]{:S(2)}, u32[]{:S(2)}) collective-permute-start(f32[624,256]{1,0:T(8,128)S(1)} %get-tuple-element.25), channel_id=1, source_target_pairs={{0,1},{1,2},{2,3},{3,0},{4,5},{5,6},{6,7},{7,4},{8,9},{9,10},{10,1... | collective-permute-start | bytes 1916936 | tf_op jit(solution)/shard_map/ppermute | solution.py:448
  25.1 1.7 %collective-permute-start.6 = (f32[624,256]{1,0:T(8,128)S(1)}, f32[624,256]{1,0:T(8,128)S(1)}, u32[]{:S(2)}, u32[]{:S(2)}) collective-permute-start(f32[624,256]{1,0:T(8,128)S(1)} %get-tuple-element.26), channel_id=1, source_target_pairs={{0,3},{1,0},{2,1},{3,2},{4,7},{5,4},{6,5},{7,6},{8,11},{9,8},{10,9... | collective-permute-start | bytes 1916936 | tf_op jit(solution)/shard_map/ppermute | solution.py:448
  26.8 2.0 %collective-permute-start.7 = (f32[192,256]{1,0:T(8,128)S(1)}, f32[192,256]{1,0:T(8,128)S(1)}, u32[]{:S(2)}, u32[]{:S(2)}) collective-permute-start(f32[192,256]{1,0:T(8,128)S(1)} %get-tuple-element.27), channel_id=1, source_target_pairs={{0,2},{1,3},{2,0},{3,1},{4,6},{5,7},{6,4},{7,5},{8,10},{9,11},{10,... | collective-permute-start | bytes 589832 | tf_op jit(solution)/shard_map/ppermute | solution.py:448
  28.8 12.8 %all_to_all.11 = f32[16,1,128]{2,1,0:T(1,128)S(1)} all-to-all(f32[16,1,128]{2,1,0:T(1,128)S(1)} %bitcast.9), channel_id=1, replica_groups=mesh['gx'=4,'gy'=16,'mz'=4] {'gy'}, dimensions={0} | all-to-all | bytes 16384 | tf_op jit(solution)/shard_map/all_to_all | solution.py:498
  41.6 4.2 %collective-permute-done.7.across_ref = f32[192,256]{1,0:T(8,128)S(1)} collective-permute-done((f32[192,256]{1,0:T(8,128)S(1)}, f32[192,256]{1,0:T(8,128)S(1)}, u32[]{:S(2)}, u32[]{:S(2)}) %collective-permute-start.7) | collective-permute-done | bytes 196640 | tf_op jit(solution)/shard_map/ppermute | solution.py:448
  45.8 0.0 collective-permute-done.5.up_ref
  45.8 0.0 collective-permute-done.6.down_ref
  45.8 0.4 late_blocks.1
  46.2 1.2 %collective-permute-start.10 = (f32[432,256]{1,0:T(8,128)S(1)}, f32[432,256]{1,0:T(8,128)S(1)}, u32[]{:S(2)}, u32[]{:S(2)}) collective-permute-start(f32[432,256]{1,0:T(8,128)S(1)} %get-tuple-element.32), channel_id=1, source_target_pairs={{0,1},{1,2},{2,3},{3,0},{4,5},{5,6},{6,7},{7,4},{8,9},{9,10},{10,1... | collective-permute-start | bytes 1327112 | tf_op jit(solution)/shard_map/ppermute | solution.py:448
  47.4 2.1 %collective-permute-start.11 = (f32[432,256]{1,0:T(8,128)S(1)}, f32[432,256]{1,0:T(8,128)S(1)}, u32[]{:S(2)}, u32[]{:S(2)}) collective-permute-start(f32[432,256]{1,0:T(8,128)S(1)} %get-tuple-element.33), channel_id=1, source_target_pairs={{0,3},{1,0},{2,1},{3,2},{4,7},{5,4},{6,5},{7,6},{8,11},{9,8},{10,9... | collective-permute-start | bytes 1327112 | tf_op jit(solution)/shard_map/ppermute | solution.py:448
  49.5 5.1 %collective-permute-start.8 = (f32[96,256]{1,0:T(8,128)S(1)}, f32[96,256]{1,0:T(8,128)S(1)}, u32[]{:S(2)}, u32[]{:S(2)}) collective-permute-start(f32[96,256]{1,0:T(8,128)S(1)} %get-tuple-element.29.high_ref), channel_id=1, source_target_pairs={{0,4},{4,8},{8,12},{12,16},{16,20},{20,24},{24,28},{28,32},{32,36}... | collective-permute-start | bytes 294920 | tf_op jit(solution)/shard_map/ppermute | solution.py:441
  54.6 1.9 %collective-permute-start.9 = (f32[96,256]{1,0:T(8,128)S(1)}, f32[96,256]{1,0:T(8,128)S(1)}, u32[]{:S(2)}, u32[]{:S(2)}) collective-permute-start(f32[96,256]{1,0:T(8,128)S(1)} %get-tuple-element.30.low_ref), channel_id=1, source_target_pairs={{4,0},{8,4},{12,8},{16,12},{20,16},{24,20},{28,24},{32,28},{36,32}... | collective-permute-start | bytes 294920 | tf_op jit(solution)/shard_map/ppermute | solution.py:441
  56.5 0.1 collective-permute-start.12
  56.7 5.1 %collective-permute-done.12.rest_1_ = f32[8,128]{1,0:T(8,128)S(1)} collective-permute-done((f32[8,128]{1,0:T(8,128)S(1)}, f32[8,128]{1,0:T(8,128)S(1)}, u32[]{:S(2)}, u32[]{:S(2)}) %collective-permute-start.12) | collective-permute-done | bytes 4128 | tf_op jit(solution)/shard_map/ppermute | solution.py:452
  61.7 0.0 collective-permute-done.8.before_ref
  61.7 1.5 %collective-permute-done.9.after_ref = f32[96,256]{1,0:T(8,128)S(1)} collective-permute-done((f32[96,256]{1,0:T(8,128)S(1)}, f32[96,256]{1,0:T(8,128)S(1)}, u32[]{:S(2)}, u32[]{:S(2)}) %collective-permute-start.9) | collective-permute-done | bytes 98336 | tf_op jit(solution)/shard_map/ppermute | solution.py:441
  63.2 0.0 collective-permute-done.10.late_up
  63.2 0.0 collective-permute-done.11.late_down
  63.2 2.5 %finish.1 = f32[48,16,256]{2,1,0:T(8,128)} custom-call(f32[3,5]{1,0:T(4,128)S(1)} %get-tuple-element.20.weights_ref, f32[96,256]{1,0:T(8,128)S(1)} %collective-permute-done.8.before_ref, f32[96,256]{1,0:T(8,128)S(1)} %collective-permute-done.9.after_ref, f32[96,256]{1,0:T(8,128)S(1)} %get-tuple-element.30.low_ref, f32[96,256]{1,0:T(8,128)S(1)} %get-tuple-element.29.high_ref, ...), custom_call_target="tpu_custom_call" | custom-call | flops 5898240 | bytes 4194304 | tf_op jit(solution)/shard_map/finish/pallas_call | solution.py:422
  (2 shorter events, 0.0 us)
Async XLA Ops:
  6.6 16.6 %collective-permute-start = (f32[16,48,256]{2,1,0:T(8,128)S(1)}, f32[16,48,256]{2,1,0:T(8,128)S(1)}, u32[]{:S(2)}, u32[]{:S(2)}) collective-permute-start(f32[16,48,256]{2,1,0:T(8,128)S(1)} %get-tuple-element.22), channel_id=1, source_target_pairs={{64,0},{128,64},{192,128},{65,1},{129,65},{193,129},{66,2},{130,66... | collective-permute-start | bytes 2359304 | tf_op jit(solution)/shard_map/ppermute | solution.py:441
  7.9 15.3 %collective-permute-start.1 = (f32[16,48,256]{2,1,0:T(8,128)S(1)}, f32[16,48,256]{2,1,0:T(8,128)S(1)}, u32[]{:S(2)}, u32[]{:S(2)}) collective-permute-start(f32[16,48,256]{2,1,0:T(8,128)S(1)} %get-tuple-element.23), channel_id=1, source_target_pairs={{0,64},{64,128},{128,192},{1,65},{65,129},{129,193},{2,66},{66,130... | collective-permute-start | bytes 2359304 | tf_op jit(solution)/shard_map/ppermute | solution.py:441
  11.0 3.4 %collective-permute-start.2 = (f32[8,128]{1,0:T(8,128)S(1)}, f32[8,128]{1,0:T(8,128)S(1)}, u32[]{:S(2)}, u32[]{:S(2)}) collective-permute-start(f32[8,128]{1,0:T(8,128)S(1)} %get-tuple-element.24.refs_0_), channel_id=1, source_target_pairs={{0,64},{64,0},{128,192},{192,128},{1,65},{65,1},{129,193},{193,129... | collective-permute-start | bytes 12296 | tf_op jit(solution)/shard_map/ppermute | solution.py:452
  14.4 3.6 %collective-permute-start.3 = (f32[8,128]{1,0:T(8,128)S(1)}, f32[8,128]{1,0:T(8,128)S(1)}, u32[]{:S(2)}, u32[]{:S(2)}) collective-permute-start(f32[8,128]{1,0:T(8,128)S(1)} %add_sums.2.refs_0_), channel_id=1, source_target_pairs={{0,1},{1,0},{2,3},{3,2},{4,5},{5,4},{6,7},{7,6},{8,9},{9,8},{10,11... | collective-permute-start | bytes 12296 | tf_op jit(solution)/shard_map/ppermute | solution.py:452
  18.0 5.1 %collective-permute-start.4 = (f32[8,128]{1,0:T(8,128)S(1)}, f32[8,128]{1,0:T(8,128)S(1)}, u32[]{:S(2)}, u32[]{:S(2)}) collective-permute-start(f32[8,128]{1,0:T(8,128)S(1)} %add_sums.3.moments_ref), channel_id=1, source_target_pairs={{0,2},{1,3},{2,0},{3,1},{4,6},{5,7},{6,4},{7,5},{8,10},{9,11},{10,... | collective-permute-start | bytes 12296 | tf_op jit(solution)/shard_map/ppermute | solution.py:452
  23.5 22.3 %collective-permute-start.5 = (f32[624,256]{1,0:T(8,128)S(1)}, f32[624,256]{1,0:T(8,128)S(1)}, u32[]{:S(2)}, u32[]{:S(2)}) collective-permute-start(f32[624,256]{1,0:T(8,128)S(1)} %get-tuple-element.25), channel_id=1, source_target_pairs={{0,1},{1,2},{2,3},{3,0},{4,5},{5,6},{6,7},{7,4},{8,9},{9,10},{10,1... | collective-permute-start | bytes 1916936 | tf_op jit(solution)/shard_map/ppermute | solution.py:448
  25.1 20.6 %collective-permute-start.6 = (f32[624,256]{1,0:T(8,128)S(1)}, f32[624,256]{1,0:T(8,128)S(1)}, u32[]{:S(2)}, u32[]{:S(2)}) collective-permute-start(f32[624,256]{1,0:T(8,128)S(1)} %get-tuple-element.26), channel_id=1, source_target_pairs={{0,3},{1,0},{2,1},{3,2},{4,7},{5,4},{6,5},{7,6},{8,11},{9,8},{10,9... | collective-permute-start | bytes 1916936 | tf_op jit(solution)/shard_map/ppermute | solution.py:448
  26.8 19.0 %collective-permute-start.7 = (f32[192,256]{1,0:T(8,128)S(1)}, f32[192,256]{1,0:T(8,128)S(1)}, u32[]{:S(2)}, u32[]{:S(2)}) collective-permute-start(f32[192,256]{1,0:T(8,128)S(1)} %get-tuple-element.27), channel_id=1, source_target_pairs={{0,2},{1,3},{2,0},{3,1},{4,6},{5,7},{6,4},{7,5},{8,10},{9,11},{10,... | collective-permute-start | bytes 589832 | tf_op jit(solution)/shard_map/ppermute | solution.py:448
  46.2 17.0 %collective-permute-start.10 = (f32[432,256]{1,0:T(8,128)S(1)}, f32[432,256]{1,0:T(8,128)S(1)}, u32[]{:S(2)}, u32[]{:S(2)}) collective-permute-start(f32[432,256]{1,0:T(8,128)S(1)} %get-tuple-element.32), channel_id=1, source_target_pairs={{0,1},{1,2},{2,3},{3,0},{4,5},{5,6},{6,7},{7,4},{8,9},{9,10},{10,1... | collective-permute-start | bytes 1327112 | tf_op jit(solution)/shard_map/ppermute | solution.py:448
  47.4 15.8 %collective-permute-start.11 = (f32[432,256]{1,0:T(8,128)S(1)}, f32[432,256]{1,0:T(8,128)S(1)}, u32[]{:S(2)}, u32[]{:S(2)}) collective-permute-start(f32[432,256]{1,0:T(8,128)S(1)} %get-tuple-element.33), channel_id=1, source_target_pairs={{0,3},{1,0},{2,1},{3,2},{4,7},{5,4},{6,5},{7,6},{8,11},{9,8},{10,9... | collective-permute-start | bytes 1327112 | tf_op jit(solution)/shard_map/ppermute | solution.py:448
  49.5 12.2 %collective-permute-start.8 = (f32[96,256]{1,0:T(8,128)S(1)}, f32[96,256]{1,0:T(8,128)S(1)}, u32[]{:S(2)}, u32[]{:S(2)}) collective-permute-start(f32[96,256]{1,0:T(8,128)S(1)} %get-tuple-element.29.high_ref), channel_id=1, source_target_pairs={{0,4},{4,8},{8,12},{12,16},{16,20},{20,24},{24,28},{28,32},{32,36}... | collective-permute-start | bytes 294920 | tf_op jit(solution)/shard_map/ppermute | solution.py:441
  54.6 8.6 %collective-permute-start.9 = (f32[96,256]{1,0:T(8,128)S(1)}, f32[96,256]{1,0:T(8,128)S(1)}, u32[]{:S(2)}, u32[]{:S(2)}) collective-permute-start(f32[96,256]{1,0:T(8,128)S(1)} %get-tuple-element.30.low_ref), channel_id=1, source_target_pairs={{4,0},{8,4},{12,8},{16,12},{20,16},{24,20},{28,24},{32,28},{36,32}... | collective-permute-start | bytes 294920 | tf_op jit(solution)/shard_map/ppermute | solution.py:441
  56.5 5.2 %collective-permute-start.12 = (f32[8,128]{1,0:T(8,128)S(1)}, f32[8,128]{1,0:T(8,128)S(1)}, u32[]{:S(2)}, u32[]{:S(2)}) collective-permute-start(f32[8,128]{1,0:T(8,128)S(1)} %get-tuple-element.34.rest_0_), channel_id=1, source_target_pairs={{0,128},{64,192},{128,0},{192,64},{1,129},{65,193},{129,1},{193,65... | collective-permute-start | bytes 12296 | tf_op jit(solution)/shard_map/ppermute | solution.py:452

commit v6 on v5

--- a/solution.py
+++ b/solution.py
@@ -503,11 +503,12 @@
     )
     late_up = turn(late_up, "mz", 1)
     late_down = turn(late_down, "mz", -1)
+    (moments,) = local_call(add_kernel, [tile], (moments, swap(moments, "gx", 2)), "add_sums")
     before = shift(high, "gy", 1)
     after = shift(low, "gy", -1)
     result = finish(
         weights,
-        (before, after, low, high, own, late_up, late_down, moments, swap(moments, "gx", 2)),
+        (before, after, low, high, own, late_up, late_down, moments),
         (local_y, depth, elements, split, local_x, size_x, size_y, MOVED),
         squared_norms(size_x, size_y, depth),
     )

time: 66 us -> 65.9 us (level)
  no operation moved by 1% of the time
where the time goes in v6:
time: 65.9 us; the launch traced here: 65.7 us
  starting transfers between devices  27.5 us (42%)
  waiting for transfers between devices  15.5 us (24%)
  blocking collectives  12.8 us (19%)
  Pallas kernels  9.83 us (15%)
    all_to_all x1, blocking collectives, shards(): gathered = lax.all_to_all(spread, 'gy', 0, 0, tiled=True)  12.8 us
    ppermute x4, starting transfers between devices, shift(): lax.ppermute(values, axis, [(i, i + by) for i in range(count) if 0 <= i +...  11.4 us
    ppermute x4, waiting for transfers between devices, swap(): lax.ppermute(values, axis, [(i, i ^ bit) for i in range(lax.axis_size(axi...  9.83 us
    ppermute x5, starting transfers between devices, turn(): lax.ppermute(values, axis, [(i, (i + by) % count) for i in range(count)])  8.6 us
    ppermute x4, starting transfers between devices, swap(): lax.ppermute(values, axis, [(i, i ^ bit) for i in range(lax.axis_size(axi...  7.52 us
    pallas_call x1, Pallas kernels, mix(): pl.pallas_call(functools.partial(mix_kernel, sizes), out_shape=[jax.Shape...  6.59 us
    ppermute x5, waiting for transfers between devices, turn(): lax.ppermute(values, axis, [(i, (i + by) % count) for i in range(count)])  4.16 us
    pallas_call x1, Pallas kernels, finish(): pl.pallas_call(functools.partial(finish_kernel, sizes, squares), out_shap...  2.47 us
  transfers between devices with their start and end apart: 13, of which 6 were waited for; matrix products, arithmetic and copies ran while one was open for 0% of the time, Pallas kernels for 0%

profile of v6, /device:TPU:98, one launch (start us, length us, event | category | flops | bytes accessed | tf_op | source)
XLA Modules:
  0.0 65.7 jit_solution(2958678709159161351)
XLA Ops:
  0.0 6.6 %mix_bins.1 = (f32[4,16,48,256]{3,2,1,0:T(8,128)S(1)}, f32[16,48,256]{2,1,0:T(8,128)S(1)}, f32[16,48,256]{2,1,0:T(8,128)S(1)}, f32[8,128]{1,0:T(8,128)S(1)}, f32[3,5]{1,0:T(4,128)S(1)}) custom-call(f32[3,5]{1,0:T(4,128)} %taps_hbm.1, s32[4,24]{1,0:T(4,128)} %bitcast.11, f32[4,24]{1,0:T(4,128)} %bitcast.12, s32[4096,256]{1,0:T(8,128)} %bitcast.10), custom_call_target="tpu_custom_call" | custom-call | flops 1207959552 | bytes 8388608 | tf_op jit(solution)/shard_map/mix_bins/pallas_call | solution.py:207
  6.6 1.3 %collective-permute-start = (f32[16,48,256]{2,1,0:T(8,128)S(1)}, f32[16,48,256]{2,1,0:T(8,128)S(1)}, u32[]{:S(2)}, u32[]{:S(2)}) collective-permute-start(f32[16,48,256]{2,1,0:T(8,128)S(1)} %get-tuple-element.22), channel_id=1, source_target_pairs={{64,0},{128,64},{192,128},{65,1},{129,65},{193,129},{66,2},{130,66... | collective-permute-start | bytes 2359304 | tf_op jit(solution)/shard_map/ppermute | solution.py:441
  7.9 3.1 %collective-permute-start.1 = (f32[16,48,256]{2,1,0:T(8,128)S(1)}, f32[16,48,256]{2,1,0:T(8,128)S(1)}, u32[]{:S(2)}, u32[]{:S(2)}) collective-permute-start(f32[16,48,256]{2,1,0:T(8,128)S(1)} %get-tuple-element.23), channel_id=1, source_target_pairs={{0,64},{64,128},{128,192},{1,65},{65,129},{129,193},{2,66},{66,130... | collective-permute-start | bytes 2359304 | tf_op jit(solution)/shard_map/ppermute | solution.py:441
  11.0 2.6 %collective-permute-start.2 = (f32[8,128]{1,0:T(8,128)S(1)}, f32[8,128]{1,0:T(8,128)S(1)}, u32[]{:S(2)}, u32[]{:S(2)}) collective-permute-start(f32[8,128]{1,0:T(8,128)S(1)} %get-tuple-element.24.refs_0_), channel_id=1, source_target_pairs={{0,64},{64,0},{128,192},{192,128},{1,65},{65,1},{129,193},{193,129... | collective-permute-start | bytes 12296 | tf_op jit(solution)/shard_map/ppermute | solution.py:452
  13.6 0.8 %collective-permute-done.2.refs_1_ = f32[8,128]{1,0:T(8,128)S(1)} collective-permute-done((f32[8,128]{1,0:T(8,128)S(1)}, f32[8,128]{1,0:T(8,128)S(1)}, u32[]{:S(2)}, u32[]{:S(2)}) %collective-permute-start.2) | collective-permute-done | bytes 4128 | tf_op jit(solution)/shard_map/ppermute | solution.py:452
  14.4 1.6 %collective-permute-start.3 = (f32[8,128]{1,0:T(8,128)S(1)}, f32[8,128]{1,0:T(8,128)S(1)}, u32[]{:S(2)}, u32[]{:S(2)}) collective-permute-start(f32[8,128]{1,0:T(8,128)S(1)} %add_sums.3.refs_0_), channel_id=1, source_target_pairs={{0,1},{1,0},{2,3},{3,2},{4,5},{5,4},{6,7},{7,6},{8,9},{9,8},{10,11... | collective-permute-start | bytes 12296 | tf_op jit(solution)/shard_map/ppermute | solution.py:452
  16.0 2.0 %collective-permute-done.3.refs_1_ = f32[8,128]{1,0:T(8,128)S(1)} collective-permute-done((f32[8,128]{1,0:T(8,128)S(1)}, f32[8,128]{1,0:T(8,128)S(1)}, u32[]{:S(2)}, u32[]{:S(2)}) %collective-permute-start.3) | collective-permute-done | bytes 4128 | tf_op jit(solution)/shard_map/ppermute | solution.py:452
  18.0 3.2 %collective-permute-start.4 = (f32[8,128]{1,0:T(8,128)S(1)}, f32[8,128]{1,0:T(8,128)S(1)}, u32[]{:S(2)}, u32[]{:S(2)}) collective-permute-start(f32[8,128]{1,0:T(8,128)S(1)} %add_sums.4.moments_ref), channel_id=1, source_target_pairs={{0,2},{1,3},{2,0},{3,1},{4,6},{5,7},{6,4},{7,5},{8,10},{9,11},{10,... | collective-permute-start | bytes 12296 | tf_op jit(solution)/shard_map/ppermute | solution.py:452
  21.2 1.9 %collective-permute-done.4.other_ref = f32[8,128]{1,0:T(8,128)S(1)} collective-permute-done((f32[8,128]{1,0:T(8,128)S(1)}, f32[8,128]{1,0:T(8,128)S(1)}, u32[]{:S(2)}, u32[]{:S(2)}) %collective-permute-start.4) | collective-permute-done | bytes 4128 | tf_op jit(solution)/shard_map/ppermute | solution.py:452
  23.2 0.0 collective-permute-done.above_ref
  23.2 0.0 collective-permute-done.1.below_ref
  23.2 0.3 first_blocks.1
  23.5 1.7 %collective-permute-start.5 = (f32[624,256]{1,0:T(8,128)S(1)}, f32[624,256]{1,0:T(8,128)S(1)}, u32[]{:S(2)}, u32[]{:S(2)}) collective-permute-start(f32[624,256]{1,0:T(8,128)S(1)} %get-tuple-element.25), channel_id=1, source_target_pairs={{0,1},{1,2},{2,3},{3,0},{4,5},{5,6},{6,7},{7,4},{8,9},{9,10},{10,1... | collective-permute-start | bytes 1916936 | tf_op jit(solution)/shard_map/ppermute | solution.py:448
  25.1 1.7 %collective-permute-start.6 = (f32[624,256]{1,0:T(8,128)S(1)}, f32[624,256]{1,0:T(8,128)S(1)}, u32[]{:S(2)}, u32[]{:S(2)}) collective-permute-start(f32[624,256]{1,0:T(8,128)S(1)} %get-tuple-element.26), channel_id=1, source_target_pairs={{0,3},{1,0},{2,1},{3,2},{4,7},{5,4},{6,5},{7,6},{8,11},{9,8},{10,9... | collective-permute-start | bytes 1916936 | tf_op jit(solution)/shard_map/ppermute | solution.py:448
  26.8 2.0 %collective-permute-start.7 = (f32[192,256]{1,0:T(8,128)S(1)}, f32[192,256]{1,0:T(8,128)S(1)}, u32[]{:S(2)}, u32[]{:S(2)}) collective-permute-start(f32[192,256]{1,0:T(8,128)S(1)} %get-tuple-element.27), channel_id=1, source_target_pairs={{0,2},{1,3},{2,0},{3,1},{4,6},{5,7},{6,4},{7,5},{8,10},{9,11},{10,... | collective-permute-start | bytes 589832 | tf_op jit(solution)/shard_map/ppermute | solution.py:448
  28.8 12.8 %all_to_all.11 = f32[16,1,128]{2,1,0:T(1,128)S(1)} all-to-all(f32[16,1,128]{2,1,0:T(1,128)S(1)} %bitcast.9), channel_id=1, replica_groups=mesh['gx'=4,'gy'=16,'mz'=4] {'gy'}, dimensions={0} | all-to-all | bytes 16384 | tf_op jit(solution)/shard_map/all_to_all | solution.py:498
  41.6 4.2 %collective-permute-done.7.across_ref = f32[192,256]{1,0:T(8,128)S(1)} collective-permute-done((f32[192,256]{1,0:T(8,128)S(1)}, f32[192,256]{1,0:T(8,128)S(1)}, u32[]{:S(2)}, u32[]{:S(2)}) %collective-permute-start.7) | collective-permute-done | bytes 196640 | tf_op jit(solution)/shard_map/ppermute | solution.py:448
  45.8 0.0 collective-permute-done.5.up_ref
  45.8 0.0 collective-permute-done.6.down_ref
  45.8 0.4 late_blocks.1
  46.2 1.2 %collective-permute-start.10 = (f32[432,256]{1,0:T(8,128)S(1)}, f32[432,256]{1,0:T(8,128)S(1)}, u32[]{:S(2)}, u32[]{:S(2)}) collective-permute-start(f32[432,256]{1,0:T(8,128)S(1)} %get-tuple-element.32), channel_id=1, source_target_pairs={{0,1},{1,2},{2,3},{3,0},{4,5},{5,6},{6,7},{7,4},{8,9},{9,10},{10,1... | collective-permute-start | bytes 1327112 | tf_op jit(solution)/shard_map/ppermute | solution.py:448
  47.4 2.1 %collective-permute-start.11 = (f32[432,256]{1,0:T(8,128)S(1)}, f32[432,256]{1,0:T(8,128)S(1)}, u32[]{:S(2)}, u32[]{:S(2)}) collective-permute-start(f32[432,256]{1,0:T(8,128)S(1)} %get-tuple-element.33), channel_id=1, source_target_pairs={{0,3},{1,0},{2,1},{3,2},{4,7},{5,4},{6,5},{7,6},{8,11},{9,8},{10,9... | collective-permute-start | bytes 1327112 | tf_op jit(solution)/shard_map/ppermute | solution.py:448
  49.5 5.1 %collective-permute-start.8 = (f32[96,256]{1,0:T(8,128)S(1)}, f32[96,256]{1,0:T(8,128)S(1)}, u32[]{:S(2)}, u32[]{:S(2)}) collective-permute-start(f32[96,256]{1,0:T(8,128)S(1)} %get-tuple-element.29.high_ref), channel_id=1, source_target_pairs={{0,4},{4,8},{8,12},{12,16},{16,20},{20,24},{24,28},{28,32},{32,36}... | collective-permute-start | bytes 294920 | tf_op jit(solution)/shard_map/ppermute | solution.py:441
  54.6 1.9 %collective-permute-start.9 = (f32[96,256]{1,0:T(8,128)S(1)}, f32[96,256]{1,0:T(8,128)S(1)}, u32[]{:S(2)}, u32[]{:S(2)}) collective-permute-start(f32[96,256]{1,0:T(8,128)S(1)} %get-tuple-element.30.low_ref), channel_id=1, source_target_pairs={{4,0},{8,4},{12,8},{16,12},{20,16},{24,20},{28,24},{32,28},{36,32}... | collective-permute-start | bytes 294920 | tf_op jit(solution)/shard_map/ppermute | solution.py:441
  56.5 0.1 collective-permute-start.12
  56.7 5.1 %collective-permute-done.12.refs_1_ = f32[8,128]{1,0:T(8,128)S(1)} collective-permute-done((f32[8,128]{1,0:T(8,128)S(1)}, f32[8,128]{1,0:T(8,128)S(1)}, u32[]{:S(2)}, u32[]{:S(2)}) %collective-permute-start.12) | collective-permute-done | bytes 4128 | tf_op jit(solution)/shard_map/ppermute | solution.py:452
  61.7 0.0 collective-permute-done.8.before_ref
  61.7 1.5 %collective-permute-done.9.after_ref = f32[96,256]{1,0:T(8,128)S(1)} collective-permute-done((f32[96,256]{1,0:T(8,128)S(1)}, f32[96,256]{1,0:T(8,128)S(1)}, u32[]{:S(2)}, u32[]{:S(2)}) %collective-permute-start.9) | collective-permute-done | bytes 98336 | tf_op jit(solution)/shard_map/ppermute | solution.py:441
  63.2 0.0 collective-permute-done.10.late_up
  63.2 0.0 collective-permute-done.11.late_down
  63.2 2.5 %finish.1 = f32[48,16,256]{2,1,0:T(8,128)} custom-call(f32[3,5]{1,0:T(4,128)S(1)} %get-tuple-element.20.weights_ref, f32[96,256]{1,0:T(8,128)S(1)} %collective-permute-done.8.before_ref, f32[96,256]{1,0:T(8,128)S(1)} %collective-permute-done.9.after_ref, f32[96,256]{1,0:T(8,128)S(1)} %get-tuple-element.30.low_ref, f32[96,256]{1,0:T(8,128)S(1)} %get-tuple-element.29.high_ref, ...), custom_call_target="tpu_custom_call" | custom-call | flops 5898240 | bytes 4194304 | tf_op jit(solution)/shard_map/finish/pallas_call | solution.py:422
  (3 shorter events, 0.0 us)
Async XLA Ops:
  6.6 16.6 %collective-permute-start = (f32[16,48,256]{2,1,0:T(8,128)S(1)}, f32[16,48,256]{2,1,0:T(8,128)S(1)}, u32[]{:S(2)}, u32[]{:S(2)}) collective-permute-start(f32[16,48,256]{2,1,0:T(8,128)S(1)} %get-tuple-element.22), channel_id=1, source_target_pairs={{64,0},{128,64},{192,128},{65,1},{129,65},{193,129},{66,2},{130,66... | collective-permute-start | bytes 2359304 | tf_op jit(solution)/shard_map/ppermute | solution.py:441
  7.9 15.3 %collective-permute-start.1 = (f32[16,48,256]{2,1,0:T(8,128)S(1)}, f32[16,48,256]{2,1,0:T(8,128)S(1)}, u32[]{:S(2)}, u32[]{:S(2)}) collective-permute-start(f32[16,48,256]{2,1,0:T(8,128)S(1)} %get-tuple-element.23), channel_id=1, source_target_pairs={{0,64},{64,128},{128,192},{1,65},{65,129},{129,193},{2,66},{66,130... | collective-permute-start | bytes 2359304 | tf_op jit(solution)/shard_map/ppermute | solution.py:441
  11.0 3.4 %collective-permute-start.2 = (f32[8,128]{1,0:T(8,128)S(1)}, f32[8,128]{1,0:T(8,128)S(1)}, u32[]{:S(2)}, u32[]{:S(2)}) collective-permute-start(f32[8,128]{1,0:T(8,128)S(1)} %get-tuple-element.24.refs_0_), channel_id=1, source_target_pairs={{0,64},{64,0},{128,192},{192,128},{1,65},{65,1},{129,193},{193,129... | collective-permute-start | bytes 12296 | tf_op jit(solution)/shard_map/ppermute | solution.py:452
  14.4 3.6 %collective-permute-start.3 = (f32[8,128]{1,0:T(8,128)S(1)}, f32[8,128]{1,0:T(8,128)S(1)}, u32[]{:S(2)}, u32[]{:S(2)}) collective-permute-start(f32[8,128]{1,0:T(8,128)S(1)} %add_sums.3.refs_0_), channel_id=1, source_target_pairs={{0,1},{1,0},{2,3},{3,2},{4,5},{5,4},{6,7},{7,6},{8,9},{9,8},{10,11... | collective-permute-start | bytes 12296 | tf_op jit(solution)/shard_map/ppermute | solution.py:452
  18.0 5.1 %collective-permute-start.4 = (f32[8,128]{1,0:T(8,128)S(1)}, f32[8,128]{1,0:T(8,128)S(1)}, u32[]{:S(2)}, u32[]{:S(2)}) collective-permute-start(f32[8,128]{1,0:T(8,128)S(1)} %add_sums.4.moments_ref), channel_id=1, source_target_pairs={{0,2},{1,3},{2,0},{3,1},{4,6},{5,7},{6,4},{7,5},{8,10},{9,11},{10,... | collective-permute-start | bytes 12296 | tf_op jit(solution)/shard_map/ppermute | solution.py:452
  23.5 22.3 %collective-permute-start.5 = (f32[624,256]{1,0:T(8,128)S(1)}, f32[624,256]{1,0:T(8,128)S(1)}, u32[]{:S(2)}, u32[]{:S(2)}) collective-permute-start(f32[624,256]{1,0:T(8,128)S(1)} %get-tuple-element.25), channel_id=1, source_target_pairs={{0,1},{1,2},{2,3},{3,0},{4,5},{5,6},{6,7},{7,4},{8,9},{9,10},{10,1... | collective-permute-start | bytes 1916936 | tf_op jit(solution)/shard_map/ppermute | solution.py:448
  25.1 20.6 %collective-permute-start.6 = (f32[624,256]{1,0:T(8,128)S(1)}, f32[624,256]{1,0:T(8,128)S(1)}, u32[]{:S(2)}, u32[]{:S(2)}) collective-permute-start(f32[624,256]{1,0:T(8,128)S(1)} %get-tuple-element.26), channel_id=1, source_target_pairs={{0,3},{1,0},{2,1},{3,2},{4,7},{5,4},{6,5},{7,6},{8,11},{9,8},{10,9... | collective-permute-start | bytes 1916936 | tf_op jit(solution)/shard_map/ppermute | solution.py:448
  26.8 19.0 %collective-permute-start.7 = (f32[192,256]{1,0:T(8,128)S(1)}, f32[192,256]{1,0:T(8,128)S(1)}, u32[]{:S(2)}, u32[]{:S(2)}) collective-permute-start(f32[192,256]{1,0:T(8,128)S(1)} %get-tuple-element.27), channel_id=1, source_target_pairs={{0,2},{1,3},{2,0},{3,1},{4,6},{5,7},{6,4},{7,5},{8,10},{9,11},{10,... | collective-permute-start | bytes 589832 | tf_op jit(solution)/shard_map/ppermute | solution.py:448
  46.2 17.0 %collective-permute-start.10 = (f32[432,256]{1,0:T(8,128)S(1)}, f32[432,256]{1,0:T(8,128)S(1)}, u32[]{:S(2)}, u32[]{:S(2)}) collective-permute-start(f32[432,256]{1,0:T(8,128)S(1)} %get-tuple-element.32), channel_id=1, source_target_pairs={{0,1},{1,2},{2,3},{3,0},{4,5},{5,6},{6,7},{7,4},{8,9},{9,10},{10,1... | collective-permute-start | bytes 1327112 | tf_op jit(solution)/shard_map/ppermute | solution.py:448
  47.4 15.8 %collective-permute-start.11 = (f32[432,256]{1,0:T(8,128)S(1)}, f32[432,256]{1,0:T(8,128)S(1)}, u32[]{:S(2)}, u32[]{:S(2)}) collective-permute-start(f32[432,256]{1,0:T(8,128)S(1)} %get-tuple-element.33), channel_id=1, source_target_pairs={{0,3},{1,0},{2,1},{3,2},{4,7},{5,4},{6,5},{7,6},{8,11},{9,8},{10,9... | collective-permute-start | bytes 1327112 | tf_op jit(solution)/shard_map/ppermute | solution.py:448
  49.5 12.2 %collective-permute-start.8 = (f32[96,256]{1,0:T(8,128)S(1)}, f32[96,256]{1,0:T(8,128)S(1)}, u32[]{:S(2)}, u32[]{:S(2)}) collective-permute-start(f32[96,256]{1,0:T(8,128)S(1)} %get-tuple-element.29.high_ref), channel_id=1, source_target_pairs={{0,4},{4,8},{8,12},{12,16},{16,20},{20,24},{24,28},{28,32},{32,36}... | collective-permute-start | bytes 294920 | tf_op jit(solution)/shard_map/ppermute | solution.py:441
  54.6 8.6 %collective-permute-start.9 = (f32[96,256]{1,0:T(8,128)S(1)}, f32[96,256]{1,0:T(8,128)S(1)}, u32[]{:S(2)}, u32[]{:S(2)}) collective-permute-start(f32[96,256]{1,0:T(8,128)S(1)} %get-tuple-element.30.low_ref), channel_id=1, source_target_pairs={{4,0},{8,4},{12,8},{16,12},{20,16},{24,20},{28,24},{32,28},{36,32}... | collective-permute-start | bytes 294920 | tf_op jit(solution)/shard_map/ppermute | solution.py:441
  56.5 5.2 %collective-permute-start.12 = (f32[8,128]{1,0:T(8,128)S(1)}, f32[8,128]{1,0:T(8,128)S(1)}, u32[]{:S(2)}, u32[]{:S(2)}) collective-permute-start(f32[8,128]{1,0:T(8,128)S(1)} %get-tuple-element.34.refs_0_), channel_id=1, source_target_pairs={{0,128},{64,192},{128,0},{192,64},{1,129},{65,193},{129,1},{193,65... | collective-permute-start | bytes 12296 | tf_op jit(solution)/shard_map/ppermute | solution.py:452
